TPU v7x, 32 devices: a whole 2x2x4 slice. The times are simulated.
32 devices in a mesh: seq: 4 (over y, x), expert: 8 (over z, core).
Axes of the slice: x: 2, y: 2, z: 4, core: 2. Of those that a mesh axis runs over, the one named last changes fastest.
Arguments:
- tokens: bfloat16 [8, 1024, 4096], P('expert', 'seq'), may hold values from -6 to 6
- norm_gain: float32 [4096], replicated, may hold values from 0.1 to 1.9
- conv_weight: float32 [4, 4096], replicated, may hold values from -3 to 3
- conv_bias: float32 [4096], replicated, may hold values from -3 to 3
- proj_weight: bfloat16 [4096, 288], replicated, may hold values from -0.09375 to 0.09375
- dt_weight: bfloat16 [256, 4096], replicated, may hold values from -0.375 to 0.375
- dt_bias: float32 [4096], replicated, may hold values from -4 to 0
- decay_rate: float32 [16, 4096], replicated, may hold values from 0.02 to 1
- skip_gain: float32 [4096], replicated, may hold values from 0.5 to 1.5
- ffn_gain: float32 [4096], replicated, may hold values from 0.1 to 1.9
- expert_ids: int32 [8, 1024, 2], P('expert', 'seq'), may hold values from 0 to 7, all different within a row; in each aligned block of 256 rows (0 to 255, 256 to 511, ..., all dimensions but the last counted through in order) at most 128 rows name the same one
- route_weights: float32 [8, 1024, 2], P('expert', 'seq'), may hold values from 0.2 to 1
- w_gate: bfloat16 [8, 4096, 512], P('expert'), may hold values from -0.09375 to 0.09375
- w_up: bfloat16 [8, 4096, 512], P('expert'), may hold values from -0.09375 to 0.09375
- w_down: bfloat16 [8, 512, 4096], P('expert'), may hold values from -0.25 to 0.25
Outputs:
- block_out: bfloat16 [8, 1024, 4096], P('expert', 'seq')
Inputs may be any that keep to these rules, and one draw needn't show every extreme that they name: `expert_ids`: the two expert slices of a position differ. Among the 256 positions of one device, no expert slice is chosen more than 128 times, and in every draw some expert slice is chosen exactly 128 times by the positions of some device; every expert slice is chosen somewhere.
All inputs are finite; a program needn't handle non-finite values.
Results may differ from a plain program's by a relative error of at most 0.0085.
Values may be sent and summed in bfloat16 or wider, within the bound.
No kernel may reach another device: no remote copies, remote signals or barrier semaphores. Data moves between devices by JAX's collectives and lax.ppermute only.
A program may use at most 128 MiB of HBM per device.

v0:
```python
import jax
import jax.numpy as jnp
from jax import lax
from jax.sharding import PartitionSpec as P


def from_behind(array, axis, by):
    peers = lax.axis_size(axis)
    pairs = [(i, i + by) for i in range(peers) if 0 <= i + by < peers]
    return lax.ppermute(array, axis, pairs)


def prefix(array, axis, combine, identity):
    peers, place = (lax.axis_size(axis), lax.axis_index(axis))
    everything = jax.tree.map(lambda part: lax.all_gather(part, axis), array)
    start = jax.tree.map(
        lambda part, zero: jnp.broadcast_to(jnp.asarray(zero, part.dtype), part.shape),
        array,
        identity,
    )

    def turn(k, before):
        reached = k < place
        new = combine(before, jax.tree.map(lambda part: part[k], everything))
        return jax.tree.map(lambda a, b: jnp.where(reached, a, b), new, before)

    return lax.fori_loop(0, peers, turn, start)


def rms_scale(values, gain):
    return values * lax.rsqrt(jnp.mean(values * values, axis=-1, keepdims=True) + 1e-05) * gain


def local_scan(start_state, step_size, conv_float, input_map, output_map, decay_neg):
    tok_count = step_size.shape[0]
    block_len = 16
    block_total = tok_count // block_len
    pieces_all = (
        step_size.reshape(block_total, block_len, -1),
        conv_float.reshape(block_total, block_len, -1),
        input_map.reshape(block_total, block_len, -1),
        output_map.reshape(block_total, block_len, -1),
    )

    def block_step(ssm_state, pieces):
        step_blk, conv_blk, in_blk, out_blk = pieces
        collected = []
        for position in range(block_len):
            ssm_state = (
                jnp.exp(step_blk[position][None, :] * decay_neg) * ssm_state
                + (step_blk[position] * conv_blk[position])[None, :] * in_blk[position][:, None]
            )
            collected.append(jnp.sum(out_blk[position][:, None] * ssm_state, axis=0))
        return (ssm_state, jnp.stack(collected))

    final_state, outputs = lax.scan(block_step, start_state, pieces_all)
    return (outputs.reshape(tok_count, -1), final_state)


def per_device(
    tokens,
    norm_gain,
    conv_weight,
    conv_bias,
    proj_weight,
    dt_weight,
    dt_bias,
    decay_rate,
    skip_gain,
    ffn_gain,
    expert_ids,
    route_weights,
    w_gate,
    w_up,
    w_down,
):
    stream = tokens[0].astype(jnp.float32)
    tok_count = stream.shape[0]
    model_width = stream.shape[1]
    kernel = conv_weight.shape[0]
    low_width = dt_weight.shape[0]
    states = decay_rate.shape[0]
    normed = rms_scale(stream, norm_gain).astype(jnp.bfloat16)
    prior_rows = from_behind(normed[tok_count - (kernel - 1) :], "seq", 1)
    padded = jnp.concatenate([prior_rows, normed], axis=0).astype(jnp.float32)
    conv_sum = jnp.zeros((tok_count, model_width), jnp.float32)
    for offset in range(kernel):
        conv_sum = conv_sum + conv_weight[offset] * padded[offset : offset + tok_count]
    conv_out = jax.nn.silu(conv_sum + conv_bias).astype(jnp.bfloat16)
    projected = jnp.dot(conv_out, proj_weight, preferred_element_type=jnp.float32)
    low_rank = projected[:, :low_width].astype(jnp.bfloat16)
    step_size = jax.nn.softplus(
        jnp.dot(low_rank, dt_weight, preferred_element_type=jnp.float32) + dt_bias
    )
    input_map = projected[:, low_width : low_width + states]
    output_map = projected[:, low_width + states :]
    decay_neg = -decay_rate
    conv_float = conv_out.astype(jnp.float32)
    zero_state = jnp.zeros((states, model_width), jnp.float32)
    local_outputs, end_state = local_scan(
        zero_state, step_size, conv_float, input_map, output_map, decay_neg
    )
    span_decay = jnp.exp(decay_neg * jnp.sum(step_size, axis=0)[None, :])

    def compose(earlier, latter):
        return (earlier[0] * latter[0], latter[0] * earlier[1] + latter[1])

    _, incoming = prefix(
        (span_decay, end_state),
        "seq",
        compose,
        (jnp.ones_like(span_decay), jnp.zeros_like(end_state)),
    )
    scanned, _ = local_scan(incoming, step_size, conv_float, input_map, output_map, decay_neg)
    hidden_state = stream + (scanned + skip_gain * conv_float)
    ffn_in = rms_scale(hidden_state, ffn_gain).astype(jnp.bfloat16)
    owners = lax.axis_size("expert")
    experts = owners * w_gate.shape[0]
    capacity = 4 * tok_count // owners
    chosen = expert_ids[0].reshape(-1)
    onehot = (chosen[:, None] == jnp.arange(experts, dtype=jnp.int32)[None, :]).astype(jnp.int32)
    before = jnp.cumsum(onehot, axis=0) - onehot
    slot_pos = jnp.sum(before * onehot, axis=1)
    dest_row = chosen * capacity + slot_pos
    outgoing = (
        jnp.zeros((experts * capacity, model_width), jnp.bfloat16)
        .at[dest_row]
        .set(jnp.repeat(ffn_in, 2, axis=0))
    )
    outgoing = outgoing.reshape(experts, capacity, model_width)
    received = lax.all_to_all(outgoing, "expert", split_axis=0, concat_axis=0, tiled=True)
    recv_shape = received.shape
    rows_in = received.reshape(-1, model_width)
    gate_part = jnp.dot(rows_in, w_gate[0], preferred_element_type=jnp.float32)
    up_part = jnp.dot(rows_in, w_up[0], preferred_element_type=jnp.float32)
    inner_act = (jax.nn.silu(gate_part) * up_part).astype(jnp.bfloat16)
    result = jnp.dot(inner_act, w_down[0], preferred_element_type=jnp.float32).astype(jnp.bfloat16)
    returned = lax.all_to_all(
        result.reshape(recv_shape), "expert", split_axis=0, concat_axis=0, tiled=True
    )
    gathered = returned.reshape(experts * capacity, model_width)[dest_row].astype(jnp.float32)
    route_scale = route_weights[0].reshape(-1)
    weighted = (route_scale[:, None] * gathered).reshape(tok_count, 2, model_width)
    routed = weighted[:, 0] + weighted[:, 1]
    block_out = (hidden_state + routed).astype(jnp.bfloat16)
    return block_out[None]


def solution(mesh):
    in_specs = (
        P("expert", "seq", None),
        P(),
        P(),
        P(),
        P(),
        P(),
        P(),
        P(),
        P(),
        P(),
        P("expert", "seq", None),
        P("expert", "seq", None),
        P("expert", None, None),
        P("expert", None, None),
        P("expert", None, None),
    )
    out_specs = P("expert", "seq", None)
    return jax.shard_map(
        per_device, mesh=mesh, in_specs=in_specs, out_specs=out_specs, check_vma=False
    )
```

profile of v0, /device:TPU:0, one launch (start us, length us, event | category | flops | bytes accessed | tf_op | source)
XLA Modules:
  0.0 787.3 jit_solution(11775179501841315374)
XLA Ops:
  12.4 4.8 collective-permute-start
  25.2 4.1 convert.19
  29.3 6.5 fusion.103
  36.5 80.9 %while.38 = (s32[]{:T(128)}, f32[16,4096]{1,0:T(8,128)S(1)}, f32[16,16,4096]{2,1,0:T(8,128)}, f32[16,4096]{1,0:T(8,128)S(1)}, f32[16,16,4096]{2,1,0:T(8,128)}, /...) while((s32[]{:T(128)}, f32[16,4096]{1,0:T(8,128)S(1)}, ...), condition=%wide.region_3.4_spmd.clone, body=%wide.region_2.3_spmd.clone.sunk | while | flops 4325394 | bytes 3149323 | solution.py:56
  46.4 3.9 constant_dynamic-slice_fusion.115
  61.6 3.9 constant_dynamic-slice_fusion.115
  76.5 4.0 constant_dynamic-slice_fusion.115
  81.8 4.0 constant_dynamic-slice_fusion.115
  121.3 25.7 %all-gather.7.cloned.1.call-done = f32[64,4096]{1,0:T(8,128)} async-done(((f32[16,4096]{1,0:T(8,128)}), f32[64,4096]{1,0:T(8,128)}) %all-gather.7.cloned.1.call-update) | async-done | bytes 1048592 | tf_op jit(solution)/shard_map/all_gather | solution.py:15
  147.0 28.5 %all-gather.5.cloned.1.call-done = f32[64,4096]{1,0:T(8,128)} async-done(((f32[16,4096]{1,0:T(8,128)}), f32[64,4096]{1,0:T(8,128)}) %all-gather.5.cloned.1.call-update) | async-done | bytes 1048592 | tf_op jit(solution)/shard_map/all_gather | solution.py:15
  175.5 5.1 while.39
  180.6 126.5 %while.37 = (s32[]{:T(128)}, f32[16,4096]{1,0:T(8,128)S(1)}, f32[16,16,4096]{2,1,0:T(8,128)}, f32[16,16,4096]{2,1,0:T(8,128)}, f32[16,4096]{1,0:T(8,128)S(1)}, /...) while((s32[]{:T(128)}, f32[16,4096]{1,0:T(8,128)S(1)}, ...), condition=%wide.region_23.24_spmd, body=%wide.region_6.23_spmd.sunk | while | flops 9437201 | bytes 7741201 | solution.py:56
  307.1 10.9 %multiply_reduce_fusion.16 = (f32[256]{0:T(256)S(1)}, f32[256,4096]{1,0:T(8,128)S(1)}) fusion(f32[4096]{0:T(1024)S(1)} %copy-done.13, f32[16,16,4096]{2,1,0:T(8,128)} %get-tuple-element.175, bf16[1,256,4096]{2,1,0:T(8,128)(2,1)} %param.21, f32[4096]{0:T(1024)S(1)} %copy-done.11, f32[259,4096]{1,0:T(8,128)} %copy-done.2, f32[4096]{0:T(1024)S(1)} %bitcast.560, ...), kind=kLoop, calls=%fused_computation.253 | loop fusion | flops 20971264 | bytes 27362304 | tf_op jit(solution)/shard_map/reduce_sum | solution.py:31
  320.5 4.7 broadcast_in_dim.13
  325.2 7.2 reshape.730
  332.5 12.8 %scatter_custom_fusion = bf16[1024,4096]{1,0:T(8,128)(2,1)} fusion(s32[512]{0:T(512)S(1)} %bitcast.563, bf16[512,4096]{1,0:T(8,128)(2,1)} %reshape.730, bf16[]{:T(256)} %constant.77.clone.1), kind=kCustom, calls=%fused_computation.254 | custom fusion | bytes 8389120 | tf_op jit(solution)/shard_map/scatter | solution.py:128
  345.3 189.0 %all_to_all.10 = bf16[8,128,4096]{2,1,0:T(8,128)(2,1)S(1)} all-to-all(bf16[8,128,4096]{2,1,0:T(8,128)(2,1)} %bitcast.421), channel_id=1, replica_groups=mesh['seq'=4,'expert'=8] {'expert'}, dimensions={0} | all-to-all | bytes 16777216 | tf_op jit(solution)/shard_map/all_to_all | solution.py:131
  537.5 4.5 fusion.86
  542.0 15.8 %convolution_convert_fusion = bf16[1024,4096]{1,0:T(8,128)(2,1)} fusion(bf16[1,512,4096]{2,1,0:T(8,128)(2,1)} %param.35, f32[1024,512]{1,0:T(8,128)S(1)} %fusion.86, bf16[1024,4096]{1,0:T(8,128)(2,1)} %bitcast.424, bf16[1,4096,512]{2,1,0:T(8,128)(2,1)} %param.34), kind=kOutput, calls=%fused_computation.226 | convolution fusion | flops 8597274624 | bytes 27262976 | tf_op jit(solution)/shard_map/dot_general | solution.py:137
  557.8 5.1 all-to-all-start.1
  563.0 183.9 %all-to-all-done.1 = bf16[8,128,4096]{2,1,0:T(8,128)(2,1)} async-done(((bf16[8,128,4096]{2,1,0:T(8,128)(2,1)}), bf16[8,128,4096]{2,1,0:T(8,128)(2,1)}, u32[]{:S(2)}, u32[]{:S(2)}) %all-to-all-start.1) | async-done | bytes 8388640 | tf_op jit(solution)/shard_map/all_to_all | solution.py:138
  746.9 13.0 %gather_fusion = bf16[512,4096]{1,0:T(8,128)(2,1)} fusion(bf16[1024,4096]{1,0:T(8,128)(2,1)} %bitcast.104, s32[1024]{0:T(1024)S(1)} %pad_clamp_fusion), kind=kCustom, calls=%fused_computation | custom fusion | bytes 8390656 | tf_op jit(solution)/shard_map/gather | solution.py:141
  759.9 9.7 %reshape.717 = f32[256,2,4096]{2,1,0:T(2,128)} reshape(bf16[512,4096]{1,0:T(8,128)(2,1)} %gather_fusion) | data formatting | bytes 12582912 | tf_op jit(solution)/shard_map/convert_element_type | solution.py:141
  769.6 8.5 %copy_multiply_fusion = f32[256,2,4096]{2,0,1:T(8,128)S(1)} fusion(f32[256,2,4096]{2,1,0:T(2,128)} %reshape.717, f32[256,2]{0,1:T(2,128)S(1)} %bitcast.566), kind=kLoop, calls=%fused_computation.225 | loop fusion | flops 2097152 | bytes 16779264 | tf_op jit(solution)/shard_map/mul | solution.py:143
  (777 shorter events, 217.4 us)
Async XLA Ops:
  6.5 17.2 %copy-start = (bf16[4096,288]{0,1:T(8,128)(2,1)S(1)}, bf16[4096,288]{0,1:T(8,128)(2,1)}, u32[]{:S(2)}) copy-start(bf16[4096,288]{0,1:T(8,128)(2,1)} %param.25) | copy-start | bytes 7077892
  6.5 10.7 %copy-start.10 = (f32[4,4096]{1,0:T(4,128)S(1)}, f32[4,4096]{1,0:T(4,128)}, u32[]{:S(2)}) copy-start(f32[4,4096]{1,0:T(4,128)} %param.23) | copy-start | bytes 196612
  6.5 140.5 %all-gather.7.cloned.1.call-start = ((), (), s32[]{:S(2)}) async-start(), calls=%async_computation.3 | async-start | bytes 1310720 | tf_op jit(solution)/shard_map/all_gather | solution.py:15
  11.0 1.3 copy-start.5
  12.4 8.7 %copy-start.11 = (f32[4096]{0:T(1024)S(1)}, f32[4096]{0:T(1024)}, u32[]{:S(2)}) copy-start(f32[4096]{0:T(1024)} %param.24) | copy-start | bytes 49156
  12.4 6.4 collective-permute-start
  21.0 2.7 copy-start.2
  23.8 1.3 copy-start.7
  25.1 4.2 copy-start.17
  29.3 6.5 copy-start.8
  36.5 82.4 %copy-start.14 = (s32[1,256,2]{1,2,0:T(2,128)S(1)}, s32[1,256,2]{1,2,0:T(2,128)}, u32[]{:S(2)}) copy-start(s32[1,256,2]{1,2,0:T(2,128)} %param.31) | copy-start | bytes 6148
  117.4 0.7 copy-start.9
  118.2 57.4 %all-gather.5.cloned.1.call-start = ((), (), s32[]{:S(2)}) async-start(), calls=%async_computation.2 | async-start | bytes 1310720 | tf_op jit(solution)/shard_map/all_gather | solution.py:15
  180.6 126.6 %copy-start.13 = (f32[4096]{0:T(1024)S(1)}, f32[4096]{0:T(1024)}, u32[]{:S(2)}) copy-start(f32[4096]{0:T(1024)} %param.29) | copy-start | bytes 49156
  307.1 12.8 %copy-start.12 = (f32[4096]{0:T(1024)S(1)}, f32[4096]{0:T(1024)}, u32[]{:S(2)}) copy-start(f32[4096]{0:T(1024)} %param.30) | copy-start | bytes 49156
  318.0 1.9 copy-start.3
  345.3 192.2 %copy-start.16 = (bf16[1,4096,512]{2,1,0:T(8,128)(2,1)S(1)}, bf16[1,4096,512]{2,1,0:T(8,128)(2,1)}, u32[]{:S(2)}) copy-start(bf16[1,4096,512]{2,1,0:T(8,128)(2,1)} %param.33) | copy-start | bytes 12582916
  534.3 3.2 copy-start.6
  557.8 189.0 %all-to-all-start.1 = ((bf16[8,128,4096]{2,1,0:T(8,128)(2,1)}), bf16[8,128,4096]{2,1,0:T(8,128)(2,1)}, u32[]{:S(2)}, u32[]{:S(2)}) async-start(bf16[8,128,4096]{2,1,0:T(8,128)(2,1)} %bitcast.422), calls=%async_computation.1 | async-start | bytes 16777216 | tf_op jit(solution)/shard_map/all_to_all | solution.py:138
  759.9 9.7 %copy-start.15 = (f32[1,256,2]{1,2,0:T(2,128)S(1)}, f32[1,256,2]{1,2,0:T(2,128)}, u32[]{:S(2)}) copy-start(f32[1,256,2]{1,2,0:T(2,128)} %param.32) | copy-start | bytes 6148
  769.6 8.5 %copy-start.4 = (f32[256,4096]{1,0:T(8,128)S(1)}, f32[256,4096]{1,0:T(8,128)}, u32[]{:S(2)}) copy-start(f32[256,4096]{1,0:T(8,128)} %copy-done.3) | copy-start | bytes 12582916
  769.6 10.7 %copy-start.1 = (bf16[4096,288]{0,1:T(8,128)(2,1)S(1)}, bf16[4096,288]{0,1:T(8,128)(2,1)}, u32[]{:S(2)}) copy-start(bf16[4096,288]{0,1:T(8,128)(2,1)} %param.25) | copy-start | bytes 7077892
Sparse Core Ops, SparseCore 0:
  118.3 28.6 all-gather.6
  148.9 26.6 all-gather.4
where the time goes:
time: 795 us; the launch traced here: 787 us
  waiting for transfers between devices  240 us (30%)
  local copies, waits for them, and re-layouts  196 us (25%)
  blocking collectives  189 us (24%)
  other arithmetic  105 us (13%)
  matrix products  27.8 us (3%)
  between operations  13.9 us (2%)
  starting transfers between devices  10.2 us (1%)
    all_to_all x1, blocking collectives, per_device(): lax.all_to_all(outgoing, 'expert', split_axis=0, concat_axis=0, tiled=True)  189 us
    all_to_all x1, waiting for transfers between devices, per_device(): lax.all_to_all(result.reshape(recv_shape), 'expert', split_axis=0, concat...  184 us
    slice x32, local copies, waits for them, and re-layouts, block_step(): conv_blk[position]  118 us
    all_gather x2, waiting for transfers between devices, prefix(): everything = jax.tree.map(lambda part: lax.all_gather(part, axis), array)  54.2 us
    reduce_sum x80, other arithmetic, block_step(): collected.append(jnp.sum(out_blk[position][:, None] * ssm_state, axis=0))  43.4 us
  transfers between devices with their start and end apart: 4, of which 4 were waited for; matrix products, arithmetic and copies ran while one was open for 0% of the time, Pallas kernels for 0%

commit v1 on v0

v1 whole, which is shorter than its diff:
```python
import functools
import math

import jax
import jax.numpy as jnp
from jax import lax
from jax.experimental import pallas as pl
from jax.experimental.pallas import tpu as pltpu
from jax.sharding import PartitionSpec as P

LANES = 128
GROUP = 8
LOG2E = math.log2(math.e)


def from_behind(array, axis, by):
    peers = lax.axis_size(axis)
    pairs = [(i, i + by) for i in range(peers) if 0 <= i + by < peers]
    return lax.ppermute(array, axis, pairs)


def silu(v):
    return v / (1.0 + jnp.exp(-v))


def softplus(v):
    return jnp.maximum(v, 0.0) + jnp.log1p(jnp.exp(-jnp.abs(v)))


def spread_columns(maps, target, first, count, rows):
    for n in range(count):
        target[n] = jnp.broadcast_to(maps[:, first + n : first + n + 1], (rows, LANES))


def front_kernel(
    tok_ref, halo_ref, norm_gain, conv_weight, conv_bias, low_weight, maps_weight,
    dt_weight, dt_bias, decay,
    conv_ref, step_ref, drive_ref, maps_ref, end_ref, total_ref,
    normed, low, block, in_rows,
):
    rows, width = tok_ref.shape
    halo = halo_ref.shape[0]
    states = decay.shape[0]
    taps = conv_weight.shape[0]
    tiles = width // LANES
    gain = norm_gain[...]

    def norm_rows(x):
        x = x.astype(jnp.float32)
        scale = lax.rsqrt(jnp.mean(x * x, axis=-1, keepdims=True) + 1e-05)
        return (x * scale * gain).astype(jnp.bfloat16).astype(jnp.float32)

    normed[pl.ds(0, halo), :] = norm_rows(halo_ref[...])

    def norm_step(i, _):
        at = pl.multiple_of(i * 16, 16)
        normed[pl.ds(halo + at, 16), :] = norm_rows(tok_ref[pl.ds(at, 16), :])
        return 0

    lax.fori_loop(0, rows // 16, norm_step, 0)

    chunk = 512

    def conv_step(i, _):
        at = pl.multiple_of(i * 16, 16)
        for c in range(width // chunk):
            cols = pl.ds(c * chunk, chunk)
            window = normed[pl.ds(pl.multiple_of(halo - 8 + at, 8), 24), cols]
            total = jnp.zeros((16, chunk), jnp.float32)
            for j in range(taps):
                back = taps - 1 - j
                moved = pltpu.roll(window, back, 0) if back else window
                total = total + conv_weight[pl.ds(j, 1), cols] * moved[8:24]
            conv_ref[pl.ds(at, 16), cols] = silu(total + conv_bias[:, cols]).astype(jnp.bfloat16)
        return 0

    lax.fori_loop(0, rows // 16, conv_step, 0)

    conv_all = conv_ref[...]
    low[...] = jnp.dot(
        conv_all, low_weight[...], preferred_element_type=jnp.float32
    ).astype(jnp.bfloat16)
    maps = jnp.dot(conv_all, maps_weight[...], preferred_element_type=jnp.float32)
    maps_ref[...] = maps
    spread_columns(maps, in_rows, 0, states, rows)

    def step_chunk(c, _):
        cols = pl.ds(pl.multiple_of(c * chunk, chunk), chunk)
        block[...] = softplus(
            jnp.dot(low[...], dt_weight[:, cols], preferred_element_type=jnp.float32)
            + dt_bias[:, cols]
        )

        def move(g, _):
            at = pl.multiple_of(g * 16, 16)
            step = block[pl.ds(at, 16), :]
            drive = step * conv_ref[pl.ds(at, 16), cols].astype(jnp.float32)
            for half in range(2):
                for j in range(chunk // LANES):
                    to = pl.ds((at + half * 8) * tiles + c * (chunk // LANES) + j, 8, stride=tiles)
                    part = (slice(half * 8, half * 8 + 8), slice(j * LANES, (j + 1) * LANES))
                    step_ref[to, :] = step[part]
                    drive_ref[to, :] = drive[part]
            return 0

        lax.fori_loop(0, rows // 16, move, 0)
        return 0

    lax.fori_loop(0, width // chunk, step_chunk, 0)

    def scan_tile(k, _):
        mine = pl.ds(pl.multiple_of(k * GROUP, GROUP), GROUP)
        rates = [decay[n, mine, :] for n in range(states)]

        def advance(i, carry):
            state, total = carry
            for p in range(4):
                t = i * 4 + p
                here = pl.ds(pl.multiple_of(t * tiles + k * GROUP, GROUP), GROUP)
                step, drive = step_ref[here, :], drive_ref[here, :]
                total = total + step
                state = tuple(
                    jnp.exp2(step * rates[n]) * state[n] + drive * in_rows[n, pl.ds(t, 1), :]
                    for n in range(states)
                )
            return state, total

        zero = jnp.zeros((GROUP, LANES), jnp.float32)
        state, total = lax.fori_loop(0, rows // 4, advance, ((zero,) * states, zero))
        for n in range(states):
            end_ref[n, mine, :] = state[n]
        total_ref[mine, :] = total
        return 0

    lax.fori_loop(0, tiles // GROUP, scan_tile, 0)


def back_kernel(
    tok_ref, conv_ref, step_ref, drive_ref, maps_ref, decay, skip_gain, ffn_gain, *rest,
    before,
):
    ends, totals = rest[:before], rest[before : 2 * before]
    hidden_ref, ffn_ref = rest[2 * before : 2 * before + 2]
    in_rows, out_rows, scanned = rest[2 * before + 2 :]
    rows, width = tok_ref.shape
    states = decay.shape[0]
    tiles = width // LANES
    maps = maps_ref[...]
    spread_columns(maps, in_rows, 0, states, rows)
    spread_columns(maps, out_rows, states, states, rows)

    def scan_tile(k, _):
        mine = pl.ds(pl.multiple_of(k * GROUP, GROUP), GROUP)
        rates = [decay[n, mine, :] for n in range(states)]
        start = []
        for n in range(states):
            entering = jnp.zeros((GROUP, LANES), jnp.float32)
            for back in reversed(range(before)):
                entering = (
                    jnp.exp2(totals[back][mine, :] * rates[n]) * entering
                    + ends[back][n, mine, :]
                )
            start.append(entering)

        def advance(i, state):
            for p in range(4):
                t = i * 4 + p
                here = pl.ds(pl.multiple_of(t * tiles + k * GROUP, GROUP), GROUP)
                step, drive = step_ref[here, :], drive_ref[here, :]
                state = tuple(
                    jnp.exp2(step * rates[n]) * state[n] + drive * in_rows[n, pl.ds(t, 1), :]
                    for n in range(states)
                )
                parts = [state[n] * out_rows[n, pl.ds(t, 1), :] for n in range(states)]
                while len(parts) > 1:
                    parts = [a + b for a, b in zip(parts[::2], parts[1::2])]
                scanned[here, :] = parts[0]
            return state

        lax.fori_loop(0, rows // 4, advance, tuple(start))
        return 0

    lax.fori_loop(0, tiles // GROUP, scan_tile, 0)

    def finish(i, _):
        at = pl.multiple_of(i * 16, 16)
        squares = jnp.zeros((16, LANES), jnp.float32)
        for j in range(tiles):
            cols = pl.ds(j * LANES, LANES)
            came = jnp.concatenate(
                [scanned[pl.ds((at + half * 8) * tiles + j, 8, stride=tiles), :] for half in range(2)],
                axis=0,
            )
            conv = conv_ref[pl.ds(at, 16), cols].astype(jnp.float32)
            hidden = tok_ref[pl.ds(at, 16), cols].astype(jnp.float32) + (
                came + skip_gain[:, cols] * conv
            )
            hidden_ref[pl.ds(at, 16), cols] = hidden
            squares = squares + hidden * hidden
        mean = jnp.sum(squares, axis=-1, keepdims=True) / width
        scale = lax.rsqrt(mean + 1e-05)
        ffn_ref[pl.ds(at, 16), :] = (
            hidden_ref[pl.ds(at, 16), :] * scale * ffn_gain[...]
        ).astype(jnp.bfloat16)
        return 0

    lax.fori_loop(0, rows // 16, finish, 0)


def mixer(
    tokens, norm_gain, conv_weight, conv_bias, proj_weight, dt_weight, dt_bias, decay_rate,
    skip_gain, ffn_gain,
):
    rows, width = tokens.shape
    states = decay_rate.shape[0]
    low_width = dt_weight.shape[0]
    tiles = width // LANES
    f32 = jnp.float32
    halo = from_behind(tokens[rows - 16 :], "seq", 1)
    decay = (decay_rate * (-LOG2E)).reshape(states, tiles, LANES)
    row = lambda v: v.reshape(1, width)
    conv, step, drive, maps, end, total = pl.pallas_call(
        front_kernel,
        out_shape=(
            jax.ShapeDtypeStruct((rows, width), jnp.bfloat16),
            jax.ShapeDtypeStruct((rows * tiles, LANES), f32),
            jax.ShapeDtypeStruct((rows * tiles, LANES), f32),
            jax.ShapeDtypeStruct((rows, 2 * states), f32),
            jax.ShapeDtypeStruct((states, tiles, LANES), f32),
            jax.ShapeDtypeStruct((tiles, LANES), f32),
        ),
        scratch_shapes=[
            pltpu.VMEM((rows + 16, width), f32),
            pltpu.VMEM((rows, low_width), jnp.bfloat16),
            pltpu.VMEM((rows, 512), f32),
            pltpu.VMEM((states, rows, LANES), f32),
        ],
        compiler_params=pltpu.CompilerParams(vmem_limit_bytes=56 * 2**20),
        cost_estimate=pl.CostEstimate(
            flops=2 * rows * width * (2 * low_width + 8 * states),
            bytes_accessed=20 * 2**20,
            transcendentals=rows * width * states,
        ),
        name="mixer_front",
    )(
        tokens, halo, row(norm_gain), conv_weight, row(conv_bias),
        proj_weight[:, :low_width], proj_weight[:, low_width:], dt_weight, row(dt_bias), decay,
    )
    before = lax.axis_size("seq") - 1
    ends = [from_behind(end, "seq", by + 1) for by in range(before)]
    totals = [from_behind(total, "seq", by + 1) for by in range(before)]
    hidden, ffn_in = pl.pallas_call(
        functools.partial(back_kernel, before=before),
        out_shape=(
            jax.ShapeDtypeStruct((rows, width), f32),
            jax.ShapeDtypeStruct((rows, width), jnp.bfloat16),
        ),
        scratch_shapes=[
            pltpu.VMEM((states, rows, LANES), f32),
            pltpu.VMEM((states, rows, LANES), f32),
            pltpu.VMEM((rows * tiles, LANES), f32),
        ],
        compiler_params=pltpu.CompilerParams(vmem_limit_bytes=56 * 2**20),
        cost_estimate=pl.CostEstimate(
            flops=2 * rows * width * 8 * states,
            bytes_accessed=20 * 2**20,
            transcendentals=rows * width * states,
        ),
        name="mixer_back",
    )(tokens, conv, step, drive, maps, decay, row(skip_gain), row(ffn_gain), *ends, *totals)
    return hidden, ffn_in


def routed_by_slots(ffn_in, chosen, route_scale, w_gate, w_up, w_down):
    tok_count, model_width = ffn_in.shape
    owners = lax.axis_size("expert")
    experts = owners * w_gate.shape[0]
    capacity = 4 * tok_count // owners
    chosen = chosen.reshape(-1)
    onehot = (chosen[:, None] == jnp.arange(experts, dtype=jnp.int32)[None, :]).astype(jnp.int32)
    before = jnp.cumsum(onehot, axis=0) - onehot
    slot_pos = jnp.sum(before * onehot, axis=1)
    dest_row = chosen * capacity + slot_pos
    outgoing = (
        jnp.zeros((experts * capacity, model_width), jnp.bfloat16)
        .at[dest_row]
        .set(jnp.repeat(ffn_in, 2, axis=0))
    )
    outgoing = outgoing.reshape(experts, capacity, model_width)
    received = lax.all_to_all(outgoing, "expert", split_axis=0, concat_axis=0, tiled=True)
    recv_shape = received.shape
    rows_in = received.reshape(-1, model_width)
    gate_part = jnp.dot(rows_in, w_gate[0], preferred_element_type=jnp.float32)
    up_part = jnp.dot(rows_in, w_up[0], preferred_element_type=jnp.float32)
    inner_act = (jax.nn.silu(gate_part) * up_part).astype(jnp.bfloat16)
    result = jnp.dot(inner_act, w_down[0], preferred_element_type=jnp.float32).astype(jnp.bfloat16)
    returned = lax.all_to_all(
        result.reshape(recv_shape), "expert", split_axis=0, concat_axis=0, tiled=True
    )
    gathered = returned.reshape(experts * capacity, model_width)[dest_row].astype(jnp.float32)
    weighted = (route_scale.reshape(-1)[:, None] * gathered).reshape(tok_count, 2, model_width)
    return weighted[:, 0] + weighted[:, 1]


def per_device(
    tokens, norm_gain, conv_weight, conv_bias, proj_weight, dt_weight, dt_bias, decay_rate,
    skip_gain, ffn_gain, expert_ids, route_weights, w_gate, w_up, w_down,
):
    hidden, ffn_in = mixer(
        tokens[0], norm_gain, conv_weight, conv_bias, proj_weight, dt_weight, dt_bias,
        decay_rate, skip_gain, ffn_gain,
    )
    routed = routed_by_slots(ffn_in, expert_ids[0], route_weights[0], w_gate, w_up, w_down)
    return (hidden + routed).astype(jnp.bfloat16)[None]


def solution(mesh):
    in_specs = (
        P("expert", "seq", None),
        P(), P(), P(), P(), P(), P(), P(), P(), P(),
        P("expert", "seq", None),
        P("expert", "seq", None),
        P("expert", None, None),
        P("expert", None, None),
        P("expert", None, None),
    )
    out_specs = P("expert", "seq", None)
    return jax.shard_map(
        per_device, mesh=mesh, in_specs=in_specs, out_specs=out_specs, check_vma=False
    )
```

time: 795 us -> 564 us (0.71)
  local copies, waits for them, and re-layouts: 196 us -> 59.7 us
  other arithmetic: 105 us -> 12 us
  Pallas kernels: 0 us -> 70 us
  waiting for transfers between devices: 240 us -> 190 us
  between operations: 13.9 us -> 0.25 us
  starting transfers between devices: 10.2 us -> 21.4 us
    slice x36 -> x6, local copies, waits for them, and re-layouts: 118 us -> 1.3 us  [the longest x1 1.08 us: mixer(): halo = from_behind(tokens[rows - 16:], 'seq', 1)]
    pallas_call x0 -> x2, Pallas kernels: none -> 70 us  [the longest x1 38.3 us: mixer(): pl.pallas_call(front_kernel, out_shape=(jax.ShapeDtypeStruct((rows, width...]
    reduce_sum x83 -> x1, other arithmetic: 56.6 us -> 0.09 us  [routed_by_slots(): slot_pos = jnp.sum(before * onehot, axis=1)]
    all_gather x2 -> x0, waiting for transfers between devices: 54.2 us -> none  [prefix(): everything = jax.tree.map(lambda part: lax.all_gather(part, axis), array)]
    add x16 -> x0, other arithmetic: 15.5 us -> none  [block_step(): jnp.exp(step_blk[position][None, :] * decay_neg) * ssm_state]
    ppermute x1 -> x7, starting transfers between devices: 4.84 us -> 16.5 us  [from_behind(): return lax.ppermute(array, axis, pairs)]
    dynamic_update_slice x16 -> x0, local copies, waits for them, and re-layouts: 11.6 us -> none  [local_scan(): final_state, outputs = lax.scan(block_step, start_state, pieces_all)]
    dot_general x4 -> x2, matrix products: 27.8 us -> 20.3 us  [the longest x1 15.9 us: routed_by_slots(): jnp.dot(inner_act, w_down[0], preferred_element_type=jnp.float32)]
  transfers between devices with their start and end apart: 4 -> 8, of which waited for: 4 -> 3; matrix products, arithmetic and copies ran while one was open for 0% -> 1% of each run, Pallas kernels for 0% -> 0%
where the time goes in v1:
time: 564 us; the launch traced here: 563 us
  waiting for transfers between devices  190 us (34%)
  blocking collectives  189 us (34%)
  Pallas kernels  70 us (12%)
  local copies, waits for them, and re-layouts  59.7 us (11%)
  starting transfers between devices  21.4 us (4%)
  matrix products  20.3 us (4%)
  other arithmetic  12 us (2%)
    all_to_all x1, blocking collectives, routed_by_slots(): lax.all_to_all(outgoing, 'expert', split_axis=0, concat_axis=0, tiled=True)  189 us
    all_to_all x1, waiting for transfers between devices, routed_by_slots(): lax.all_to_all(result.reshape(recv_shape), 'expert', split_axis=0, concat...  184 us
    pallas_call x1, Pallas kernels, mixer(): pl.pallas_call(front_kernel, out_shape=(jax.ShapeDtypeStruct((rows, width...  38.3 us
    pallas_call x1, Pallas kernels, mixer(): pl.pallas_call(functools.partial(back_kernel, before=before), out_shape=(...  31.7 us
    ppermute x7, starting transfers between devices, from_behind(): return lax.ppermute(array, axis, pairs)  16.5 us
    dot_general x1, matrix products, routed_by_slots(): jnp.dot(inner_act, w_down[0], preferred_element_type=jnp.float32)  15.9 us
    gather x1, local copies, waits for them, and re-layouts, routed_by_slots(): returned.reshape(experts * capacity, model_width)[dest_row]  13.1 us
    scatter x1, local copies, waits for them, and re-layouts, routed_by_slots(): outgoing = jnp.zeros((experts * capacity, model_width), jnp.bfloat16).at[...  12.4 us
  transfers between devices with their start and end apart: 8, of which 3 were waited for; matrix products, arithmetic and copies ran while one was open for 1% of the time, Pallas kernels for 0%

profile of v1, /device:TPU:0, one launch (start us, length us, event | category | flops | bytes accessed | tf_op | source)
XLA Modules:
  0.0 562.7 jit_solution(6085979847683605956)
XLA Ops:
  1.1 5.0 collective-permute-start
  6.5 2.5 copy.24.low_weight
  9.0 1.3 copy.25.maps_weight
  13.2 38.3 %mixer_front.1 = (bf16[256,4096]{1,0:T(8,128)(2,1)}, f32[8192,128]{1,0:T(8,128)}, f32[8192,128]{1,0:T(8,128)}, f32[256,32]{1,0:T(8,128)}, f32[16,32,128]{2,1,0:T(8,128)}, /*index=5*/f32[32,128]{1,0:T(8,128)}) custom-call(bf16[256,4096]{1,0:T(8,128)(2,1)} %bitcast.59, bf16[16,4096]{1,0:T(8,128)(2,1)} %copy-done.9, f32[1,4096]{1,0:T(1,128)} %bitcast.63, ...), custom_call_target="tpu_custom_call" | custom-call | flops 1342177280 | bytes 20971520 | tf_op jit(solution)/shard_map/mixer_front/pallas_call | solution.py:222
  51.5 3.4 collective-permute-start.1
  55.0 1.9 collective-permute-start.2
  58.2 2.1 collective-permute-start.4
  62.0 4.4 collective-permute-done.4.rest_3_
  66.4 1.5 collective-permute-start.6
  67.9 1.4 collective-permute-done.6.rest_5_
  70.3 31.7 %mixer_back.1 = (f32[256,4096]{1,0:T(8,128)}, bf16[256,4096]{1,0:T(8,128)(2,1)}) custom-call(bf16[256,4096]{1,0:T(8,128)(2,1)} %bitcast.60, bf16[256,4096]{1,0:T(8,128)(2,1)} %get-tuple-element.13.conv_ref, f32[8192,128]{1,0:T(8,128)} %get-tuple-element.14.step_ref, f32[8192,128]{1,0:T(8,128)} %get-tuple-element.15.drive_ref, ...), custom_call_target="tpu_custom_call" | custom-call | flops 268435456 | bytes 20971520 | tf_op jit(solution)/shard_map/mixer_back/pallas_call | solution.py:252
  101.9 6.0 %broadcast_in_dim.13 = bf16[256,2,4096]{2,1,0:T(2,128)(2,1)} broadcast(bf16[256,4096]{1,0:T(8,128)(2,1)} %get-tuple-element.20), dimensions={0,2} | broadcast | bytes 6291456 | tf_op jit(solution)/shard_map/broadcast_in_dim | solution.py:287
  108.0 7.2 %reshape.115 = bf16[512,4096]{1,0:T(8,128)(2,1)} reshape(bf16[256,2,4096]{2,1,0:T(2,128)(2,1)} %broadcast_in_dim.13) | data formatting | bytes 8388608 | tf_op jit(solution)/shard_map/reshape | solution.py:287
  115.1 12.4 %scatter_custom_fusion = bf16[1024,4096]{1,0:T(8,128)(2,1)} fusion(s32[512]{0:T(512)S(1)} %bitcast.57, bf16[512,4096]{1,0:T(8,128)(2,1)} %reshape.115, bf16[]{:T(256)} %constant.4.clone.1), kind=kCustom, calls=%fused_computation.13 | custom fusion | bytes 8389120 | tf_op jit(solution)/shard_map/scatter | solution.py:287
  127.6 189.3 %all_to_all.10 = bf16[8,128,4096]{2,1,0:T(8,128)(2,1)S(1)} all-to-all(bf16[8,128,4096]{2,1,0:T(8,128)(2,1)} %bitcast.51), channel_id=1, replica_groups=mesh['seq'=4,'expert'=8] {'expert'}, dimensions={0} | all-to-all | bytes 16777216 | tf_op jit(solution)/shard_map/all_to_all | solution.py:290
  316.8 3.2 copy-done
  320.1 4.5 fusion.6
  324.5 15.9 %convolution_convert_fusion = bf16[1024,4096]{1,0:T(8,128)(2,1)} fusion(bf16[1,512,4096]{2,1,0:T(8,128)(2,1)} %param.29, f32[1024,512]{1,0:T(8,128)S(1)} %fusion.6, bf16[1024,4096]{1,0:T(8,128)(2,1)} %bitcast.54, bf16[1,4096,512]{2,1,0:T(8,128)(2,1)} %param.28), kind=kOutput, calls=%fused_computation.3 | convolution fusion | flops 8597274624 | bytes 27262976 | tf_op jit(solution)/shard_map/dot_general | solution.py:296
  340.4 5.0 all-to-all-start.1
  345.4 183.9 %all-to-all-done.1 = bf16[8,128,4096]{2,1,0:T(8,128)(2,1)} async-done(((bf16[8,128,4096]{2,1,0:T(8,128)(2,1)}), bf16[8,128,4096]{2,1,0:T(8,128)(2,1)}, u32[]{:S(2)}, u32[]{:S(2)}) %all-to-all-start.1) | async-done | bytes 8388640 | tf_op jit(solution)/shard_map/all_to_all | solution.py:297
  529.3 13.1 %gather_fusion = bf16[512,4096]{1,0:T(8,128)(2,1)} fusion(bf16[1024,4096]{1,0:T(8,128)(2,1)} %bitcast.18, s32[1024]{0:T(1024)S(1)} %pad_clamp_fusion), kind=kCustom, calls=%fused_computation | custom fusion | bytes 8390656 | tf_op jit(solution)/shard_map/gather | solution.py:300
  542.3 9.7 %reshape.102 = f32[256,2,4096]{2,1,0:T(2,128)} reshape(bf16[512,4096]{1,0:T(8,128)(2,1)} %gather_fusion) | data formatting | bytes 12582912 | tf_op jit(solution)/shard_map/convert_element_type | solution.py:300
  552.0 8.5 %copy_multiply_fusion = f32[256,2,4096]{2,0,1:T(8,128)S(1)} fusion(f32[256,2,4096]{2,1,0:T(2,128)} %reshape.102, f32[256,2]{0,1:T(2,128)S(1)} %bitcast.62), kind=kLoop, calls=%fused_computation.2 | loop fusion | flops 2097152 | bytes 16779264 | tf_op jit(solution)/shard_map/mul | solution.py:301
  560.6 2.2 fusion.10
  (53 shorter events, 8.2 us)
Async XLA Ops:
  0.0 6.5 %slice-start = ((bf16[4096,288]{0,1:T(8,128)(2,1)}), bf16[4096,256]{0,1:T(8,128)(2,1)S(1)}, s32[]{:S(2)}) async-start(bf16[4096,288]{0,1:T(8,128)(2,1)} %param.19), calls=%async_computation.2 | async-start | bytes 4194304 | tf_op jit(solution)/shard_map/slice | solution.py:247
  0.0 6.1 %copy-start.3 = (s32[1,256,2]{1,2,0:T(2,128)S(1)}, s32[1,256,2]{1,2,0:T(2,128)}, u32[]{:S(2)}) copy-start(s32[1,256,2]{1,2,0:T(2,128)} %param.25) | copy-start | bytes 6148
  1.1 7.9 %slice-start.1 = ((bf16[4096,288]{0,1:T(8,128)(2,1)}), bf16[4096,32]{0,1:T(8,128)(2,1)S(1)}, s32[]{:S(2)}) async-start(bf16[4096,288]{0,1:T(8,128)(2,1)} %param.19), calls=%async_computation.3 | async-start | bytes 524288 | tf_op jit(solution)/shard_map/slice | solution.py:247
  1.1 11.4 %collective-permute-start = (bf16[16,4096]{1,0:T(8,128)(2,1)S(1)}, bf16[16,4096]{1,0:T(8,128)(2,1)S(1)}, u32[]{:S(2)}, u32[]{:S(2)}) collective-permute-start(bf16[16,4096]{1,0:T(8,128)(2,1)S(1)} %slice_bitcast_fusion), channel_id=1, source_target_pairs={{0,8},{8,16},{16,24},{1,9},{9,17},{17,25},{2,10},{10,18},{18,26},{... | collective-permute-start | bytes 393224 | tf_op jit(solution)/shard_map/ppermute | solution.py:19
  6.1 4.3 copy-start.2
  12.5 0.7 copy-start.9
  51.5 17.8 %collective-permute-start.1 = (f32[16,32,128]{2,1,0:T(8,128)}, f32[16,32,128]{2,1,0:T(8,128)S(1)}, u32[]{:S(2)}, u32[]{:S(2)}) collective-permute-start(f32[16,32,128]{2,1,0:T(8,128)} %get-tuple-element.17), channel_id=1, source_target_pairs={{0,8},{8,16},{16,24},{1,9},{9,17},{17,25},{2,10},{10,18},{18,26},{... | collective-permute-start | bytes 786440 | tf_op jit(solution)/shard_map/ppermute | solution.py:19
  55.0 14.4 %collective-permute-start.2 = (f32[16,32,128]{2,1,0:T(8,128)}, f32[16,32,128]{2,1,0:T(8,128)S(1)}, u32[]{:S(2)}, u32[]{:S(2)}) collective-permute-start(f32[16,32,128]{2,1,0:T(8,128)} %get-tuple-element.17), channel_id=1, source_target_pairs={{0,16},{8,24},{1,17},{9,25},{2,18},{10,26},{3,19},{11,27},{4,20},{... | collective-permute-start | bytes 786440 | tf_op jit(solution)/shard_map/ppermute | solution.py:19
  56.9 12.5 %collective-permute-start.3 = (f32[16,32,128]{2,1,0:T(8,128)}, f32[16,32,128]{2,1,0:T(8,128)S(1)}, u32[]{:S(2)}, u32[]{:S(2)}) collective-permute-start(f32[16,32,128]{2,1,0:T(8,128)} %get-tuple-element.17), channel_id=1, source_target_pairs={{0,24},{1,25},{2,26},{3,27},{4,28},{5,29},{6,30},{7,31}} | collective-permute-start | bytes 786440 | tf_op jit(solution)/shard_map/ppermute | solution.py:19
  58.2 8.2 %collective-permute-start.4 = (f32[32,128]{1,0:T(8,128)}, f32[32,128]{1,0:T(8,128)S(1)}, u32[]{:S(2)}, u32[]{:S(2)}) collective-permute-start(f32[32,128]{1,0:T(8,128)} %get-tuple-element.18), channel_id=1, source_target_pairs={{0,8},{8,16},{16,24},{1,9},{9,17},{17,25},{2,10},{10,18},{18,26},{... | collective-permute-start | bytes 49160 | tf_op jit(solution)/shard_map/ppermute | solution.py:19
  60.7 7.2 %collective-permute-start.5 = (f32[32,128]{1,0:T(8,128)}, f32[32,128]{1,0:T(8,128)S(1)}, u32[]{:S(2)}, u32[]{:S(2)}) collective-permute-start(f32[32,128]{1,0:T(8,128)} %get-tuple-element.18), channel_id=1, source_target_pairs={{0,16},{8,24},{1,17},{9,25},{2,18},{10,26},{3,19},{11,27},{4,20},{... | collective-permute-start | bytes 49160 | tf_op jit(solution)/shard_map/ppermute | solution.py:19
  66.4 3.0 copy-start.10
  66.4 2.9 collective-permute-start.6
  67.9 1.5 copy-start.11
  69.4 0.6 copy-start.12
  69.4 0.7 copy-start.6
  69.4 0.8 copy-start.7
  69.4 0.9 copy-start.8
  127.6 192.5 %copy-start.5 = (bf16[1,4096,512]{2,1,0:T(8,128)(2,1)S(1)}, bf16[1,4096,512]{2,1,0:T(8,128)(2,1)}, u32[]{:S(2)}) copy-start(bf16[1,4096,512]{2,1,0:T(8,128)(2,1)} %param.27) | copy-start | bytes 12582916
  316.8 3.2 copy-start
  340.4 188.8 %all-to-all-start.1 = ((bf16[8,128,4096]{2,1,0:T(8,128)(2,1)}), bf16[8,128,4096]{2,1,0:T(8,128)(2,1)}, u32[]{:S(2)}, u32[]{:S(2)}) async-start(bf16[8,128,4096]{2,1,0:T(8,128)(2,1)} %bitcast.52), calls=%async_computation.1 | async-start | bytes 16777216 | tf_op jit(solution)/shard_map/all_to_all | solution.py:297
  542.3 9.7 %copy-start.4 = (f32[1,256,2]{1,2,0:T(2,128)S(1)}, f32[1,256,2]{1,2,0:T(2,128)}, u32[]{:S(2)}) copy-start(f32[1,256,2]{1,2,0:T(2,128)} %param.26) | copy-start | bytes 6148
  552.0 8.5 %copy-start.1 = (f32[256,4096]{1,0:T(8,128)S(1)}, f32[256,4096]{1,0:T(8,128)}, u32[]{:S(2)}) copy-start(f32[256,4096]{1,0:T(8,128)} %get-tuple-element.19) | copy-start | bytes 12582916

commit v2 on v1

--- a/solution.py
+++ b/solution.py
@@ -11,6 +11,38 @@
 LANES = 128
 GROUP = 8
 LOG2E = math.log2(math.e)
+VMEM_LIMIT = 56 * 2**20
+COST = 0.5
+DEEP = (1536, 1024, 1536)
+BROAD = (1024, 1024, 1024, 1024)
+PANEL = 1024
+CORNERS_X = (0, 2)
+STARTS = {
+    "z1": ["front"], "x0": ["front"], "y0": ["front"], "w2": ["front"],
+    "z2": ["ends"],
+    "x1": ["e1", "e2", "e3"], "y1": ["e1", "e2", "e3"], "c0": ["e1", "e2", "e3"],
+    "z3": ["back0"], "x2": ["back0"], "y2": ["back0"],
+    "z4": ["back1"], "c1": ["back1"], "c2": ["back1"], "m0": ["t0"],
+    "x3": ["n0"], "y3": ["n0"], "z5": ["n0"], "m1": ["n0"],
+    "z6": ["near0"], "x4": ["near0"], "y4": ["near0"], "c3": ["near0"],
+    "x5": ["far0"], "y5": ["far0"], "c4": ["far0"],
+    "x6": ["near1"], "y6": ["near1"], "c5": ["near1"],
+    "c6": ["far1"],
+}
+WAITS = {
+    "front": ["z0", "w1"],
+    "ends": ["x0", "y0", "z1", "w2"],
+    "back0": ["z2", "x1", "y1"],
+    "back1": ["z3", "x2", "y2", "c0"],
+    "near0": ["x3", "y3", "z5", "m1"],
+    "far0": ["x4", "y4", "c3", "z6"],
+    "near1": ["x5", "y5", "c4"],
+    "far1": ["x6", "y6", "c5"],
+    "down0": ["c6"],
+    "down1": ["s0"],
+    "down2": ["s1"],
+    "down3": ["s2", "r0"],
+}
 
 
 def from_behind(array, axis, by):
@@ -32,16 +64,23 @@
         target[n] = jnp.broadcast_to(maps[:, first + n : first + n + 1], (rows, LANES))
 
 
+def cost(micros):
+    return pl.CostEstimate(flops=int(micros * 1.15e9), bytes_accessed=2**16, transcendentals=0)
+
+
+def params():
+    return pltpu.CompilerParams(vmem_limit_bytes=VMEM_LIMIT)
+
+
 def front_kernel(
-    tok_ref, halo_ref, norm_gain, conv_weight, conv_bias, low_weight, maps_weight,
-    dt_weight, dt_bias, decay,
-    conv_ref, step_ref, drive_ref, maps_ref, end_ref, total_ref,
-    normed, low, block, in_rows,
+    tok_ref, halo_ref, norm_gain, conv_weight, conv_bias, proj_weight, dt_weight, dt_bias,
+    conv_ref, step_ref, drive_ref, maps_ref,
+    normed, low, block,
 ):
     rows, width = tok_ref.shape
     halo = halo_ref.shape[0]
-    states = decay.shape[0]
     taps = conv_weight.shape[0]
+    low_width = dt_weight.shape[0]
     tiles = width // LANES
     gain = norm_gain[...]
 
@@ -78,11 +117,11 @@
 
     conv_all = conv_ref[...]
     low[...] = jnp.dot(
-        conv_all, low_weight[...], preferred_element_type=jnp.float32
+        conv_all, proj_weight[:, :low_width], preferred_element_type=jnp.float32
     ).astype(jnp.bfloat16)
-    maps = jnp.dot(conv_all, maps_weight[...], preferred_element_type=jnp.float32)
-    maps_ref[...] = maps
-    spread_columns(maps, in_rows, 0, states, rows)
+    maps_ref[...] = jnp.dot(
+        conv_all, proj_weight[:, low_width:], preferred_element_type=jnp.float32
+    )
 
     def step_chunk(c, _):
         cols = pl.ds(pl.multiple_of(c * chunk, chunk), chunk)
@@ -108,40 +147,50 @@
 
     lax.fori_loop(0, width // chunk, step_chunk, 0)
 
-    def scan_tile(k, _):
-        mine = pl.ds(pl.multiple_of(k * GROUP, GROUP), GROUP)
-        rates = [decay[n, mine, :] for n in range(states)]
-
-        def advance(i, carry):
-            state, total = carry
-            for p in range(4):
-                t = i * 4 + p
-                here = pl.ds(pl.multiple_of(t * tiles + k * GROUP, GROUP), GROUP)
-                step, drive = step_ref[here, :], drive_ref[here, :]
-                total = total + step
-                state = tuple(
-                    jnp.exp2(step * rates[n]) * state[n] + drive * in_rows[n, pl.ds(t, 1), :]
-                    for n in range(states)
-                )
-            return state, total
-
-        zero = jnp.zeros((GROUP, LANES), jnp.float32)
-        state, total = lax.fori_loop(0, rows // 4, advance, ((zero,) * states, zero))
-        for n in range(states):
-            end_ref[n, mine, :] = state[n]
-        total_ref[mine, :] = total
-        return 0
-
-    lax.fori_loop(0, tiles // GROUP, scan_tile, 0)
+
+def advance_state(state, step, drive, rates, in_rows, t):
+    return tuple(
+        jnp.exp2(step * rates[n]) * state[n] + drive * in_rows[n, pl.ds(t, 1), :]
+        for n in range(len(rates))
+    )
+
+
+def ends_kernel(step_ref, drive_ref, maps_ref, decay, end_ref, in_rows):
+    rows = step_ref.shape[0]
+    states = decay.shape[0]
+
+    @pl.when(pl.program_id(0) == 0)
+    def _():
+        spread_columns(maps_ref[...], in_rows, 0, states, rows)
+
+    rates = [decay[n] for n in range(states)]
+
+    def advance(i, carry):
+        state, total = carry
+        for p in range(4):
+            t = i * 4 + p
+            step = step_ref[t]
+            total = total + step
+            state = advance_state(state, step, drive_ref[t], rates, in_rows, t)
+        return state, total
+
+    zero = jnp.zeros((GROUP, LANES), jnp.float32)
+    state, total = lax.fori_loop(0, rows // 4, advance, ((zero,) * states, zero))
+    for n in range(states):
+        end_ref[n] = state[n]
+    end_ref[states] = total
 
 
 def back_kernel(
     tok_ref, conv_ref, step_ref, drive_ref, maps_ref, decay, skip_gain, ffn_gain, *rest,
-    before,
+    before, final,
 ):
-    ends, totals = rest[:before], rest[before : 2 * before]
-    hidden_ref, ffn_ref = rest[2 * before : 2 * before + 2]
-    in_rows, out_rows, scanned = rest[2 * before + 2 :]
+    count = max(before, 1)
+    entry, rest = rest[:count], rest[count:]
+    if final:
+        hidden_ref, ffn_ref, kept, in_rows, out_rows, scanned = rest
+    else:
+        hidden_ref, ffn_ref, state_ref, kept, in_rows, out_rows, scanned = rest
     rows, width = tok_ref.shape
     states = decay.shape[0]
     tiles = width // LANES
@@ -149,38 +198,45 @@
     spread_columns(maps, in_rows, 0, states, rows)
     spread_columns(maps, out_rows, states, states, rows)
 
+    @pl.when(pl.program_id(0) == 0)
+    def _():
+        if not before:
+            kept[...] = entry[0][...]
+            return
+
+        def enter(n, _):
+            entering = entry[before - 1][n]
+            for back in reversed(range(before - 1)):
+                entering = jnp.exp2(entry[back][states] * decay[n]) * entering + entry[back][n]
+            kept[n] = entering
+            return 0
+
+        lax.fori_loop(0, states, enter, 0)
+
     def scan_tile(k, _):
         mine = pl.ds(pl.multiple_of(k * GROUP, GROUP), GROUP)
         rates = [decay[n, mine, :] for n in range(states)]
-        start = []
-        for n in range(states):
-            entering = jnp.zeros((GROUP, LANES), jnp.float32)
-            for back in reversed(range(before)):
-                entering = (
-                    jnp.exp2(totals[back][mine, :] * rates[n]) * entering
-                    + ends[back][n, mine, :]
-                )
-            start.append(entering)
 
         def advance(i, state):
             for p in range(4):
                 t = i * 4 + p
-                here = pl.ds(pl.multiple_of(t * tiles + k * GROUP, GROUP), GROUP)
-                step, drive = step_ref[here, :], drive_ref[here, :]
-                state = tuple(
-                    jnp.exp2(step * rates[n]) * state[n] + drive * in_rows[n, pl.ds(t, 1), :]
-                    for n in range(states)
+                state = advance_state(
+                    state, step_ref[t, mine, :], drive_ref[t, mine, :], rates, in_rows, t
                 )
                 parts = [state[n] * out_rows[n, pl.ds(t, 1), :] for n in range(states)]
                 while len(parts) > 1:
                     parts = [a + b for a, b in zip(parts[::2], parts[1::2])]
-                scanned[here, :] = parts[0]
+                scanned[pl.ds(pl.multiple_of(t * tiles + k * GROUP, GROUP), GROUP), :] = parts[0]
             return state
 
-        lax.fori_loop(0, rows // 4, advance, tuple(start))
+        state = lax.fori_loop(0, rows // 4, advance, tuple(kept[n, mine, :] for n in range(states)))
+        for n in range(states):
+            kept[n, mine, :] = state[n]
         return 0
 
     lax.fori_loop(0, tiles // GROUP, scan_tile, 0)
+    if not final:
+        state_ref[...] = kept[...]
 
     def finish(i, _):
         at = pl.multiple_of(i * 16, 16)
@@ -209,66 +265,315 @@
 
 def mixer(
     tokens, norm_gain, conv_weight, conv_bias, proj_weight, dt_weight, dt_bias, decay_rate,
-    skip_gain, ffn_gain,
+    skip_gain, ffn_gain, parts, hold, note,
 ):
     rows, width = tokens.shape
     states = decay_rate.shape[0]
     low_width = dt_weight.shape[0]
     tiles = width // LANES
-    f32 = jnp.float32
+    f32, bf16 = jnp.float32, jnp.bfloat16
+    shape = jax.ShapeDtypeStruct
     halo = from_behind(tokens[rows - 16 :], "seq", 1)
     decay = (decay_rate * (-LOG2E)).reshape(states, tiles, LANES)
     row = lambda v: v.reshape(1, width)
-    conv, step, drive, maps, end, total = pl.pallas_call(
+    conv, step, drive, maps = pl.pallas_call(
         front_kernel,
         out_shape=(
-            jax.ShapeDtypeStruct((rows, width), jnp.bfloat16),
-            jax.ShapeDtypeStruct((rows * tiles, LANES), f32),
-            jax.ShapeDtypeStruct((rows * tiles, LANES), f32),
-            jax.ShapeDtypeStruct((rows, 2 * states), f32),
-            jax.ShapeDtypeStruct((states, tiles, LANES), f32),
-            jax.ShapeDtypeStruct((tiles, LANES), f32),
+            shape((rows, width), bf16),
+            shape((rows * tiles, LANES), f32),
+            shape((rows * tiles, LANES), f32),
+            shape((rows, 2 * states), f32),
         ),
         scratch_shapes=[
             pltpu.VMEM((rows + 16, width), f32),
-            pltpu.VMEM((rows, low_width), jnp.bfloat16),
+            pltpu.VMEM((rows, low_width), bf16),
             pltpu.VMEM((rows, 512), f32),
-            pltpu.VMEM((states, rows, LANES), f32),
         ],
-        compiler_params=pltpu.CompilerParams(vmem_limit_bytes=56 * 2**20),
-        cost_estimate=pl.CostEstimate(
-            flops=2 * rows * width * (2 * low_width + 8 * states),
-            bytes_accessed=20 * 2**20,
-            transcendentals=rows * width * states,
-        ),
+        compiler_params=params(),
+        cost_estimate=cost(COST),
         name="mixer_front",
     )(
         tokens, halo, row(norm_gain), conv_weight, row(conv_bias),
-        proj_weight[:, :low_width], proj_weight[:, low_width:], dt_weight, row(dt_bias), decay,
-    )
+        proj_weight, dt_weight, row(dt_bias),
+    )
+    conv, step, drive, maps = hold("front", conv, step, drive, maps)
+    step = step.reshape(rows, tiles, LANES)
+    drive = drive.reshape(rows, tiles, LANES)
+    slab = pl.BlockSpec((rows, GROUP, LANES), lambda k: (0, k, 0))
+    per_state = pl.BlockSpec((states, GROUP, LANES), lambda k: (0, k, 0))
+    ended = pl.BlockSpec((states + 1, GROUP, LANES), lambda k: (0, k, 0))
+    end = pl.pallas_call(
+        ends_kernel,
+        grid=(tiles // GROUP,),
+        out_shape=shape((states + 1, tiles, LANES), f32),
+        in_specs=[slab, slab, pl.BlockSpec((rows, 2 * states), lambda k: (0, 0)), per_state],
+        out_specs=ended,
+        scratch_shapes=[pltpu.VMEM((states, rows, LANES), f32)],
+        compiler_params=params(),
+        cost_estimate=cost(COST),
+        name="mixer_ends",
+    )(step, drive, maps, decay)
+    end, = hold("ends", end)
     before = lax.axis_size("seq") - 1
-    ends = [from_behind(end, "seq", by + 1) for by in range(before)]
-    totals = [from_behind(total, "seq", by + 1) for by in range(before)]
-    hidden, ffn_in = pl.pallas_call(
-        functools.partial(back_kernel, before=before),
+    ends = [note(f"e{by + 1}", from_behind(end, "seq", by + 1)) for by in range(before)]
+
+    count = rows // parts
+    piece = min(64, count)
+    steps = count // piece
+    outs = []
+    state = None
+    for part in range(parts):
+        first = part * steps
+        wide = pl.BlockSpec((piece, width), lambda i, first=first: (first + i, 0))
+        deep = pl.BlockSpec((piece, tiles, LANES), lambda i, first=first: (first + i, 0, 0))
+        narrow = pl.BlockSpec((piece, 2 * states), lambda i, first=first: (first + i, 0))
+        whole = lambda v: pl.BlockSpec(v.shape, lambda i, r=v.ndim: (0,) * r)
+        out = pl.BlockSpec((piece, width), lambda i: (i, 0))
+        entry = ends if part == 0 else [state]
+        final = part == parts - 1
+        fixed = [decay, row(skip_gain), row(ffn_gain), *entry]
+        got = pl.pallas_call(
+            functools.partial(back_kernel, before=before if part == 0 else 0, final=final),
+            grid=(steps,),
+            out_shape=(shape((count, width), f32), shape((count, width), bf16))
+            + (() if final else (shape(decay.shape, f32),)),
+            in_specs=[wide, wide, deep, deep, narrow] + [whole(v) for v in fixed],
+            out_specs=(out, out) + (() if final else (whole(decay),)),
+            scratch_shapes=[
+                pltpu.VMEM((states, tiles, LANES), f32),
+                pltpu.VMEM((states, piece, LANES), f32),
+                pltpu.VMEM((states, piece, LANES), f32),
+                pltpu.VMEM((piece * tiles, LANES), f32),
+            ],
+            compiler_params=params(),
+            cost_estimate=cost(COST),
+            name="mixer_back",
+        )(tokens, conv, step, drive, maps, *fixed)
+        got = hold(f"back{part}", *got)
+        outs.append(got[:2])
+        state = got[2] if not final else None
+    return [o[0] for o in outs], [o[1] for o in outs]
+
+
+def swap(array, axis, mask):
+    peers = lax.axis_size(axis)
+    return lax.ppermute(array, axis, [(i, i ^ mask) for i in range(peers)])
+
+
+def after(array, *others):
+    return lax.optimization_barrier((array, *others))[0]
+
+
+class Transfers:
+    def __init__(self, w_gate, w_up, w_down):
+        share = w_gate.shape[1] // lax.axis_size("seq")
+        at = lax.axis_index("seq") * share
+        both = jnp.concatenate(
+            [lax.dynamic_slice_in_dim(w, at, share, axis=1) for w in (w_gate, w_up)], axis=1
+        )
+        down = lax.dynamic_slice_in_dim(w_down, at, share, axis=0)
+        self.chunks = []
+        for whole, sizes, axis in ((both, DEEP, 0), (down, BROAD, 1)):
+            at = 0
+            for size in sizes:
+                self.chunks.append(lax.slice_in_dim(whole, at, at + size, axis=axis))
+                at += size
+        self.made = {}
+
+    def put(self, name, array, axis, mask):
+        self.made[name] = swap(self.ready(name, array), axis, mask)
+        return self.made[name]
+
+    def ready(self, name, array):
+        return after(array, *[self.get(other) for other in STARTS.get(name, ())])
+
+    def note(self, name, array):
+        self.made[name] = array
+        return array
+
+    def weigh(self, chosen, route_scale):
+        experts = jnp.arange(lax.axis_size("expert"), dtype=jnp.int32)[:, None, None]
+        self.dense = jnp.sum(jnp.where(chosen[None] == experts, route_scale[None], 0.0), axis=2)
+
+    def get(self, name):
+        if name not in self.made:
+            kind, c = name[0], int(name[1:])
+            if name == "w1":
+                send, axis, mask = self.dense, "expert", 1
+            elif name == "w2":
+                self.pair = jnp.concatenate([self.dense, self.get("w1")], axis=1)
+                send, axis, mask = self.pair, "expert", 2
+            elif kind == "z":
+                send, axis, mask = self.chunks[c], "expert", 4
+            elif kind == "x":
+                send, axis, mask = self.get(f"z{c}"), "seq", 1
+            elif kind == "y":
+                send, axis, mask = self.get(f"z{c}"), "seq", 2
+            elif c in CORNERS_X:
+                send, axis, mask = self.get(f"y{c}"), "seq", 1
+            else:
+                send, axis, mask = self.get(f"x{c}"), "seq", 2
+            self.put(name, send, axis, mask)
+        return self.made[name]
+
+    def pieces(self, c):
+        return [self.get(f"{kind}{c}") for kind in "zxyc"]
+
+    def hold(self, kernel, *arrays):
+        self.made[kernel] = arrays[-1]
+        others = [self.get(name) for name in WAITS.get(kernel, ())]
+        return lax.optimization_barrier((*arrays, *others))[: len(arrays)]
+
+
+def near_act_kernel(*refs, blocks):
+    xs, (gate, up, scale, act_ref, rows_in) = refs[:blocks], refs[blocks:]
+    count = xs[0].shape[0]
+
+    @pl.when(pl.program_id(0) == 0)
+    def _():
+        for b in range(blocks):
+            rows_in[b * count : (b + 1) * count, :] = xs[b][...]
+
+    g = jnp.dot(rows_in[...], gate[...], preferred_element_type=jnp.float32)
+    u = jnp.dot(rows_in[...], up[...], preferred_element_type=jnp.float32)
+    act_ref[...] = (silu(g) * u * scale[:, 0:1]).astype(jnp.bfloat16)
+
+
+def near_act(xs, w_gate, w_up, scale):
+    rows = sum(x.shape[0] for x in xs)
+    width, hidden = w_gate.shape
+    tile = 256
+    whole = lambda v: pl.BlockSpec(v.shape, lambda i: (0, 0))
+    cols = pl.BlockSpec((width, tile), lambda i: (0, i))
+    return pl.pallas_call(
+        functools.partial(near_act_kernel, blocks=len(xs)),
+        grid=(hidden // tile,),
+        out_shape=jax.ShapeDtypeStruct((rows, hidden), jnp.bfloat16),
+        in_specs=[whole(x) for x in xs] + [cols, cols, whole(scale)],
+        out_specs=pl.BlockSpec((rows, tile), lambda i: (0, i)),
+        scratch_shapes=[pltpu.VMEM((rows, width), jnp.bfloat16)],
+        compiler_params=params(),
+        cost_estimate=cost(COST),
+        name="near_act",
+    )(*xs, w_gate, w_up, scale)
+
+
+def far_act_kernel(*refs, blocks, deep):
+    xs, refs = refs[:blocks], refs[blocks:]
+    weights, (scale, act_ref, rows_in) = refs[: 4 * deep], refs[4 * deep :]
+    count = xs[0].shape[0]
+    for b in range(blocks):
+        rows_in[b * count : (b + 1) * count, :] = xs[b][...]
+    share = weights[0].shape[1] // 2
+    for origin in range(4):
+        total, at = None, 0
+        for c in range(deep):
+            weight = weights[4 * c + origin]
+            term = jnp.dot(
+                rows_in[:, at : at + weight.shape[0]], weight[...],
+                preferred_element_type=jnp.float32,
+            )
+            total = term if total is None else total + term
+            at += weight.shape[0]
+        act_ref[:, origin * share : (origin + 1) * share] = (
+            silu(total[:, :share]) * total[:, share:] * scale[:, 1:2]
+        ).astype(jnp.bfloat16)
+
+
+def far_act(xs, chunks, scale):
+    rows = sum(x.shape[0] for x in xs)
+    width = xs[0].shape[1]
+    share = chunks[0][0].shape[1] // 2
+    pieces = [piece for chunk in chunks for piece in chunk]
+    return pl.pallas_call(
+        functools.partial(far_act_kernel, blocks=len(xs), deep=len(chunks)),
+        out_shape=jax.ShapeDtypeStruct((rows, 4 * share), jnp.bfloat16),
+        scratch_shapes=[pltpu.VMEM((rows, width), jnp.bfloat16)],
+        compiler_params=params(),
+        cost_estimate=cost(COST),
+        name="far_act",
+    )(*xs, *pieces, scale)
+
+
+def down_kernel(*refs, halves):
+    nears, fars, refs = refs[:halves], refs[halves : 2 * halves], refs[2 * halves :]
+    near_weight, pieces, (keep_ref, send_ref) = refs[0], refs[1:5], refs[5:]
+    far_weight = jnp.concatenate([p[...] for p in pieces], axis=0)
+    for h in range(halves):
+        total = jnp.dot(nears[h][...], near_weight[...], preferred_element_type=jnp.float32)
+        total = total + jnp.dot(fars[h][...], far_weight, preferred_element_type=jnp.float32)
+        count = total.shape[0] // 4
+        own, mate, ahead, ahead_mate = [total[b * count : (b + 1) * count] for b in range(4)]
+        rows = count * halves
+        keep_ref[h * count : (h + 1) * count, :] = own
+        keep_ref[rows + h * count : rows + (h + 1) * count, :] = ahead
+        send_ref[h * count : (h + 1) * count, :] = mate.astype(jnp.bfloat16)
+        send_ref[rows + h * count : rows + (h + 1) * count, :] = ahead_mate.astype(jnp.bfloat16)
+
+
+def down(nears, fars, w_down, pieces, c, panel):
+    cols, share = PANEL, pieces[0].shape[0]
+    hidden = w_down.shape[0]
+    rows = 2 * sum(a.shape[0] // 4 for a in nears)
+    whole = lambda v: pl.BlockSpec(v.shape, lambda i: (0, 0))
+    fixed = [*nears, *fars]
+    return pl.pallas_call(
+        functools.partial(down_kernel, halves=len(nears)),
+        grid=(1,),
         out_shape=(
-            jax.ShapeDtypeStruct((rows, width), f32),
-            jax.ShapeDtypeStruct((rows, width), jnp.bfloat16),
+            jax.ShapeDtypeStruct((rows, cols), jnp.float32),
+            jax.ShapeDtypeStruct((rows, cols), jnp.bfloat16),
         ),
-        scratch_shapes=[
-            pltpu.VMEM((states, rows, LANES), f32),
-            pltpu.VMEM((states, rows, LANES), f32),
-            pltpu.VMEM((rows * tiles, LANES), f32),
-        ],
-        compiler_params=pltpu.CompilerParams(vmem_limit_bytes=56 * 2**20),
-        cost_estimate=pl.CostEstimate(
-            flops=2 * rows * width * 8 * states,
-            bytes_accessed=20 * 2**20,
-            transcendentals=rows * width * states,
+        in_specs=[whole(v) for v in fixed]
+        + [pl.BlockSpec((hidden, cols), lambda i: (0, c))]
+        + [pl.BlockSpec((share, cols), lambda i: (0, panel)) for _ in pieces],
+        out_specs=(
+            pl.BlockSpec((rows, cols), lambda i: (0, 0)),
+            pl.BlockSpec((rows, cols), lambda i: (0, 0)),
         ),
-        name="mixer_back",
-    )(tokens, conv, step, drive, maps, decay, row(skip_gain), row(ffn_gain), *ends, *totals)
-    return hidden, ffn_in
+        compiler_params=params(),
+        cost_estimate=cost(COST),
+        name="down",
+    )(*fixed, w_down, *pieces)
+
+
+def routed_by_weights(hidden, ffn_in, w_gate, w_up, w_down, moves):
+    me = lax.axis_index("expert")
+    far = moves.get("w2")
+    group = jnp.concatenate([moves.pair, far], axis=1)
+    scale = jnp.stack([group[me], group[me ^ 4]], axis=1)
+    rows = hidden[0].shape[0] * len(hidden)
+    halves = len(ffn_in)
+    count = rows // halves
+    nears, fars = [], []
+    order = None
+    ahead = [moves.put(f"t{h}", ffn_in[h], "expert", 2) for h in range(halves)]
+    for h in range(halves):
+        mate = moves.put(f"m{h}", ffn_in[h], "expert", 1)
+        ahead_mate = moves.put(f"n{h}", ahead[h], "expert", 1)
+        xs = [ffn_in[h], mate, ahead[h], ahead_mate]
+        part = scale.reshape(4, halves, count, 2)[:, h].reshape(4 * count, 2)
+        part = part if order is None else after(part, order)
+        near, = moves.hold(f"near{h}", near_act(xs, w_gate, w_up, part))
+        nears.append(near)
+        deep_chunks = [moves.pieces(c) for c in range(len(DEEP))]
+        order, = moves.hold(f"far{h}", far_act(xs, deep_chunks, after(part, near)))
+        fars.append(order)
+    columns = []
+    whole_hidden = jnp.concatenate(hidden, axis=0)
+    for c, wide in enumerate(BROAD):
+        pieces = moves.pieces(len(DEEP) + c)
+        for panel in range(wide // PANEL):
+            d = len(columns)
+            cols = slice(d * PANEL, (d + 1) * PANEL)
+            held = [after(pieces[0], order), *pieces[1:]]
+            keep, send = moves.hold(f"down{d}", *down(nears, fars, w_down, held, d, panel))
+            order = send
+            came = moves.put(f"s{d}", send, "expert", 1).astype(jnp.float32)
+            back = (keep[rows:] + came[rows:]).astype(jnp.bfloat16)
+            back = moves.put(f"r{d}", back, "expert", 2).astype(jnp.float32)
+            columns.append(whole_hidden[:, cols] + ((keep[:rows] + came[:rows]) + back))
+    return jnp.concatenate(columns, axis=1)
 
 
 def routed_by_slots(ffn_in, chosen, route_scale, w_gate, w_up, w_down):
@@ -306,12 +611,26 @@
     tokens, norm_gain, conv_weight, conv_bias, proj_weight, dt_weight, dt_bias, decay_rate,
     skip_gain, ffn_gain, expert_ids, route_weights, w_gate, w_up, w_down,
 ):
+    by_weights = lax.axis_size("expert") == 8 and lax.axis_size("seq") == 4
+    hold = lambda kernel, *arrays: arrays
+    note = lambda name, array: array
+    if by_weights:
+        moves = Transfers(w_gate[0], w_up[0], w_down[0])
+        moves.weigh(expert_ids[0], route_weights[0])
+        hold, note = moves.hold, moves.note
     hidden, ffn_in = mixer(
         tokens[0], norm_gain, conv_weight, conv_bias, proj_weight, dt_weight, dt_bias,
-        decay_rate, skip_gain, ffn_gain,
-    )
-    routed = routed_by_slots(ffn_in, expert_ids[0], route_weights[0], w_gate, w_up, w_down)
-    return (hidden + routed).astype(jnp.bfloat16)[None]
+        decay_rate, skip_gain, ffn_gain, 2 if by_weights else 1, hold, note,
+    )
+    if by_weights:
+        out = routed_by_weights(
+            hidden, ffn_in, w_gate[0], w_up[0], w_down[0], moves
+        )
+    else:
+        out = hidden[0] + routed_by_slots(
+            ffn_in[0], expert_ids[0], route_weights[0], w_gate, w_up, w_down
+        )
+    return out.astype(jnp.bfloat16)[None]
 
 
 def solution(mesh):

time: 564 us -> 323 us (0.57)
  blocking collectives: 189 us -> 0 us
  waiting for transfers between devices: 190 us -> 110 us
  Pallas kernels: 70 us -> 136 us
  local copies, waits for them, and re-layouts: 59.7 us -> 17.2 us
  starting transfers between devices: 21.4 us -> 50.4 us
  matrix products: 20.3 us -> 0 us
    all_to_all x1 -> x0, blocking collectives: 189 us -> none  [routed_by_slots(): lax.all_to_all(outgoing, 'expert', split_axis=0, concat_axis=0, tiled=True)]
    all_to_all x1 -> x0, waiting for transfers between devices: 184 us -> none  [routed_by_slots(): lax.all_to_all(result.reshape(recv_shape), 'expert', split_axis=0, concat...]
    ppermute x0 -> x44, waiting for transfers between devices: none -> 102 us  [swap(): return lax.ppermute(array, axis, [(i, i ^ mask) for i in range(peers)])]
    pallas_call x2 -> x12, Pallas kernels: 70 us -> 136 us  [the longest x2 32.5 us: mixer(): pl.pallas_call(functools.partial(back_kernel, before=before if part == 0...]
    ppermute x0 -> x44, starting transfers between devices: none -> 40.4 us  [swap(): return lax.ppermute(array, axis, [(i, i ^ mask) for i in range(peers)])]
    dot_general x2 -> x0, matrix products: 20.3 us -> none  [the longest x1 15.9 us: routed_by_slots(): jnp.dot(inner_act, w_down[0], preferred_element_type=jnp.float32)]
    gather x1 -> x0, local copies, waits for them, and re-layouts: 13.1 us -> none  [routed_by_slots(): returned.reshape(experts * capacity, model_width)[dest_row]]
    scatter x1 -> x0, local copies, waits for them, and re-layouts: 12.4 us -> none  [routed_by_slots(): outgoing = jnp.zeros((experts * capacity, model_width), jnp.bfloat16).at[...]
  transfers between devices with their start and end apart: 8 -> 48, of which waited for: 3 -> 16; matrix products, arithmetic and copies ran while one was open for 1% -> 4% of each run, Pallas kernels for 0% -> 42%
where the time goes in v2:
time: 323 us
  Pallas kernels  136 us (42%)
  waiting for transfers between devices  110 us (34%)
  starting transfers between devices  50.4 us (16%)
  local copies, waits for them, and re-layouts  17.2 us (5%)
  other arithmetic  7.91 us (2%)
    ppermute x44, waiting for transfers between devices, swap(): return lax.ppermute(array, axis, [(i, i ^ mask) for i in range(peers)])  102 us
    ppermute x44, starting transfers between devices, swap(): return lax.ppermute(array, axis, [(i, i ^ mask) for i in range(peers)])  40.4 us
    pallas_call x2, Pallas kernels, mixer(): pl.pallas_call(functools.partial(back_kernel, before=before if part == 0...  32.5 us
    pallas_call x4, Pallas kernels, down(): pl.pallas_call(functools.partial(down_kernel, halves=len(nears)), grid=(1...  24.7 us
    pallas_call x1, Pallas kernels, mixer(): pl.pallas_call(front_kernel, out_shape=(shape((rows, width), bf16), shape...  23.4 us
    pallas_call x2, Pallas kernels, far_act(): pl.pallas_call(functools.partial(far_act_kernel, blocks=len(xs), deep=len...  20 us
    pallas_call x2, Pallas kernels, near_act(): pl.pallas_call(functools.partial(near_act_kernel, blocks=len(xs)), grid=(...  18.5 us
    pallas_call x1, Pallas kernels, mixer(): pl.pallas_call(ends_kernel, grid=(tiles // GROUP,), out_shape=shape((stat...  17.2 us
  transfers between devices with their start and end apart: 48, of which 16 were waited for; matrix products, arithmetic and copies ran while one was open for 4% of the time, Pallas kernels for 42%

profile of v2, /device:TPU:0, one launch (start us, length us, event | category | flops | bytes accessed | tf_op | source)
XLA Modules:
  0.0 322.9 jit_solution(8008347382379622203)
XLA Ops:
  11.4 4.6 %copy.24.proj_weight = bf16[4096,288]{1,0:T(8,128)(2,1)} copy(bf16[4096,288]{0,1:T(8,128)(2,1)} %param.19) | data formatting | bytes 4718592 | tf_op args[4]
  16.6 23.4 %mixer_front.1 = (bf16[256,4096]{1,0:T(8,128)(2,1)}, f32[8192,128]{1,0:T(8,128)}, f32[8192,128]{1,0:T(8,128)}, f32[256,32]{1,0:T(8,128)}) custom-call(bf16[256,4096]{1,0:T(8,128)(2,1)} %bitcast.50, bf16[16,4096]{1,0:T(8,128)(2,1)} %copy-done.41, f32[1,4096]{1,0:T(1,128)} %bitcast.64, f32[4,4096]{1,0:T(4,128)} %conv_weight.1, f32[1,4096]{1,0:T(1,128)} %bitcast.65, ...), custom_call_target="tpu_custom_call" | custom-call | flops 575000000 | bytes 65536 | tf_op jit(solution)/shard_map/mixer_front/pallas_call | solution.py:279
  50.2 17.2 %mixer_ends.1 = f32[17,32,128]{2,1,0:T(8,128)} custom-call(f32[256,32,128]{2,1,0:T(8,128)} %bitcast.40, f32[256,32,128]{2,1,0:T(8,128)} %bitcast.43, f32[256,32]{1,0:T(8,128)} %get-tuple-element.81.maps_ref, f32[16,32,128]{2,1,0:T(8,128)} %bitcast.53), custom_call_target="tpu_custom_call" | custom-call | flops 575000000 | bytes 65536 | tf_op jit(solution)/shard_map/mixer_ends/pallas_call | solution.py:305
  79.1 4.7 %collective-permute-done.8.rest_1_ = f32[17,32,128]{2,1,0:T(8,128)S(1)} collective-permute-done((f32[17,32,128]{2,1,0:T(8,128)}, f32[17,32,128]{2,1,0:T(8,128)S(1)}, u32[]{:S(2)}, u32[]{:S(2)}) %collective-permute-start.8) | collective-permute-done | bytes 278560 | tf_op jit(solution)/shard_map/ppermute | solution.py:51
  86.5 16.6 %mixer_back.2 = (f32[128,4096]{1,0:T(8,128)}, bf16[128,4096]{1,0:T(8,128)(2,1)}, f32[16,32,128]{2,1,0:T(8,128)}) custom-call(bf16[256,4096]{1,0:T(8,128)(2,1)} %bitcast.51, bf16[256,4096]{1,0:T(8,128)(2,1)} %get-tuple-element.78.conv_ref, f32[256,32,128]{2,1,0:T(8,128)} %bitcast.41, f32[256,32,128]{2,1,0:T(8,128)} %bitcast.44, ...), custom_call_target="tpu_custom_call" | custom-call | flops 575000000 | bytes 65536 | tf_op jit(solution)/shard_map/mixer_back/pallas_call | solution.py:335
  103.0 7.9 %collective-permute-done.10.refs_12_ = bf16[1536,256]{1,0:T(8,128)(2,1)S(1)} collective-permute-done((bf16[1536,256]{1,0:T(8,128)(2,1)S(1)}, bf16[1536,256]{1,0:T(8,128)(2,1)S(1)}, u32[]{:S(2)}, u32[]{:S(2)}) %collective-permute-start.10) | collective-permute-done | bytes 786464 | tf_op jit(solution)/shard_map/ppermute | solution.py:360
  117.0 16.0 %mixer_back.3 = (f32[128,4096]{1,0:T(8,128)}, bf16[128,4096]{1,0:T(8,128)(2,1)}) custom-call(bf16[256,4096]{1,0:T(8,128)(2,1)} %bitcast.52, bf16[256,4096]{1,0:T(8,128)(2,1)} %get-tuple-element.78.conv_ref, f32[256,32,128]{2,1,0:T(8,128)} %bitcast.42, f32[256,32,128]{2,1,0:T(8,128)} %bitcast.45, f32[256,32]{1,0:T(8,128)} %get-tuple-element.81.maps_ref, ...), custom_call_target="tpu_custom_call" | custom-call | flops 575000000 | bytes 65536 | tf_op jit(solution)/shard_map/mixer_back/pallas_call | solution.py:335
  133.0 6.4 %collective-permute-done.13.refs_5_ = bf16[128,1024]{1,0:T(8,128)(2,1)S(1)} collective-permute-done((bf16[128,1024]{1,0:T(8,128)(2,1)S(1)}, bf16[128,1024]{1,0:T(8,128)(2,1)S(1)}, u32[]{:S(2)}, u32[]{:S(2)}) %collective-permute-start.13) | collective-permute-done | bytes 262176 | tf_op jit(solution)/shard_map/ppermute | solution.py:360
  139.4 8.3 %collective-permute-done.16.refs_7_ = bf16[1536,256]{1,0:T(8,128)(2,1)S(1)} collective-permute-done((bf16[1536,256]{1,0:T(8,128)(2,1)S(1)}, bf16[1536,256]{1,0:T(8,128)(2,1)S(1)}, u32[]{:S(2)}, u32[]{:S(2)}) %collective-permute-start.16) | collective-permute-done | bytes 786464 | tf_op jit(solution)/shard_map/ppermute | solution.py:360
  150.7 26.8 %collective-permute-done.24.refs_2_ = bf16[128,4096]{1,0:T(8,128)(2,1)S(1)} collective-permute-done((bf16[128,4096]{1,0:T(8,128)(2,1)}, bf16[128,4096]{1,0:T(8,128)(2,1)S(1)}, u32[]{:S(2)}, u32[]{:S(2)}) %collective-permute-start.24) | collective-permute-done | bytes 1048608 | tf_op jit(solution)/shard_map/ppermute | solution.py:360
  181.7 9.3 %near_act.2.refs_0_ = bf16[512,512]{1,0:T(8,128)(2,1)} custom-call(bf16[128,4096]{1,0:T(8,128)(2,1)} %get-tuple-element.100.refs_0_, bf16[128,4096]{1,0:T(8,128)(2,1)} %collective-permute-done.18.refs_1_, bf16[128,4096]{1,0:T(8,128)(2,1)} %copy-done.2, bf16[128,4096]{1,0:T(8,128)(2,1)} %copy-done.3, bf16[4096,512]{1,0:T(8,128)(2,1)} %bitcast.46, ...), custom_call_target="tpu_custom_call" | custom-call | flops 575000000 | bytes 65536 | tf_op jit(solution)/shard_map/near_act/pallas_call | solution.py:448
  194.2 4.9 %collective-permute-done.21.refs_7_ = bf16[128,1024]{1,0:T(8,128)(2,1)S(1)} collective-permute-done((bf16[128,1024]{1,0:T(8,128)(2,1)S(1)}, bf16[128,1024]{1,0:T(8,128)(2,1)S(1)}, u32[]{:S(2)}, u32[]{:S(2)}) %collective-permute-start.21) | collective-permute-done | bytes 262176 | tf_op jit(solution)/shard_map/ppermute | solution.py:360
  200.3 5.5 %collective-permute-done.22.refs_5_ = bf16[128,1024]{1,0:T(8,128)(2,1)S(1)} collective-permute-done((bf16[128,1024]{1,0:T(8,128)(2,1)S(1)}, bf16[128,1024]{1,0:T(8,128)(2,1)S(1)}, u32[]{:S(2)}, u32[]{:S(2)}) %collective-permute-start.22) | collective-permute-done | bytes 262176 | tf_op jit(solution)/shard_map/ppermute | solution.py:360
  207.5 10.0 %far_act.2.refs_2_ = bf16[512,512]{1,0:T(8,128)(2,1)} custom-call(bf16[128,4096]{1,0:T(8,128)(2,1)} %get-tuple-element.100.refs_0_, bf16[128,4096]{1,0:T(8,128)(2,1)} %collective-permute-done.18.refs_1_, bf16[128,4096]{1,0:T(8,128)(2,1)} %copy-done.2, bf16[128,4096]{1,0:T(8,128)(2,1)} %copy-done.3, bf16[1536,256]{1,0:T(8,128)(2,1)} %copy-done.4, ...), custom_call_target="tpu_custom_call" | custom-call | flops 575000000 | bytes 65536 | tf_op jit(solution)/shard_map/far_act/pallas_call | solution.py:488
  222.6 9.2 %near_act.3.refs_1_ = bf16[512,512]{1,0:T(8,128)(2,1)} custom-call(bf16[128,4096]{1,0:T(8,128)(2,1)} %get-tuple-element.105.refs_0_, bf16[128,4096]{1,0:T(8,128)(2,1)} %collective-permute-done.23.refs_1_, bf16[128,4096]{1,0:T(8,128)(2,1)} %copy-done.1, bf16[128,4096]{1,0:T(8,128)(2,1)} %collective-permute-done.25.refs_3_, bf16[4096,512]{1,0:T(8,128)(2,1)} %bitcast.47, ...), custom_call_target="tpu_custom_call" | custom-call | flops 575000000 | bytes 65536 | tf_op jit(solution)/shard_map/near_act/pallas_call | solution.py:448
  234.3 10.0 %far_act.3.refs_3_ = bf16[512,512]{1,0:T(8,128)(2,1)} custom-call(bf16[128,4096]{1,0:T(8,128)(2,1)} %get-tuple-element.105.refs_0_, bf16[128,4096]{1,0:T(8,128)(2,1)} %collective-permute-done.23.refs_1_, bf16[128,4096]{1,0:T(8,128)(2,1)} %copy-done.1, bf16[128,4096]{1,0:T(8,128)(2,1)} %collective-permute-done.25.refs_3_, bf16[1536,256]{1,0:T(8,128)(2,1)} %copy-done.4, ...), custom_call_target="tpu_custom_call" | custom-call | flops 575000000 | bytes 65536 | tf_op jit(solution)/shard_map/far_act/pallas_call | solution.py:488
  245.6 6.4 %down.4 = (f32[512,1024]{1,0:T(8,128)}, bf16[512,1024]{1,0:T(8,128)(2,1)}) custom-call(bf16[512,512]{1,0:T(8,128)(2,1)} %near_act.2.refs_0_, bf16[512,512]{1,0:T(8,128)(2,1)} %near_act.3.refs_1_, bf16[512,512]{1,0:T(8,128)(2,1)} %far_act.2.refs_2_, bf16[512,512]{1,0:T(8,128)(2,1)} %far_act.3.refs_3_, bf16[512,4096]{1,0:T(8,128)(2,1)} %bitcast.36, ...), custom_call_target="tpu_custom_call" | custom-call | flops 575000000 | bytes 65536 | tf_op jit(solution)/shard_map/down/pallas_call | solution.py:520
  252.1 6.1 %down.5 = (f32[512,1024]{1,0:T(8,128)}, bf16[512,1024]{1,0:T(8,128)(2,1)}) custom-call(bf16[512,512]{1,0:T(8,128)(2,1)} %near_act.2.refs_0_, bf16[512,512]{1,0:T(8,128)(2,1)} %near_act.3.refs_1_, bf16[512,512]{1,0:T(8,128)(2,1)} %far_act.2.refs_2_, bf16[512,512]{1,0:T(8,128)(2,1)} %far_act.3.refs_3_, bf16[512,4096]{1,0:T(8,128)(2,1)} %bitcast.37, ...), custom_call_target="tpu_custom_call" | custom-call | flops 575000000 | bytes 65536 | tf_op jit(solution)/shard_map/down/pallas_call | solution.py:520
  258.8 6.1 %down.6 = (f32[512,1024]{1,0:T(8,128)}, bf16[512,1024]{1,0:T(8,128)(2,1)}) custom-call(bf16[512,512]{1,0:T(8,128)(2,1)} %near_act.2.refs_0_, bf16[512,512]{1,0:T(8,128)(2,1)} %near_act.3.refs_1_, bf16[512,512]{1,0:T(8,128)(2,1)} %far_act.2.refs_2_, bf16[512,512]{1,0:T(8,128)(2,1)} %far_act.3.refs_3_, bf16[512,4096]{1,0:T(8,128)(2,1)} %bitcast.38, ...), custom_call_target="tpu_custom_call" | custom-call | flops 575000000 | bytes 65536 | tf_op jit(solution)/shard_map/down/pallas_call | solution.py:520
  268.1 6.1 %down.7 = (f32[512,1024]{1,0:T(8,128)}, bf16[512,1024]{1,0:T(8,128)(2,1)}) custom-call(bf16[512,512]{1,0:T(8,128)(2,1)} %near_act.2.refs_0_, bf16[512,512]{1,0:T(8,128)(2,1)} %near_act.3.refs_1_, bf16[512,512]{1,0:T(8,128)(2,1)} %far_act.2.refs_2_, bf16[512,512]{1,0:T(8,128)(2,1)} %far_act.3.refs_3_, bf16[512,4096]{1,0:T(8,128)(2,1)} %bitcast.39, ...), custom_call_target="tpu_custom_call" | custom-call | flops 575000000 | bytes 65536 | tf_op jit(solution)/shard_map/down/pallas_call | solution.py:520
  274.2 6.5 %collective-permute-done.41 = bf16[256,1024]{1,0:T(8,128)(2,1)S(1)} collective-permute-done((bf16[256,1024]{1,0:T(8,128)(2,1)S(1)}, bf16[256,1024]{1,0:T(8,128)(2,1)S(1)}, u32[]{:S(2)}, u32[]{:S(2)}) %collective-permute-start.41) | collective-permute-done | bytes 524320 | tf_op jit(solution)/shard_map/ppermute | solution.py:360
  287.0 8.9 %collective-permute-done.43 = bf16[256,1024]{1,0:T(8,128)(2,1)S(1)} collective-permute-done((bf16[256,1024]{1,0:T(8,128)(2,1)S(1)}, bf16[256,1024]{1,0:T(8,128)(2,1)S(1)}, u32[]{:S(2)}, u32[]{:S(2)}) %collective-permute-start.43) | collective-permute-done | bytes 524320 | tf_op jit(solution)/shard_map/ppermute | solution.py:360
  295.9 11.2 %collective-permute-done.45 = bf16[256,1024]{1,0:T(8,128)(2,1)S(1)} collective-permute-done((bf16[256,1024]{1,0:T(8,128)(2,1)S(1)}, bf16[256,1024]{1,0:T(8,128)(2,1)S(1)}, u32[]{:S(2)}, u32[]{:S(2)}) %collective-permute-start.45) | collective-permute-done | bytes 524320 | tf_op jit(solution)/shard_map/ppermute | solution.py:360
  307.1 11.0 %collective-permute-done.47 = bf16[256,1024]{1,0:T(8,128)(2,1)} collective-permute-done((bf16[256,1024]{1,0:T(8,128)(2,1)S(1)}, bf16[256,1024]{1,0:T(8,128)(2,1)}, u32[]{:S(2)}, u32[]{:S(2)}) %collective-permute-start.47) | collective-permute-done | bytes 524320 | tf_op jit(solution)/shard_map/ppermute | solution.py:360
  (200 shorter events, 79.3 us)
Async XLA Ops:
  3.0 38.6 %collective-permute-start.1 = (bf16[1536,256]{1,0:T(8,128)(2,1)}, bf16[1536,256]{1,0:T(8,128)(2,1)S(1)}, u32[]{:S(2)}, u32[]{:S(2)}) collective-permute-start(bf16[1536,256]{1,0:T(8,128)(2,1)} %get-tuple-element.148), channel_id=1, source_target_pairs={{0,4},{1,5},{2,6},{3,7},{4,0},{5,1},{6,2},{7,3},{8,12},{9,13},{10,... | collective-permute-start | bytes 2359304 | tf_op jit(solution)/shard_map/ppermute | solution.py:360
  41.7 27.6 %collective-permute-start.4 = (bf16[1536,256]{1,0:T(8,128)(2,1)S(1)}, bf16[1536,256]{1,0:T(8,128)(2,1)S(1)}, u32[]{:S(2)}, u32[]{:S(2)}) collective-permute-start(bf16[1536,256]{1,0:T(8,128)(2,1)S(1)} %collective-permute-done.1.refs_4_), channel_id=1, source_target_pairs={{0,16},{8,24},{16,0},{24,8},{1,17},{9,25},{17,1},{25,9},{2,18},{10... | collective-permute-start | bytes 2359304 | tf_op jit(solution)/shard_map/ppermute | solution.py:360
  43.2 26.0 %collective-permute-start.3 = (bf16[1536,256]{1,0:T(8,128)(2,1)S(1)}, bf16[1536,256]{1,0:T(8,128)(2,1)S(1)}, u32[]{:S(2)}, u32[]{:S(2)}) collective-permute-start(bf16[1536,256]{1,0:T(8,128)(2,1)S(1)} %collective-permute-done.1.refs_4_), channel_id=1, source_target_pairs={{0,8},{8,0},{16,24},{24,16},{1,9},{9,1},{17,25},{25,17},{2,10},{10... | collective-permute-start | bytes 2359304 | tf_op jit(solution)/shard_map/ppermute | solution.py:360
  44.8 24.5 %collective-permute-start.5 = (bf16[1024,256]{1,0:T(8,128)(2,1)S(1)}, bf16[1024,256]{1,0:T(8,128)(2,1)S(1)}, u32[]{:S(2)}, u32[]{:S(2)}) collective-permute-start(bf16[1024,256]{1,0:T(8,128)(2,1)S(1)} %fusion.21), channel_id=1, source_target_pairs={{0,4},{1,5},{2,6},{3,7},{4,0},{5,1},{6,2},{7,3},{8,12},{9,13},{10,... | collective-permute-start | bytes 1572872 | tf_op jit(solution)/shard_map/ppermute | solution.py:360
  46.1 21.2 %collective-permute-start.6 = (f32[8,512]{1,0:T(8,128)S(1)}, f32[8,512]{1,0:T(8,128)S(1)}, u32[]{:S(2)}, u32[]{:S(2)}) collective-permute-start(f32[8,512]{1,0:T(8,128)S(1)} %pad_maximum_fusion.3), channel_id=1, source_target_pairs={{0,2},{1,3},{2,0},{3,1},{4,6},{5,7},{6,4},{7,5},{8,10},{9,11},{10,... | collective-permute-start | bytes 49160 | tf_op jit(solution)/shard_map/ppermute | solution.py:360
  75.9 35.0 %collective-permute-start.10 = (bf16[1536,256]{1,0:T(8,128)(2,1)S(1)}, bf16[1536,256]{1,0:T(8,128)(2,1)S(1)}, u32[]{:S(2)}, u32[]{:S(2)}) collective-permute-start(bf16[1536,256]{1,0:T(8,128)(2,1)S(1)} %copy-done.18), channel_id=1, source_target_pairs={{0,4},{1,5},{2,6},{3,7},{4,0},{5,1},{6,2},{7,3},{8,12},{9,13},{10,... | collective-permute-start | bytes 2359304 | tf_op jit(solution)/shard_map/ppermute | solution.py:360
  83.9 27.0 %collective-permute-start.12 = (bf16[1024,256]{1,0:T(8,128)(2,1)S(1)}, bf16[1024,256]{1,0:T(8,128)(2,1)S(1)}, u32[]{:S(2)}, u32[]{:S(2)}) collective-permute-start(bf16[1024,256]{1,0:T(8,128)(2,1)S(1)} %collective-permute-done.5.refs_8_), channel_id=1, source_target_pairs={{0,16},{8,24},{16,0},{24,8},{1,17},{9,25},{17,1},{25,9},{2,18},{10... | collective-permute-start | bytes 1572872 | tf_op jit(solution)/shard_map/ppermute | solution.py:360
  86.3 24.6 %collective-permute-start.11 = (bf16[1024,256]{1,0:T(8,128)(2,1)S(1)}, bf16[1024,256]{1,0:T(8,128)(2,1)}, u32[]{:S(2)}, u32[]{:S(2)}) collective-permute-start(bf16[1024,256]{1,0:T(8,128)(2,1)S(1)} %collective-permute-done.5.refs_8_), channel_id=1, source_target_pairs={{0,8},{8,0},{16,24},{24,16},{1,9},{9,1},{17,25},{25,17},{2,10},{10... | collective-permute-start | bytes 1572872 | tf_op jit(solution)/shard_map/ppermute | solution.py:360
  110.9 37.9 %collective-permute-start.17 = (bf16[128,4096]{1,0:T(8,128)(2,1)}, bf16[128,4096]{1,0:T(8,128)(2,1)S(1)}, u32[]{:S(2)}, u32[]{:S(2)}) collective-permute-start(bf16[128,4096]{1,0:T(8,128)(2,1)} %get-tuple-element.100.refs_0_), channel_id=1, source_target_pairs={{0,2},{1,3},{2,0},{3,1},{4,6},{5,7},{6,4},{7,5},{8,10},{9,11},{10,... | collective-permute-start | bytes 3145736 | tf_op jit(solution)/shard_map/ppermute | solution.py:360
  111.0 36.7 %collective-permute-start.15 = (bf16[1536,256]{1,0:T(8,128)(2,1)S(1)}, bf16[1536,256]{1,0:T(8,128)(2,1)}, u32[]{:S(2)}, u32[]{:S(2)}) collective-permute-start(bf16[1536,256]{1,0:T(8,128)(2,1)S(1)} %collective-permute-done.10.refs_12_), channel_id=1, source_target_pairs={{0,16},{8,24},{16,0},{24,8},{1,17},{9,25},{17,1},{25,9},{2,18},{10... | collective-permute-start | bytes 2359304 | tf_op jit(solution)/shard_map/ppermute | solution.py:360
  111.7 36.0 %collective-permute-start.14 = (bf16[1536,256]{1,0:T(8,128)(2,1)S(1)}, bf16[1536,256]{1,0:T(8,128)(2,1)S(1)}, u32[]{:S(2)}, u32[]{:S(2)}) collective-permute-start(bf16[1536,256]{1,0:T(8,128)(2,1)S(1)} %collective-permute-done.10.refs_12_), channel_id=1, source_target_pairs={{0,8},{8,0},{16,24},{24,16},{1,9},{9,1},{17,25},{25,17},{2,10},{10... | collective-permute-start | bytes 2359304 | tf_op jit(solution)/shard_map/ppermute | solution.py:360
  112.0 35.7 %collective-permute-start.16 = (bf16[1536,256]{1,0:T(8,128)(2,1)S(1)}, bf16[1536,256]{1,0:T(8,128)(2,1)S(1)}, u32[]{:S(2)}, u32[]{:S(2)}) collective-permute-start(bf16[1536,256]{1,0:T(8,128)(2,1)S(1)} %collective-permute-done.4.refs_6_), channel_id=1, source_target_pairs={{0,8},{8,0},{16,24},{24,16},{1,9},{9,1},{17,25},{25,17},{2,10},{10... | collective-permute-start | bytes 2359304 | tf_op jit(solution)/shard_map/ppermute | solution.py:360
  116.0 23.4 %collective-permute-start.13 = (bf16[128,1024]{1,0:T(8,128)(2,1)S(1)}, bf16[128,1024]{1,0:T(8,128)(2,1)S(1)}, u32[]{:S(2)}, u32[]{:S(2)}) collective-permute-start(bf16[128,1024]{1,0:T(8,128)(2,1)S(1)} %get-tuple-element.95), channel_id=1, source_target_pairs={{0,4},{1,5},{2,6},{3,7},{4,0},{5,1},{6,2},{7,3},{8,12},{9,13},{10,... | collective-permute-start | bytes 786440 | tf_op jit(solution)/shard_map/ppermute | solution.py:360
  147.7 29.8 %collective-permute-start.24 = (bf16[128,4096]{1,0:T(8,128)(2,1)}, bf16[128,4096]{1,0:T(8,128)(2,1)S(1)}, u32[]{:S(2)}, u32[]{:S(2)}) collective-permute-start(bf16[128,4096]{1,0:T(8,128)(2,1)} %get-tuple-element.105.refs_0_), channel_id=1, source_target_pairs={{0,2},{1,3},{2,0},{3,1},{4,6},{5,7},{6,4},{7,5},{8,10},{9,11},{10,... | collective-permute-start | bytes 3145736 | tf_op jit(solution)/shard_map/ppermute | solution.py:360
  148.8 29.5 %collective-permute-start.19 = (bf16[128,4096]{1,0:T(8,128)(2,1)S(1)}, bf16[128,4096]{1,0:T(8,128)(2,1)S(1)}, u32[]{:S(2)}, u32[]{:S(2)}) collective-permute-start(bf16[128,4096]{1,0:T(8,128)(2,1)S(1)} %collective-permute-done.17.refs_2_), channel_id=1, source_target_pairs={{0,1},{1,0},{2,3},{3,2},{4,5},{5,4},{6,7},{7,6},{8,9},{9,8},{10,11... | collective-permute-start | bytes 3145736 | tf_op jit(solution)/shard_map/ppermute | solution.py:360
  148.8 31.7 %collective-permute-start.18 = (bf16[128,4096]{1,0:T(8,128)(2,1)S(1)}, bf16[128,4096]{1,0:T(8,128)(2,1)}, u32[]{:S(2)}, u32[]{:S(2)}) collective-permute-start(bf16[128,4096]{1,0:T(8,128)(2,1)S(1)} %copy-done), channel_id=1, source_target_pairs={{0,1},{1,0},{2,3},{3,2},{4,5},{5,4},{6,7},{7,6},{8,9},{9,8},{10,11... | collective-permute-start | bytes 3145736 | tf_op jit(solution)/shard_map/ppermute | solution.py:360
  149.3 43.0 %collective-permute-start.27 = (bf16[1536,256]{1,0:T(8,128)(2,1)}, bf16[1536,256]{1,0:T(8,128)(2,1)}, u32[]{:S(2)}, u32[]{:S(2)}) collective-permute-start(bf16[1536,256]{1,0:T(8,128)(2,1)} %collective-permute-done.15.refs_14_), channel_id=1, source_target_pairs={{0,8},{8,0},{16,24},{24,16},{1,9},{9,1},{17,25},{25,17},{2,10},{10... | collective-permute-start | bytes 2359304 | tf_op jit(solution)/shard_map/ppermute | solution.py:360
  149.6 29.7 %collective-permute-start.28 = (bf16[128,1024]{1,0:T(8,128)(2,1)S(1)}, bf16[128,1024]{1,0:T(8,128)(2,1)S(1)}, u32[]{:S(2)}, u32[]{:S(2)}) collective-permute-start(bf16[128,1024]{1,0:T(8,128)(2,1)S(1)} %get-tuple-element.109), channel_id=1, source_target_pairs={{0,4},{1,5},{2,6},{3,7},{4,0},{5,1},{6,2},{7,3},{8,12},{9,13},{10,... | collective-permute-start | bytes 786440 | tf_op jit(solution)/shard_map/ppermute | solution.py:360
  179.3 43.3 %collective-permute-start.25 = (bf16[128,4096]{1,0:T(8,128)(2,1)S(1)}, bf16[128,4096]{1,0:T(8,128)(2,1)}, u32[]{:S(2)}, u32[]{:S(2)}) collective-permute-start(bf16[128,4096]{1,0:T(8,128)(2,1)S(1)} %collective-permute-done.24.refs_2_), channel_id=1, source_target_pairs={{0,1},{1,0},{2,3},{3,2},{4,5},{5,4},{6,7},{7,6},{8,9},{9,8},{10,11... | collective-permute-start | bytes 3145736 | tf_op jit(solution)/shard_map/ppermute | solution.py:360
  180.0 42.6 %collective-permute-start.23 = (bf16[128,4096]{1,0:T(8,128)(2,1)}, bf16[128,4096]{1,0:T(8,128)(2,1)}, u32[]{:S(2)}, u32[]{:S(2)}) collective-permute-start(bf16[128,4096]{1,0:T(8,128)(2,1)} %get-tuple-element.105.refs_0_), channel_id=1, source_target_pairs={{0,1},{1,0},{2,3},{3,2},{4,5},{5,4},{6,7},{7,6},{8,9},{9,8},{10,11... | collective-permute-start | bytes 3145736 | tf_op jit(solution)/shard_map/ppermute | solution.py:360
  199.1 18.4 %collective-permute-start.30 = (bf16[128,1024]{1,0:T(8,128)(2,1)S(1)}, bf16[128,1024]{1,0:T(8,128)(2,1)S(1)}, u32[]{:S(2)}, u32[]{:S(2)}) collective-permute-start(bf16[128,1024]{1,0:T(8,128)(2,1)S(1)} %copy-done.25), channel_id=1, source_target_pairs={{0,16},{8,24},{16,0},{24,8},{1,17},{9,25},{17,1},{25,9},{2,18},{10... | collective-permute-start | bytes 786440 | tf_op jit(solution)/shard_map/ppermute | solution.py:360
  205.8 16.0 %collective-permute-start.31 = (bf16[128,1024]{1,0:T(8,128)(2,1)S(1)}, bf16[128,1024]{1,0:T(8,128)(2,1)}, u32[]{:S(2)}, u32[]{:S(2)}) collective-permute-start(bf16[128,1024]{1,0:T(8,128)(2,1)S(1)} %collective-permute-done.20.refs_6_), channel_id=1, source_target_pairs={{0,16},{8,24},{16,0},{24,8},{1,17},{9,25},{17,1},{25,9},{2,18},{10... | collective-permute-start | bytes 786440 | tf_op jit(solution)/shard_map/ppermute | solution.py:360
  282.9 24.2 %collective-permute-start.45 = (bf16[256,1024]{1,0:T(8,128)(2,1)S(1)}, bf16[256,1024]{1,0:T(8,128)(2,1)S(1)}, u32[]{:S(2)}, u32[]{:S(2)}) collective-permute-start(bf16[256,1024]{1,0:T(8,128)(2,1)S(1)} %fusion.4), channel_id=1, source_target_pairs={{0,2},{1,3},{2,0},{3,1},{4,6},{5,7},{6,4},{7,5},{8,10},{9,11},{10,... | collective-permute-start | bytes 1572872 | tf_op jit(solution)/shard_map/ppermute | solution.py:360
  284.7 33.4 %collective-permute-start.47 = (bf16[256,1024]{1,0:T(8,128)(2,1)S(1)}, bf16[256,1024]{1,0:T(8,128)(2,1)}, u32[]{:S(2)}, u32[]{:S(2)}) collective-permute-start(bf16[256,1024]{1,0:T(8,128)(2,1)S(1)} %fusion), channel_id=1, source_target_pairs={{0,2},{1,3},{2,0},{3,1},{4,6},{5,7},{6,4},{7,5},{8,10},{9,11},{10,... | collective-permute-start | bytes 1572872 | tf_op jit(solution)/shard_map/ppermute | solution.py:360
  (68 other events, 862.3 us)

commit v3 on v2

v3 whole, which is shorter than its diff:
```python
import functools
import math

import jax
import jax.numpy as jnp
from jax import lax
from jax.experimental import pallas as pl
from jax.experimental.pallas import tpu as pltpu
from jax.sharding import PartitionSpec as P

LANES = 128
GROUP = 8
LOG2E = math.log2(math.e)
VMEM_LIMIT = 56 * 2**20
COST = 0.3
MERGE = False
TOGETHER = False
IN_TURN = False
DEEP = (1024, 1024, 768, 1280)
BROAD = (2048, 1024, 1024)
PANEL = 1024
CORNERS_X = (0, 2)
DIRECT = ()
STARTS = {'z0': ['w1', 'w2', 'w3'], 'z1': ['front'], 'x0': ['front'], 'y0': ['front'], 'c0': ['ends'], 'x1': ['e1', 'e2', 'e3'], 'y1': ['e1', 'e2', 'e3'], 'z2': ['e1', 'e2', 'e3', 'z1'], 'z3': ['back0'], 'x2': ['back0'], 'y2': ['back0'], 'c1': ['back0'], 'c2': ['back1'], 'm0': ['back1'], 'z4': ['z3', 'c1'], 'x3': ['z3', 'c2'], 'y3': ['z3'], 'c3': ['near0'], 'm1': ['near0'], 'z5': ['near0', 'z4'], 'x4': ['near0'], 'y4': ['near0'], 'c4': ['far0'], 'z6': ['far0'], 'x5': ['far0'], 'y5': ['y1'], 'c5': ['act1'], 'x6': ['act1'], 'y6': ['act1'], 'c6': ['down0'], 't1': ['front'], 'r2': ['s0']}
WAITS = {'front': ['z0'], 'ends': ['x0', 'y0'], 'back0': ['c0', 'y1', 'z2'], 'back1': ['x2', 'y2', 'c1'], 'near0': ['z4', 'x3', 'y3'], 'far0': ['z5', 'y4'], 'act1': ['x4', 'z6', 'x5', 'x6'], 'down0': ['c5'], 'down1': ['c6'], 'down2': ['y5', 'y6', 'r0'], 'down3': ['c4', 'r1']}


def from_behind(array, axis, by):
    peers = lax.axis_size(axis)
    pairs = [(i, i + by) for i in range(peers) if 0 <= i + by < peers]
    return lax.ppermute(array, axis, pairs)


def silu(v):
    return v / (1.0 + jnp.exp(-v))


def softplus(v):
    return jnp.maximum(v, 0.0) + jnp.log(1.0 + jnp.exp(-jnp.abs(v)))


def spread_columns(maps, target, first, count, rows):
    for n in range(count):
        target[n] = jnp.broadcast_to(maps[:, first + n : first + n + 1], (rows, LANES))


def cost(micros):
    return pl.CostEstimate(flops=int(micros * 1.15e9), bytes_accessed=2**16, transcendentals=0)


def params():
    return pltpu.CompilerParams(vmem_limit_bytes=VMEM_LIMIT)


def front_kernel(
    tok_ref, halo_ref, norm_gain, conv_weight, conv_bias, proj_weight, dt_weight, dt_bias,
    conv_ref, step_ref, drive_ref, maps_ref,
    normed, low, block,
):
    rows, width = tok_ref.shape
    halo = halo_ref.shape[0]
    taps = conv_weight.shape[0]
    low_width = dt_weight.shape[0]
    chunk = block.shape[1]
    part = pl.program_id(0)

    @pl.when(part == 0)
    def _():
        gain = norm_gain[...]

        def norm_rows(x):
            x = x.astype(jnp.float32)
            scale = lax.rsqrt(jnp.mean(x * x, axis=-1, keepdims=True) + 1e-05)
            return (x * scale * gain).astype(jnp.bfloat16).astype(jnp.float32)

        normed[pl.ds(0, halo), :] = norm_rows(halo_ref[...])

        def norm_step(i, _):
            at = pl.multiple_of(i * 16, 16)
            normed[pl.ds(halo + at, 16), :] = norm_rows(tok_ref[pl.ds(at, 16), :])
            return 0

        lax.fori_loop(0, rows // 16, norm_step, 0)

        def conv_step(i, _):
            at = pl.multiple_of(i * 16, 16)
            for c in range(width // chunk):
                cols = pl.ds(c * chunk, chunk)
                window = normed[pl.ds(pl.multiple_of(halo - 8 + at, 8), 24), cols]
                total = jnp.zeros((16, chunk), jnp.float32)
                for j in range(taps):
                    back = taps - 1 - j
                    moved = pltpu.roll(window, back, 0) if back else window
                    total = total + conv_weight[pl.ds(j, 1), cols] * moved[8:24]
                conv_ref[pl.ds(at, 16), cols] = silu(total + conv_bias[:, cols]).astype(
                    jnp.bfloat16
                )
            return 0

        lax.fori_loop(0, rows // 16, conv_step, 0)

        conv_all = conv_ref[...]
        project = lambda weight: lax.dot_general(
            conv_all, weight, (((1,), (1,)), ((), ())), preferred_element_type=jnp.float32
        )
        low[...] = project(proj_weight[:low_width, :]).astype(jnp.bfloat16)
        maps_ref[...] = project(proj_weight[low_width:, :])

    own = dt_weight.shape[1]
    for c in range(own // chunk):
        cols = slice(c * chunk, (c + 1) * chunk)
        block[...] = softplus(
            jnp.dot(low[...], dt_weight[:, cols], preferred_element_type=jnp.float32)
            + dt_bias[:, cols]
        )
        first = pl.multiple_of(part * own + c * chunk, chunk)

        def move(g, _):
            at = pl.multiple_of(g * 16, 16)
            step = block[pl.ds(at, 16), :]
            drive = step * conv_ref[pl.ds(at, 16), pl.ds(first, chunk)].astype(jnp.float32)
            for half in range(2):
                for j in range(chunk // LANES):
                    lane = c * (chunk // LANES) + j
                    to = pl.ds((at + half * 8) * GROUP + lane, 8, stride=GROUP)
                    part = (slice(half * 8, half * 8 + 8), slice(j * LANES, (j + 1) * LANES))
                    step_ref[to, :] = step[part]
                    drive_ref[to, :] = drive[part]
            return 0

        lax.fori_loop(0, rows // 16, move, 0)


def advance_state(state, step, drive, rates, in_rows, t):
    return tuple(
        jnp.exp2(step * rates[n]) * state[n] + drive * in_rows[n, pl.ds(t, 1), :]
        for n in range(len(rates))
    )


def ends_kernel(step_ref, drive_ref, maps_ref, decay, end_ref, in_rows):
    rows = step_ref.shape[0]
    states = decay.shape[0]

    @pl.when(pl.program_id(0) == 0)
    def _():
        spread_columns(maps_ref[...], in_rows, 0, states, rows)

    rates = [decay[n] for n in range(states)]

    def advance(i, carry):
        state, total = carry
        for p in range(16):
            t = i * 16 + p
            step = step_ref[t]
            total = total + step
            state = advance_state(state, step, drive_ref[t], rates, in_rows, t)
        return state, total

    zero = jnp.zeros((GROUP, LANES), jnp.float32)
    state, total = lax.fori_loop(0, rows // 16, advance, ((zero,) * states, zero))
    for n in range(states):
        end_ref[n] = state[n]
    end_ref[states] = total


def back_kernel(
    tok_ref, conv_ref, step_ref, drive_ref, maps_ref, decay, skip_gain, ffn_gain, *rest,
    before, final,
):
    count = max(before, 1)
    entry, rest = rest[:count], rest[count:]
    if final:
        hidden_ref, ffn_ref, kept, in_rows, out_rows, scanned = rest
    else:
        hidden_ref, ffn_ref, state_ref, kept, in_rows, out_rows, scanned = rest
    rows, width = tok_ref.shape
    states = decay.shape[0]
    tiles = width // LANES
    maps = maps_ref[...]
    spread_columns(maps, in_rows, 0, states, rows)
    spread_columns(maps, out_rows, states, states, rows)

    @pl.when(pl.program_id(0) == 0)
    def _():
        if not before:
            kept[...] = entry[0][...]
            return

        def enter(n, _):
            entering = entry[before - 1][n]
            for back in reversed(range(before - 1)):
                entering = jnp.exp2(entry[back][states] * decay[n]) * entering + entry[back][n]
            kept[n] = entering
            return 0

        lax.fori_loop(0, states, enter, 0)

    def scan_tile(k, _):
        mine = pl.ds(pl.multiple_of(k * GROUP, GROUP), GROUP)
        rates = [decay[n, mine, :] for n in range(states)]

        def advance(i, state):
            for p in range(8):
                t = i * 8 + p
                state = advance_state(state, step_ref[k, t], drive_ref[k, t], rates, in_rows, t)
                parts = [state[n] * out_rows[n, pl.ds(t, 1), :] for n in range(states)]
                while len(parts) > 1:
                    parts = [a + b for a, b in zip(parts[::2], parts[1::2])]
                scanned[k, pl.ds(pl.multiple_of(t * GROUP, GROUP), GROUP), :] = parts[0]
            return state

        state = lax.fori_loop(0, rows // 8, advance, tuple(kept[n, mine, :] for n in range(states)))
        for n in range(states):
            kept[n, mine, :] = state[n]
        return 0

    lax.fori_loop(0, tiles // GROUP, scan_tile, 0)
    if not final:
        state_ref[...] = kept[...]

    def finish(i, _):
        at = pl.multiple_of(i * 16, 16)
        squares = jnp.zeros((16, LANES), jnp.float32)
        for j in range(tiles):
            cols = pl.ds(j * LANES, LANES)
            group, lane = divmod(j, GROUP)
            came = jnp.concatenate(
                [
                    scanned[group, pl.ds((at + half * 8) * GROUP + lane, 8, stride=GROUP), :]
                    for half in range(2)
                ],
                axis=0,
            )
            conv = conv_ref[pl.ds(at, 16), cols].astype(jnp.float32)
            hidden = tok_ref[pl.ds(at, 16), cols].astype(jnp.float32) + (
                came + skip_gain[:, cols] * conv
            )
            hidden_ref[pl.ds(at, 16), cols] = hidden
            squares = squares + hidden * hidden
        mean = jnp.sum(squares, axis=-1, keepdims=True) / width
        scale = lax.rsqrt(mean + 1e-05)
        ffn_ref[pl.ds(at, 16), :] = (
            hidden_ref[pl.ds(at, 16), :] * scale * ffn_gain[...]
        ).astype(jnp.bfloat16)
        return 0

    lax.fori_loop(0, rows // 16, finish, 0)


def mixer(
    tokens, norm_gain, conv_weight, conv_bias, proj_weight, dt_weight, dt_bias, decay_rate,
    skip_gain, ffn_gain, parts, hold, note,
):
    rows, width = tokens.shape
    states = decay_rate.shape[0]
    low_width = dt_weight.shape[0]
    tiles = width // LANES
    f32, bf16 = jnp.float32, jnp.bfloat16
    shape = jax.ShapeDtypeStruct
    halo = note("h1", from_behind(tokens[rows - 16 :], "seq", 1))
    decay = (decay_rate * (-LOG2E)).reshape(states, tiles, LANES)
    row = lambda v: v.reshape(1, width)
    groups = tiles // GROUP
    wide = GROUP * LANES
    fixed = lambda v: pl.BlockSpec(v.shape, lambda k: (0,) * len(v.shape))
    slab = pl.BlockSpec((None, rows * GROUP, LANES), lambda k: (k, 0, 0))
    whole = [
        tokens, halo, row(norm_gain), conv_weight, row(conv_bias), proj_weight.T,
    ]
    conv, step, drive, maps = pl.pallas_call(
        front_kernel,
        grid=(groups,),
        out_shape=(
            shape((rows, width), bf16),
            shape((groups, rows * GROUP, LANES), f32),
            shape((groups, rows * GROUP, LANES), f32),
            shape((rows, 2 * states), f32),
        ),
        in_specs=[fixed(v) for v in whole]
        + [
            pl.BlockSpec((low_width, wide), lambda k: (0, k)),
            pl.BlockSpec((1, wide), lambda k: (0, k)),
        ],
        out_specs=(
            fixed(shape((rows, width), bf16)), slab, slab, fixed(shape((rows, 2 * states), f32)),
        ),
        scratch_shapes=[
            pltpu.VMEM((rows + 16, width), f32),
            pltpu.VMEM((rows, low_width), bf16),
            pltpu.VMEM((rows, 512), f32),
        ],
        compiler_params=params(),
        cost_estimate=cost(COST),
        name="mixer_front",
    )(*whole, dt_weight, row(dt_bias))
    conv, step, drive, maps = hold("front", conv, step, drive, maps)
    step = step.reshape(groups, rows, GROUP, LANES)
    drive = drive.reshape(groups, rows, GROUP, LANES)
    slab = pl.BlockSpec((None, rows, GROUP, LANES), lambda k: (k, 0, 0, 0))
    per_state = pl.BlockSpec((states, GROUP, LANES), lambda k: (0, k, 0))
    end = pl.pallas_call(
        ends_kernel,
        grid=(groups,),
        out_shape=shape((states + 1, tiles, LANES), f32),
        in_specs=[slab, slab, fixed(maps), per_state],
        out_specs=pl.BlockSpec((states + 1, GROUP, LANES), lambda k: (0, k, 0)),
        scratch_shapes=[pltpu.VMEM((states, rows, LANES), f32)],
        compiler_params=params(),
        cost_estimate=cost(COST),
        name="mixer_ends",
    )(step, drive, maps, decay)
    end, = hold("ends", end)
    before = lax.axis_size("seq") - 1
    ends = [note(f"e{by + 1}", from_behind(end, "seq", by + 1)) for by in range(before)]

    count = rows // parts
    piece = min(64, count)
    steps = count // piece
    outs = []
    state = None
    for part in range(parts):
        first = part * steps
        wide = pl.BlockSpec((piece, width), lambda i, first=first: (first + i, 0))
        deep = pl.BlockSpec((groups, piece, GROUP, LANES), lambda i, first=first: (0, first + i, 0, 0))
        narrow = pl.BlockSpec((piece, 2 * states), lambda i, first=first: (first + i, 0))
        whole = lambda v: pl.BlockSpec(v.shape, lambda i, r=v.ndim: (0,) * r)
        out = pl.BlockSpec((piece, width), lambda i: (i, 0))
        entry = ends if part == 0 else [state]
        final = part == parts - 1
        fixed = [decay, row(skip_gain), row(ffn_gain), *entry]
        got = pl.pallas_call(
            functools.partial(back_kernel, before=before if part == 0 else 0, final=final),
            grid=(steps,),
            out_shape=(shape((count, width), f32), shape((count, width), bf16))
            + (() if final else (shape(decay.shape, f32),)),
            in_specs=[wide, wide, deep, deep, narrow] + [whole(v) for v in fixed],
            out_specs=(out, out) + (() if final else (whole(decay),)),
            scratch_shapes=[
                pltpu.VMEM((states, tiles, LANES), f32),
                pltpu.VMEM((states, piece, LANES), f32),
                pltpu.VMEM((states, piece, LANES), f32),
                pltpu.VMEM((groups, piece * GROUP, LANES), f32),
            ],
            compiler_params=params(),
            cost_estimate=cost(COST),
            name="mixer_back",
        )(tokens, conv, step, drive, maps, *fixed)
        got = hold(f"back{part}", *got)
        outs.append(got[:2])
        state = got[2] if not final else None
    return [o[0] for o in outs], [o[1] for o in outs]


def swap(array, axis, mask):
    peers = lax.axis_size(axis)
    return lax.ppermute(array, axis, [(i, i ^ mask) for i in range(peers)])


def after(array, *others):
    return lax.optimization_barrier((array, *others))[0]


class Transfers:
    def __init__(self, w_gate, w_up, w_down):
        share = w_gate.shape[1] // lax.axis_size("seq")
        at = lax.axis_index("seq") * share
        both = jnp.concatenate(
            [lax.dynamic_slice_in_dim(w, at, share, axis=1) for w in (w_gate, w_up)], axis=1
        )
        down = lax.dynamic_slice_in_dim(w_down, at, share, axis=0)
        self.chunks = []
        for whole, sizes, axis in ((both, DEEP, 0), (down, BROAD, 1)):
            at = 0
            for size in sizes:
                self.chunks.append(lax.slice_in_dim(whole, at, at + size, axis=axis))
                at += size
        self.made = {}

    def put(self, name, array, axis, mask):
        self.made[name] = swap(self.ready(name, array), axis, mask)
        return self.made[name]

    def ready(self, name, array):
        return after(array, *[self.get(other) for other in STARTS.get(name, ())])

    def note(self, name, array):
        self.made[name] = array
        return array

    def weigh(self, chosen, route_scale):
        experts = jnp.arange(lax.axis_size("expert"), dtype=jnp.int32)[:, None, None]
        self.dense = jnp.sum(jnp.where(chosen[None] == experts, route_scale[None], 0.0), axis=2)

    def scales(self):
        if not hasattr(self, "parts"):
            me = lax.axis_index("expert")
            group = jnp.concatenate([self.dense] + [self.get(f"w{c}") for c in (2, 1, 3)], axis=1)
            both = jnp.stack([group[me], group[me ^ 4]], axis=1).reshape(4, 2, -1, 2)
            self.parts = [both[:, h].reshape(-1, 2) for h in range(2)]
        return self.parts

    def get(self, name):
        if name not in self.made:
            kind, c = name[0], int(name[1:])
            if kind == "q":
                return self.scales()[c] if c < 2 else self.chunks[len(DEEP) + c - 2]
            if kind == "w":
                send, axis, mask = self.dense, "expert", c
            elif kind == "z":
                send, axis, mask = self.chunks[c], "expert", 4
            elif kind == "x":
                send, axis, mask = self.get(f"z{c}"), "seq", 1
            elif kind == "y":
                send, axis, mask = self.get(f"z{c}"), "seq", 2
            elif c in DIRECT:
                send, axis, mask = self.get(f"z{c}"), "seq", 3
            elif c in CORNERS_X:
                send, axis, mask = self.get(f"y{c}"), "seq", 1
            else:
                send, axis, mask = self.get(f"x{c}"), "seq", 2
            self.put(name, send, axis, mask)
        return self.made[name]

    def pieces(self, c):
        return [self.get(f"{kind}{c}") for kind in "zxyc"]

    def hold(self, kernel, *arrays):
        self.made[kernel] = arrays[-1]
        others = [self.get(name) for name in WAITS.get(kernel, ())]
        return lax.optimization_barrier((*arrays, *others))[: len(arrays)]


def act_kernel(*refs, blocks, near, deep):
    xs, refs = refs[:blocks], refs[blocks:]
    fixed, refs = refs[: 2 * near], refs[2 * near :]
    pieces, refs = refs[: 4 * deep], refs[4 * deep :]
    scale, refs = refs[0], refs[1:]
    outs, refs = refs[: near + bool(deep)], refs[near + bool(deep) :]
    rows_in, held, sems = refs[0], refs[1:-1], refs[-1]
    count = xs[0].shape[0]
    copies = [(xs[b], rows_in.at[pl.ds(b * count, count), :]) for b in range(blocks)]
    copies += list(zip(fixed, held))
    first = len(copies)
    at = 0
    for c in range(deep):
        depth, both = pieces[4 * c].shape
        for origin in range(4):
            target = held[-1].at[pl.ds(at, depth), pl.ds(origin * both, both)]
            copies.append((pieces[4 * c + origin], target))
        at += depth
    copies = [pltpu.make_async_copy(a, b, sems.at[i]) for i, (a, b) in enumerate(copies)]
    for copy in copies:
        copy.start()
    for copy in copies[:first]:
        copy.wait()
    if near:
        hidden = held[0].shape[1]
        tile = hidden // 2
        for j in range(2):
            cols = slice(j * tile, (j + 1) * tile)
            g = jnp.dot(rows_in[...], held[0][:, cols], preferred_element_type=jnp.float32)
            u = jnp.dot(rows_in[...], held[1][:, cols], preferred_element_type=jnp.float32)
            outs[0][:, cols] = (silu(g) * u * scale[:, 0:1]).astype(jnp.bfloat16)
    for copy in copies[first:]:
        copy.wait()
    if deep:
        share = both // 2
        for origin in range(4):
            cols = slice(origin * both, (origin + 1) * both)
            got = jnp.dot(rows_in[...], held[-1][:, cols], preferred_element_type=jnp.float32)
            outs[-1][:, origin * share : (origin + 1) * share] = (
                silu(got[:, :share]) * got[:, share:] * scale[:, 1:2]
            ).astype(jnp.bfloat16)


def act(xs, scale, near=(), chunks=()):
    rows = sum(x.shape[0] for x in xs)
    width = xs[0].shape[1]
    pieces = [piece for chunk in chunks for piece in chunk]
    away = pl.BlockSpec(memory_space=pl.ANY)
    copies = len(xs) + len(near) + len(pieces)
    hidden = [w.shape[1] for w in near[:1]] + [2 * p.shape[1] for p in pieces[:1]]
    held = [w.shape for w in near] + [(width, 4 * p.shape[1]) for p in pieces[:1]]
    return pl.pallas_call(
        functools.partial(
            act_kernel, blocks=len(xs), near=int(bool(near)), deep=len(chunks)
        ),
        out_shape=[jax.ShapeDtypeStruct((rows, h), jnp.bfloat16) for h in hidden],
        in_specs=[away] * copies + [pl.BlockSpec(memory_space=pltpu.VMEM)],
        scratch_shapes=[pltpu.VMEM((rows, width), jnp.bfloat16)]
        + [pltpu.VMEM(shape, jnp.bfloat16) for shape in held]
        + [pltpu.SemaphoreType.DMA((copies,))],
        compiler_params=params(),
        cost_estimate=cost(COST),
        name="act",
    )(*xs, *near, *pieces, scale)


def down_kernel(*refs, halves):
    nears, fars, refs = refs[:halves], refs[halves : 2 * halves], refs[2 * halves :]
    near_weight, pieces, (keep_ref, send_ref, weight) = refs[0], refs[1:5], refs[5:]
    share = pieces[0].shape[0]
    for origin in range(4):
        weight[origin * share : (origin + 1) * share, :] = pieces[origin][...]
    rows = keep_ref.shape[0] // 2
    count = rows // halves
    for h in range(halves):
        total = jnp.dot(nears[h][...], near_weight[...], preferred_element_type=jnp.float32)
        total = total + jnp.dot(fars[h][...], weight[...], preferred_element_type=jnp.float32)
        own, ahead, mate, ahead_mate = [total[b * count : (b + 1) * count] for b in range(4)]
        keep_ref[h * count : (h + 1) * count, :] = own
        keep_ref[rows + h * count : rows + (h + 1) * count, :] = ahead
        send_ref[h * count : (h + 1) * count, :] = mate.astype(jnp.bfloat16)
        send_ref[rows + h * count : rows + (h + 1) * count, :] = ahead_mate.astype(jnp.bfloat16)


def down(nears, fars, w_down, pieces, at, skip):
    share = pieces[0].shape[0]
    hidden = w_down.shape[0]
    rows = 2 * sum(a.shape[0] // 4 for a in nears)
    tile = 512
    whole = lambda v: pl.BlockSpec(v.shape, lambda i: (0, 0))
    out = pl.BlockSpec((rows, tile), lambda i: (0, i))
    acts = [*nears, *fars]
    return pl.pallas_call(
        functools.partial(down_kernel, halves=len(nears)),
        grid=(PANEL // tile,),
        out_shape=(
            jax.ShapeDtypeStruct((rows, PANEL), jnp.float32),
            jax.ShapeDtypeStruct((rows, PANEL), jnp.bfloat16),
        ),
        in_specs=[whole(v) for v in acts]
        + [pl.BlockSpec((hidden, tile), lambda i: (0, at // tile + i))]
        + [pl.BlockSpec((share, tile), lambda i: (0, skip // tile + i)) for _ in pieces],
        out_specs=(out, out),
        scratch_shapes=[pltpu.VMEM((4 * share, tile), jnp.bfloat16)],
        compiler_params=params(),
        cost_estimate=cost(COST),
        name="down",
    )(*acts, w_down, *pieces)


def routed_by_weights(hidden, ffn_in, w_gate, w_up, w_down, moves):
    rows = hidden[0].shape[0] * len(hidden)
    halves = len(ffn_in)
    ahead = [moves.put(f"t{h}", ffn_in[h], "expert", 2) for h in range(halves)]
    parts = moves.scales()
    own = (w_gate, w_up)

    def group_rows(h):
        if MERGE:
            own = jnp.concatenate([ffn_in[h], ahead[h]], axis=0)
            return [own, moves.put(f"n{h}", own, "expert", 1)]
        mate = moves.put(f"m{h}", ffn_in[h], "expert", 1)
        return [ffn_in[h], ahead[h], mate, moves.put(f"n{h}", ahead[h], "expert", 1)]

    xs = group_rows(0)
    if TOGETHER:
        chunks = [moves.pieces(c) for c in range(len(DEEP))]
        near0, far0 = moves.hold("near0", *act(xs, parts[0], near=own, chunks=chunks))
        far0, = moves.hold("far0", far0)
    else:
        near0, = moves.hold("near0", *act(xs, parts[0], near=own))
        chunks = [moves.pieces(c) for c in range(len(DEEP))]
        far0, = moves.hold("far0", *act(xs, after(parts[0], near0), chunks=chunks))
    xs = group_rows(1)
    near1, far1 = moves.hold("act1", *act(xs, after(parts[1], far0), near=own, chunks=chunks))
    columns = []
    whole_hidden = jnp.concatenate(hidden, axis=0)
    order = [far1]
    for c, wide in enumerate(BROAD):
        pieces = moves.pieces(len(DEEP) + c)
        for skip in range(0, wide, PANEL):
            d = len(columns)
            at = d * PANEL
            held = [after(pieces[0], *order), *pieces[1:]]
            keep, send = down([near0, near1], [far0, far1], w_down, held, at, skip)
            keep, send = moves.hold(f"down{d}", keep, send)
            came = moves.put(f"s{d}", send, "expert", 1)
            order = [send, came] if IN_TURN else [send]
            came = came.astype(jnp.float32)
            back = (keep[rows:] + came[rows:]).astype(jnp.bfloat16)
            back = moves.put(f"r{d}", back, "expert", 2).astype(jnp.float32)
            total = (keep[:rows] + came[:rows]) + back
            columns.append(whole_hidden[:, at : at + PANEL] + total)
    return jnp.concatenate(columns, axis=1)


def routed_by_slots(ffn_in, chosen, route_scale, w_gate, w_up, w_down):
    tok_count, model_width = ffn_in.shape
    owners = lax.axis_size("expert")
    experts = owners * w_gate.shape[0]
    capacity = 4 * tok_count // owners
    chosen = chosen.reshape(-1)
    onehot = (chosen[:, None] == jnp.arange(experts, dtype=jnp.int32)[None, :]).astype(jnp.int32)
    before = jnp.cumsum(onehot, axis=0) - onehot
    slot_pos = jnp.sum(before * onehot, axis=1)
    dest_row = chosen * capacity + slot_pos
    outgoing = (
        jnp.zeros((experts * capacity, model_width), jnp.bfloat16)
        .at[dest_row]
        .set(jnp.repeat(ffn_in, 2, axis=0))
    )
    outgoing = outgoing.reshape(experts, capacity, model_width)
    received = lax.all_to_all(outgoing, "expert", split_axis=0, concat_axis=0, tiled=True)
    recv_shape = received.shape
    rows_in = received.reshape(-1, model_width)
    gate_part = jnp.dot(rows_in, w_gate[0], preferred_element_type=jnp.float32)
    up_part = jnp.dot(rows_in, w_up[0], preferred_element_type=jnp.float32)
    inner_act = (jax.nn.silu(gate_part) * up_part).astype(jnp.bfloat16)
    result = jnp.dot(inner_act, w_down[0], preferred_element_type=jnp.float32).astype(jnp.bfloat16)
    returned = lax.all_to_all(
        result.reshape(recv_shape), "expert", split_axis=0, concat_axis=0, tiled=True
    )
    gathered = returned.reshape(experts * capacity, model_width)[dest_row].astype(jnp.float32)
    weighted = (route_scale.reshape(-1)[:, None] * gathered).reshape(tok_count, 2, model_width)
    return weighted[:, 0] + weighted[:, 1]


def per_device(
    tokens, norm_gain, conv_weight, conv_bias, proj_weight, dt_weight, dt_bias, decay_rate,
    skip_gain, ffn_gain, expert_ids, route_weights, w_gate, w_up, w_down,
):
    by_weights = lax.axis_size("expert") == 8 and lax.axis_size("seq") == 4
    hold = lambda kernel, *arrays: arrays
    note = lambda name, array: array
    if by_weights:
        moves = Transfers(w_gate[0], w_up[0], w_down[0])
        moves.weigh(expert_ids[0], route_weights[0])
        hold, note = moves.hold, moves.note
    hidden, ffn_in = mixer(
        tokens[0], norm_gain, conv_weight, conv_bias, proj_weight, dt_weight, dt_bias,
        decay_rate, skip_gain, ffn_gain, 2 if by_weights else 1, hold, note,
    )
    if by_weights:
        out = routed_by_weights(
            hidden, ffn_in, w_gate[0], w_up[0], w_down[0], moves
        )
    else:
        out = hidden[0] + routed_by_slots(
            ffn_in[0], expert_ids[0], route_weights[0], w_gate, w_up, w_down
        )
    return out.astype(jnp.bfloat16)[None]


def solution(mesh):
    in_specs = (
        P("expert", "seq", None),
        P(), P(), P(), P(), P(), P(), P(), P(), P(),
        P("expert", "seq", None),
        P("expert", "seq", None),
        P("expert", None, None),
        P("expert", None, None),
        P("expert", None, None),
    )
    out_specs = P("expert", "seq", None)
    return jax.shard_map(
        per_device, mesh=mesh, in_specs=in_specs, out_specs=out_specs, check_vma=False
    )
```

time: 323 us -> 283 us (0.88)
  waiting for transfers between devices: 110 us -> 74.8 us
  Pallas kernels: 136 us -> 122 us
  starting transfers between devices: 50.4 us -> 62.7 us
  local copies, waits for them, and re-layouts: 17.2 us -> 12.8 us
    ppermute x44 -> x45, waiting for transfers between devices: 102 us -> 63.6 us  [swap(): return lax.ppermute(array, axis, [(i, i ^ mask) for i in range(peers)])]
    ppermute x44 -> x45, starting transfers between devices: 40.4 us -> 52.7 us  [swap(): return lax.ppermute(array, axis, [(i, i ^ mask) for i in range(peers)])]
    pallas_call x10 -> x9, Pallas kernels: 104 us -> 93.4 us  [the longest x3 38.3 us: act(): pl.pallas_call(functools.partial(act_kernel, blocks=len(xs), near=int(boo...]
    unnamed x91 -> x86, local copies, waits for them, and re-layouts: 10.5 us -> 5.41 us
    pallas_call x2, Pallas kernels: 32.5 us -> 28.7 us  [mixer(): pl.pallas_call(functools.partial(back_kernel, before=before if part == 0...]
    ppermute x4, waiting for transfers between devices: 7.9 us -> 11.2 us  [from_behind(): return lax.ppermute(array, axis, pairs)]
  transfers between devices with their start and end apart: 48 -> 49, of which waited for: 16 -> 18; matrix products, arithmetic and copies ran while one was open for 4% -> 4% of each run, Pallas kernels for 42% -> 43%
where the time goes in v3:
time: 283 us
  Pallas kernels  122 us (43%)
  waiting for transfers between devices  74.8 us (26%)
  starting transfers between devices  62.7 us (22%)
  local copies, waits for them, and re-layouts  12.8 us (5%)
  other arithmetic  9.74 us (3%)
    ppermute x45, waiting for transfers between devices, swap(): return lax.ppermute(array, axis, [(i, i ^ mask) for i in range(peers)])  63.6 us
    ppermute x45, starting transfers between devices, swap(): return lax.ppermute(array, axis, [(i, i ^ mask) for i in range(peers)])  52.7 us
    pallas_call x3, Pallas kernels, act(): pl.pallas_call(functools.partial(act_kernel, blocks=len(xs), near=int(boo...  38.3 us
    pallas_call x2, Pallas kernels, mixer(): pl.pallas_call(functools.partial(back_kernel, before=before if part == 0...  28.7 us
    pallas_call x4, Pallas kernels, down(): pl.pallas_call(functools.partial(down_kernel, halves=len(nears)), grid=(P...  22.7 us
    pallas_call x1, Pallas kernels, mixer(): pl.pallas_call(front_kernel, grid=(groups,), out_shape=(shape((rows, widt...  17.2 us
    pallas_call x1, Pallas kernels, mixer(): pl.pallas_call(ends_kernel, grid=(groups,), out_shape=shape((states + 1,...  15.2 us
    ppermute x4, waiting for transfers between devices, from_behind(): return lax.ppermute(array, axis, pairs)  11.2 us
  transfers between devices with their start and end apart: 49, of which 18 were waited for; matrix products, arithmetic and copies ran while one was open for 4% of the time, Pallas kernels for 43%

profile of v3, /device:TPU:0, one launch (start us, length us, event | category | flops | bytes accessed | tf_op | source)
XLA Modules:
  0.0 282.8 jit_solution(13178152476370647187)
XLA Ops:
  10.4 3.4 %collective-permute-start = (bf16[16,4096]{1,0:T(8,128)(2,1)S(1)}, bf16[16,4096]{1,0:T(8,128)(2,1)S(1)}, u32[]{:S(2)}, u32[]{:S(2)}) collective-permute-start(bf16[16,4096]{1,0:T(8,128)(2,1)S(1)} %slice_bitcast_fusion), channel_id=1, source_target_pairs={{0,8},{8,16},{16,24},{1,9},{9,17},{17,25},{2,10},{10,18},{18,26},{... | collective-permute-start | bytes 393224 | tf_op jit(solution)/shard_map/ppermute | solution.py:31
  16.9 17.2 %mixer_front.1 = (bf16[256,4096]{1,0:T(8,128)(2,1)}, f32[4,2048,128]{2,1,0:T(8,128)}, f32[4,2048,128]{2,1,0:T(8,128)}, f32[256,32]{1,0:T(8,128)}) custom-call(bf16[256,4096]{1,0:T(8,128)(2,1)} %bitcast.51, bf16[16,4096]{1,0:T(8,128)(2,1)} %copy-done.39, f32[1,4096]{1,0:T(1,128)} %bitcast.65, f32[4,4096]{1,0:T(4,128)} %conv_weight.1, f32[1,4096]{1,0:T(1,128)} %bitcast.66, ...), custom_call_target="tpu_custom_call" | custom-call | flops 345000000 | bytes 65536 | tf_op jit(solution)/shard_map/mixer_front/pallas_call | solution.py:271
  34.1 3.4 %collective-permute-start.6 = (bf16[1024,256]{1,0:T(8,128)(2,1)S(1)}, bf16[1024,256]{1,0:T(8,128)(2,1)S(1)}, u32[]{:S(2)}, u32[]{:S(2)}) collective-permute-start(bf16[1024,256]{1,0:T(8,128)(2,1)S(1)} %collective-permute-done.4.refs_4_.refs_6_), channel_id=1, source_target_pairs={{0,16},{8,24},{16,0},{24,8},{1,17},{9,25},{17,1},{25,9},{2,18},{10... | collective-permute-start | bytes 1572872 | tf_op jit(solution)/shard_map/ppermute | solution.py:357
  39.3 15.2 %mixer_ends.1 = f32[17,32,128]{2,1,0:T(8,128)} custom-call(f32[4,256,8,128]{3,2,1,0:T(8,128)} %bitcast.41, f32[4,256,8,128]{3,2,1,0:T(8,128)} %bitcast.44, f32[256,32]{1,0:T(8,128)} %get-tuple-element.87.maps_ref, f32[16,32,128]{2,1,0:T(8,128)} %bitcast.54), custom_call_target="tpu_custom_call" | custom-call | flops 345000000 | bytes 65536 | tf_op jit(solution)/shard_map/mixer_ends/pallas_call | solution.py:302
  64.4 5.0 %collective-permute-done.8.rest_1_ = f32[17,32,128]{2,1,0:T(8,128)S(1)} collective-permute-done((f32[17,32,128]{2,1,0:T(8,128)}, f32[17,32,128]{2,1,0:T(8,128)S(1)}, u32[]{:S(2)}, u32[]{:S(2)}) %collective-permute-start.8) | collective-permute-done | bytes 278560 | tf_op jit(solution)/shard_map/ppermute | solution.py:31
  74.4 14.6 %mixer_back.2 = (f32[128,4096]{1,0:T(8,128)}, bf16[128,4096]{1,0:T(8,128)(2,1)}, f32[16,32,128]{2,1,0:T(8,128)}) custom-call(bf16[256,4096]{1,0:T(8,128)(2,1)} %bitcast.52, bf16[256,4096]{1,0:T(8,128)(2,1)} %get-tuple-element.84.conv_ref, f32[4,256,8,128]{3,2,1,0:T(8,128)} %bitcast.42, f32[4,256,8,128]{3,2,1,0:T(8,128)} %bitcast.45, ...), custom_call_target="tpu_custom_call" | custom-call | flops 345000000 | bytes 65536 | tf_op jit(solution)/shard_map/mixer_back/pallas_call | solution.py:332
  96.1 7.2 %collective-permute-done.16.refs_9_.refs_11_ = bf16[1024,256]{1,0:T(8,128)(2,1)S(1)} collective-permute-done((bf16[1024,256]{1,0:T(8,128)(2,1)S(1)}, bf16[1024,256]{1,0:T(8,128)(2,1)S(1)}, u32[]{:S(2)}, u32[]{:S(2)}) %collective-permute-start.16) | collective-permute-done | bytes 524320 | tf_op jit(solution)/shard_map/ppermute | solution.py:357
  105.0 14.1 %mixer_back.3 = (f32[128,4096]{1,0:T(8,128)}, bf16[128,4096]{1,0:T(8,128)(2,1)}) custom-call(bf16[256,4096]{1,0:T(8,128)(2,1)} %bitcast.53, bf16[256,4096]{1,0:T(8,128)(2,1)} %get-tuple-element.84.conv_ref, f32[4,256,8,128]{3,2,1,0:T(8,128)} %bitcast.43, f32[4,256,8,128]{3,2,1,0:T(8,128)} %bitcast.46, f32[256,32]{1,0:T(8,128)} %get-tuple-element.87.maps_ref, ...), custom_call_target="tpu_custom_call" | custom-call | flops 345000000 | bytes 65536 | tf_op jit(solution)/shard_map/mixer_back/pallas_call | solution.py:332
  119.5 6.7 %collective-permute-done.18.refs_1_ = bf16[128,4096]{1,0:T(8,128)(2,1)S(1)} collective-permute-done((bf16[128,4096]{1,0:T(8,128)(2,1)}, bf16[128,4096]{1,0:T(8,128)(2,1)S(1)}, u32[]{:S(2)}, u32[]{:S(2)}) %collective-permute-start.18) | collective-permute-done | bytes 1048608 | tf_op jit(solution)/shard_map/ppermute | solution.py:357
  135.5 4.0 %collective-permute-start.22 = (bf16[128,2048]{1,0:T(8,128)(2,1)}, bf16[128,2048]{1,0:T(8,128)(2,1)}, u32[]{:S(2)}, u32[]{:S(2)}) collective-permute-start(bf16[128,2048]{1,0:T(8,128)(2,1)} %slice.133), channel_id=1, source_target_pairs={{0,4},{1,5},{2,6},{3,7},{4,0},{5,1},{6,2},{7,3},{8,12},{9,13},{10,... | collective-permute-start | bytes 1572872 | tf_op jit(solution)/shard_map/ppermute | solution.py:357
  140.4 11.3 %act.3.refs_0_ = bf16[512,512]{1,0:T(8,128)(2,1)} custom-call(bf16[128,4096]{1,0:T(8,128)(2,1)} %get-tuple-element.105.refs_0_, bf16[128,4096]{1,0:T(8,128)(2,1)} %copy-done.1, bf16[128,4096]{1,0:T(8,128)(2,1)} %copy-done.2, bf16[128,4096]{1,0:T(8,128)(2,1)} %collective-permute-done.20.refs_3_, bf16[4096,512]{1,0:T(8,128)(2,1)} %bitcast.47, ...), custom_call_target="tpu_custom_call" | custom-call | flops 345000000 | bytes 65536 | tf_op jit(solution)/shard_map/act/pallas_call | solution.py:485
  153.7 10.5 %collective-permute-done.26.refs_1_ = bf16[128,4096]{1,0:T(8,128)(2,1)} collective-permute-done((bf16[128,4096]{1,0:T(8,128)(2,1)}, bf16[128,4096]{1,0:T(8,128)(2,1)}, u32[]{:S(2)}, u32[]{:S(2)}) %collective-permute-start.26) | collective-permute-done | bytes 1048608 | tf_op jit(solution)/shard_map/ppermute | solution.py:357
  164.8 3.8 %collective-permute-start.32 = (bf16[128,2048]{1,0:T(8,128)(2,1)}, bf16[128,2048]{1,0:T(8,128)(2,1)S(1)}, u32[]{:S(2)}, u32[]{:S(2)}) collective-permute-start(bf16[128,2048]{1,0:T(8,128)(2,1)} %collective-permute-done.22.refs_5_), channel_id=1, source_target_pairs={{0,8},{8,0},{16,24},{24,16},{1,9},{9,1},{17,25},{25,17},{2,10},{10... | collective-permute-start | bytes 1572872 | tf_op jit(solution)/shard_map/ppermute | solution.py:357
  171.2 11.1 %act.4.refs_2_ = bf16[512,512]{1,0:T(8,128)(2,1)} custom-call(bf16[128,4096]{1,0:T(8,128)(2,1)} %get-tuple-element.105.refs_0_, bf16[128,4096]{1,0:T(8,128)(2,1)} %copy-done.1, bf16[128,4096]{1,0:T(8,128)(2,1)} %copy-done.2, bf16[128,4096]{1,0:T(8,128)(2,1)} %collective-permute-done.20.refs_3_, bf16[1024,256]{1,0:T(8,128)(2,1)} %copy-done.16, ...), custom_call_target="tpu_custom_call" | custom-call | flops 345000000 | bytes 65536 | tf_op jit(solution)/shard_map/act/pallas_call | solution.py:485
  186.8 16.0 %act.5 = (bf16[512,512]{1,0:T(8,128)(2,1)}, bf16[512,512]{1,0:T(8,128)(2,1)}) custom-call(bf16[128,4096]{1,0:T(8,128)(2,1)} %get-tuple-element.114.refs_0_, bf16[128,4096]{1,0:T(8,128)(2,1)} %collective-permute-done.26.refs_1_, bf16[128,4096]{1,0:T(8,128)(2,1)} %collective-permute-done.27.refs_2_, bf16[128,4096]{1,0:T(8,128)(2,1)} %collective-permute-done.28.refs_3_, ...), custom_call_target="tpu_custom_call" | custom-call | flops 345000000 | bytes 65536 | tf_op jit(solution)/shard_map/act/pallas_call | solution.py:485
  204.9 4.6 %collective-permute-done.35.refs_6_ = bf16[128,1024]{1,0:T(8,128)(2,1)S(1)} collective-permute-done((bf16[128,1024]{1,0:T(8,128)(2,1)S(1)}, bf16[128,1024]{1,0:T(8,128)(2,1)S(1)}, u32[]{:S(2)}, u32[]{:S(2)}) %collective-permute-start.35) | collective-permute-done | bytes 262176 | tf_op jit(solution)/shard_map/ppermute | solution.py:357
  210.4 5.7 %down.4 = (f32[512,1024]{1,0:T(8,128)}, bf16[512,1024]{1,0:T(8,128)(2,1)}) custom-call(bf16[512,512]{1,0:T(8,128)(2,1)} %act.3.refs_0_, bf16[512,512]{1,0:T(8,128)(2,1)} %get-tuple-element.126.refs_1_, bf16[512,512]{1,0:T(8,128)(2,1)} %act.4.refs_2_, bf16[512,512]{1,0:T(8,128)(2,1)} %get-tuple-element.127.refs_3_, bf16[512,4096]{1,0:T(8,128)(2,1)} %bitcast.37, ...), custom_call_target="tpu_custom_call" | custom-call | flops 345000000 | bytes 65536 | tf_op jit(solution)/shard_map/down/pallas_call | solution.py:526
  216.8 5.7 %down.5 = (f32[512,1024]{1,0:T(8,128)}, bf16[512,1024]{1,0:T(8,128)(2,1)}) custom-call(bf16[512,512]{1,0:T(8,128)(2,1)} %act.3.refs_0_, bf16[512,512]{1,0:T(8,128)(2,1)} %get-tuple-element.126.refs_1_, bf16[512,512]{1,0:T(8,128)(2,1)} %act.4.refs_2_, bf16[512,512]{1,0:T(8,128)(2,1)} %get-tuple-element.127.refs_3_, bf16[512,4096]{1,0:T(8,128)(2,1)} %bitcast.38, ...), custom_call_target="tpu_custom_call" | custom-call | flops 345000000 | bytes 65536 | tf_op jit(solution)/shard_map/down/pallas_call | solution.py:526
  231.7 5.6 %collective-permute-done.43.refs_7_ = bf16[128,1024]{1,0:T(8,128)(2,1)} collective-permute-done((bf16[128,1024]{1,0:T(8,128)(2,1)S(1)}, bf16[128,1024]{1,0:T(8,128)(2,1)}, u32[]{:S(2)}, u32[]{:S(2)}) %collective-permute-start.43) | collective-permute-done | bytes 262176 | tf_op jit(solution)/shard_map/ppermute | solution.py:357
  237.2 5.7 %down.6 = (f32[512,1024]{1,0:T(8,128)}, bf16[512,1024]{1,0:T(8,128)(2,1)}) custom-call(bf16[512,512]{1,0:T(8,128)(2,1)} %act.3.refs_0_, bf16[512,512]{1,0:T(8,128)(2,1)} %get-tuple-element.126.refs_1_, bf16[512,512]{1,0:T(8,128)(2,1)} %act.4.refs_2_, bf16[512,512]{1,0:T(8,128)(2,1)} %get-tuple-element.127.refs_3_, bf16[512,4096]{1,0:T(8,128)(2,1)} %bitcast.39, ...), custom_call_target="tpu_custom_call" | custom-call | flops 345000000 | bytes 65536 | tf_op jit(solution)/shard_map/down/pallas_call | solution.py:526
  243.7 5.6 %down.7 = (f32[512,1024]{1,0:T(8,128)}, bf16[512,1024]{1,0:T(8,128)(2,1)}) custom-call(bf16[512,512]{1,0:T(8,128)(2,1)} %act.3.refs_0_, bf16[512,512]{1,0:T(8,128)(2,1)} %get-tuple-element.126.refs_1_, bf16[512,512]{1,0:T(8,128)(2,1)} %act.4.refs_2_, bf16[512,512]{1,0:T(8,128)(2,1)} %get-tuple-element.127.refs_3_, bf16[512,4096]{1,0:T(8,128)(2,1)} %bitcast.40, ...), custom_call_target="tpu_custom_call" | custom-call | flops 345000000 | bytes 65536 | tf_op jit(solution)/shard_map/down/pallas_call | solution.py:526
  257.3 9.7 %collective-permute-done.46 = bf16[256,1024]{1,0:T(8,128)(2,1)S(1)} collective-permute-done((bf16[256,1024]{1,0:T(8,128)(2,1)S(1)}, bf16[256,1024]{1,0:T(8,128)(2,1)S(1)}, u32[]{:S(2)}, u32[]{:S(2)}) %collective-permute-start.46) | collective-permute-done | bytes 524320 | tf_op jit(solution)/shard_map/ppermute | solution.py:357
  267.0 11.0 %collective-permute-done.48 = bf16[256,1024]{1,0:T(8,128)(2,1)} collective-permute-done((bf16[256,1024]{1,0:T(8,128)(2,1)S(1)}, bf16[256,1024]{1,0:T(8,128)(2,1)}, u32[]{:S(2)}, u32[]{:S(2)}) %collective-permute-start.48) | collective-permute-done | bytes 524320 | tf_op jit(solution)/shard_map/ppermute | solution.py:357
  277.9 3.3 %fusion.16 = (bf16[1,256,1024]{2,1,0:T(8,128)(2,1)S(1)}, bf16[1,256,1024]{2,1,0:T(8,128)(2,1)S(1)}, bf16[1,256,1024]{2,1,0:T(8,128)(2,1)S(1)}, bf16[1,256,1024]{2,1,0:T(8,128)(2,1)S(1)}) fusion(bf16[256,1024]{1,0:T(8,128)(2,1)S(1)} %collective-permute-done.39, f32[512,1024]{1,0:T(8,128)S(1)} %convert_element_type.44, f32[512,1024]{1,0:T(8,128)S(1)} %copy-done.9, ...), kind=kLoop, calls=%fused_computation.35 | loop fusion | flops 5242880 | bytes 16777216 | tf_op jit(solution)/shard_map/concatenate | solution.py:587
  (197 shorter events, 82.0 us)
Async XLA Ops:
  6.8 27.3 %collective-permute-start.4 = (bf16[1024,256]{1,0:T(8,128)(2,1)S(1)}, bf16[1024,256]{1,0:T(8,128)(2,1)S(1)}, u32[]{:S(2)}, u32[]{:S(2)}) collective-permute-start(bf16[1024,256]{1,0:T(8,128)(2,1)S(1)} %get-tuple-element.83), channel_id=1, source_target_pairs={{0,4},{1,5},{2,6},{3,7},{4,0},{5,1},{6,2},{7,3},{8,12},{9,13},{10,... | collective-permute-start | bytes 1572872 | tf_op jit(solution)/shard_map/ppermute | solution.py:357
  34.1 20.4 %collective-permute-start.6 = (bf16[1024,256]{1,0:T(8,128)(2,1)S(1)}, bf16[1024,256]{1,0:T(8,128)(2,1)S(1)}, u32[]{:S(2)}, u32[]{:S(2)}) collective-permute-start(bf16[1024,256]{1,0:T(8,128)(2,1)S(1)} %collective-permute-done.4.refs_4_.refs_6_), channel_id=1, source_target_pairs={{0,16},{8,24},{16,0},{24,8},{1,17},{9,25},{17,1},{25,9},{2,18},{10... | collective-permute-start | bytes 1572872 | tf_op jit(solution)/shard_map/ppermute | solution.py:357
  38.2 23.5 %collective-permute-start.11 = (bf16[1024,256]{1,0:T(8,128)(2,1)S(1)}, bf16[1024,256]{1,0:T(8,128)(2,1)S(1)}, u32[]{:S(2)}, u32[]{:S(2)}) collective-permute-start(bf16[1024,256]{1,0:T(8,128)(2,1)S(1)} %get-tuple-element.94), channel_id=1, source_target_pairs={{0,4},{1,5},{2,6},{3,7},{4,0},{5,1},{6,2},{7,3},{8,12},{9,13},{10,... | collective-permute-start | bytes 1572872 | tf_op jit(solution)/shard_map/ppermute | solution.py:357
  61.2 27.8 %collective-permute-start.10 = (bf16[1024,256]{1,0:T(8,128)(2,1)S(1)}, bf16[1024,256]{1,0:T(8,128)(2,1)S(1)}, u32[]{:S(2)}, u32[]{:S(2)}) collective-permute-start(bf16[1024,256]{1,0:T(8,128)(2,1)S(1)} %collective-permute-done.6.refs_6_.refs_8_), channel_id=1, source_target_pairs={{0,8},{8,0},{16,24},{24,16},{1,9},{9,1},{17,25},{25,17},{2,10},{10... | collective-permute-start | bytes 1572872 | tf_op jit(solution)/shard_map/ppermute | solution.py:357
  70.4 18.7 %collective-permute-start.12 = (bf16[1024,256]{1,0:T(8,128)(2,1)S(1)}, bf16[1024,256]{1,0:T(8,128)(2,1)S(1)}, u32[]{:S(2)}, u32[]{:S(2)}) collective-permute-start(bf16[1024,256]{1,0:T(8,128)(2,1)S(1)} %collective-permute-done.11.refs_8_.refs_10_), channel_id=1, source_target_pairs={{0,16},{8,24},{16,0},{24,8},{1,17},{9,25},{17,1},{25,9},{2,18},{10... | collective-permute-start | bytes 1572872 | tf_op jit(solution)/shard_map/ppermute | solution.py:357
  89.1 37.1 %collective-permute-start.18 = (bf16[128,4096]{1,0:T(8,128)(2,1)}, bf16[128,4096]{1,0:T(8,128)(2,1)S(1)}, u32[]{:S(2)}, u32[]{:S(2)}) collective-permute-start(bf16[128,4096]{1,0:T(8,128)(2,1)} %get-tuple-element.105.refs_0_), channel_id=1, source_target_pairs={{0,2},{1,3},{2,0},{3,1},{4,6},{5,7},{6,4},{7,5},{8,10},{9,11},{10,... | collective-permute-start | bytes 3145736 | tf_op jit(solution)/shard_map/ppermute | solution.py:357
  91.7 27.4 %collective-permute-start.15 = (bf16[768,256]{1,0:T(8,128)(2,1)S(1)}, bf16[768,256]{1,0:T(8,128)(2,1)}, u32[]{:S(2)}, u32[]{:S(2)}) collective-permute-start(bf16[768,256]{1,0:T(8,128)(2,1)S(1)} %collective-permute-done.13.refs_12_.refs_14_), channel_id=1, source_target_pairs={{0,16},{8,24},{16,0},{24,8},{1,17},{9,25},{17,1},{25,9},{2,18},{10... | collective-permute-start | bytes 1179656 | tf_op jit(solution)/shard_map/ppermute | solution.py:357
  94.4 33.1 %collective-permute-start.21 = (bf16[1280,256]{1,0:T(8,128)(2,1)}, bf16[1280,256]{1,0:T(8,128)(2,1)}, u32[]{:S(2)}, u32[]{:S(2)}) collective-permute-start(bf16[1280,256]{1,0:T(8,128)(2,1)} %pad_maximum_fusion.1), channel_id=1, source_target_pairs={{0,4},{1,5},{2,6},{3,7},{4,0},{5,1},{6,2},{7,3},{8,12},{9,13},{10,... | collective-permute-start | bytes 1966088 | tf_op jit(solution)/shard_map/ppermute | solution.py:357
  103.3 23.4 %collective-permute-start.17 = (bf16[1024,256]{1,0:T(8,128)(2,1)S(1)}, bf16[1024,256]{1,0:T(8,128)(2,1)S(1)}, u32[]{:S(2)}, u32[]{:S(2)}) collective-permute-start(bf16[1024,256]{1,0:T(8,128)(2,1)S(1)} %collective-permute-done.16.refs_9_.refs_11_), channel_id=1, source_target_pairs={{0,16},{8,24},{16,0},{24,8},{1,17},{9,25},{17,1},{25,9},{2,18},{10... | collective-permute-start | bytes 1572872 | tf_op jit(solution)/shard_map/ppermute | solution.py:357
  103.3 22.9 %collective-permute-start.14 = (bf16[768,256]{1,0:T(8,128)(2,1)S(1)}, bf16[768,256]{1,0:T(8,128)(2,1)S(1)}, u32[]{:S(2)}, u32[]{:S(2)}) collective-permute-start(bf16[768,256]{1,0:T(8,128)(2,1)S(1)} %collective-permute-done.13.refs_12_.refs_14_), channel_id=1, source_target_pairs={{0,8},{8,0},{16,24},{24,16},{1,9},{9,1},{17,25},{25,17},{2,10},{10... | collective-permute-start | bytes 1179656 | tf_op jit(solution)/shard_map/ppermute | solution.py:357
  127.5 36.8 %collective-permute-start.26 = (bf16[128,4096]{1,0:T(8,128)(2,1)}, bf16[128,4096]{1,0:T(8,128)(2,1)}, u32[]{:S(2)}, u32[]{:S(2)}) collective-permute-start(bf16[128,4096]{1,0:T(8,128)(2,1)} %get-tuple-element.114.refs_0_), channel_id=1, source_target_pairs={{0,2},{1,3},{2,0},{3,1},{4,6},{5,7},{6,4},{7,5},{8,10},{9,11},{10,... | collective-permute-start | bytes 3145736 | tf_op jit(solution)/shard_map/ppermute | solution.py:357
  128.9 22.7 %collective-permute-start.24 = (bf16[1280,256]{1,0:T(8,128)(2,1)}, bf16[1280,256]{1,0:T(8,128)(2,1)}, u32[]{:S(2)}, u32[]{:S(2)}) collective-permute-start(bf16[1280,256]{1,0:T(8,128)(2,1)} %collective-permute-done.21.refs_16_.refs_18_), channel_id=1, source_target_pairs={{0,8},{8,0},{16,24},{24,16},{1,9},{9,1},{17,25},{25,17},{2,10},{10... | collective-permute-start | bytes 1966088 | tf_op jit(solution)/shard_map/ppermute | solution.py:357
  135.2 33.4 %collective-permute-start.25 = (bf16[1280,256]{1,0:T(8,128)(2,1)}, bf16[1280,256]{1,0:T(8,128)(2,1)}, u32[]{:S(2)}, u32[]{:S(2)}) collective-permute-start(bf16[1280,256]{1,0:T(8,128)(2,1)} %collective-permute-done.21.refs_16_.refs_18_), channel_id=1, source_target_pairs={{0,16},{8,24},{16,0},{24,8},{1,17},{9,25},{17,1},{25,9},{2,18},{10... | collective-permute-start | bytes 1966088 | tf_op jit(solution)/shard_map/ppermute | solution.py:357
  135.5 29.3 %collective-permute-start.22 = (bf16[128,2048]{1,0:T(8,128)(2,1)}, bf16[128,2048]{1,0:T(8,128)(2,1)}, u32[]{:S(2)}, u32[]{:S(2)}) collective-permute-start(bf16[128,2048]{1,0:T(8,128)(2,1)} %slice.133), channel_id=1, source_target_pairs={{0,4},{1,5},{2,6},{3,7},{4,0},{5,1},{6,2},{7,3},{8,12},{9,13},{10,... | collective-permute-start | bytes 1572872 | tf_op jit(solution)/shard_map/ppermute | solution.py:357
  151.7 18.0 %collective-permute-start.29 = (bf16[1280,256]{1,0:T(8,128)(2,1)}, bf16[1280,256]{1,0:T(8,128)(2,1)S(1)}, u32[]{:S(2)}, u32[]{:S(2)}) collective-permute-start(bf16[1280,256]{1,0:T(8,128)(2,1)} %collective-permute-done.24.refs_17_.refs_19_), channel_id=1, source_target_pairs={{0,16},{8,24},{16,0},{24,8},{1,17},{9,25},{17,1},{25,9},{2,18},{10... | collective-permute-start | bytes 1966088 | tf_op jit(solution)/shard_map/ppermute | solution.py:357
  164.3 22.6 %collective-permute-start.28 = (bf16[128,4096]{1,0:T(8,128)(2,1)}, bf16[128,4096]{1,0:T(8,128)(2,1)}, u32[]{:S(2)}, u32[]{:S(2)}) collective-permute-start(bf16[128,4096]{1,0:T(8,128)(2,1)} %collective-permute-done.26.refs_1_), channel_id=1, source_target_pairs={{0,1},{1,0},{2,3},{3,2},{4,5},{5,4},{6,7},{7,6},{8,9},{9,8},{10,11... | collective-permute-start | bytes 3145736 | tf_op jit(solution)/shard_map/ppermute | solution.py:357
  164.3 22.6 %collective-permute-start.27 = (bf16[128,4096]{1,0:T(8,128)(2,1)S(1)}, bf16[128,4096]{1,0:T(8,128)(2,1)}, u32[]{:S(2)}, u32[]{:S(2)}) collective-permute-start(bf16[128,4096]{1,0:T(8,128)(2,1)S(1)} %copy-done.26), channel_id=1, source_target_pairs={{0,1},{1,0},{2,3},{3,2},{4,5},{5,4},{6,7},{7,6},{8,9},{9,8},{10,11... | collective-permute-start | bytes 3145736 | tf_op jit(solution)/shard_map/ppermute | solution.py:357
  164.8 17.5 %collective-permute-start.32 = (bf16[128,2048]{1,0:T(8,128)(2,1)}, bf16[128,2048]{1,0:T(8,128)(2,1)S(1)}, u32[]{:S(2)}, u32[]{:S(2)}) collective-permute-start(bf16[128,2048]{1,0:T(8,128)(2,1)} %collective-permute-done.22.refs_5_), channel_id=1, source_target_pairs={{0,8},{8,0},{16,24},{24,16},{1,9},{9,1},{17,25},{25,17},{2,10},{10... | collective-permute-start | bytes 1572872 | tf_op jit(solution)/shard_map/ppermute | solution.py:357
  182.3 20.6 %collective-permute-start.33 = (bf16[128,1024]{1,0:T(8,128)(2,1)}, bf16[128,1024]{1,0:T(8,128)(2,1)S(1)}, u32[]{:S(2)}, u32[]{:S(2)}) collective-permute-start(bf16[128,1024]{1,0:T(8,128)(2,1)} %get-tuple-element.123), channel_id=1, source_target_pairs={{0,4},{1,5},{2,6},{3,7},{4,0},{5,1},{6,2},{7,3},{8,12},{9,13},{10,... | collective-permute-start | bytes 786440 | tf_op jit(solution)/shard_map/ppermute | solution.py:357
  183.9 25.7 %collective-permute-start.36 = (bf16[128,2048]{1,0:T(8,128)(2,1)S(1)}, bf16[128,2048]{1,0:T(8,128)(2,1)S(1)}, u32[]{:S(2)}, u32[]{:S(2)}) collective-permute-start(bf16[128,2048]{1,0:T(8,128)(2,1)S(1)} %collective-permute-done.32.refs_6_), channel_id=1, source_target_pairs={{0,16},{8,24},{16,0},{24,8},{1,17},{9,25},{17,1},{25,9},{2,18},{10... | collective-permute-start | bytes 1572872 | tf_op jit(solution)/shard_map/ppermute | solution.py:357
  185.6 19.0 %collective-permute-start.34 = (bf16[128,1024]{1,0:T(8,128)(2,1)S(1)}, bf16[128,1024]{1,0:T(8,128)(2,1)S(1)}, u32[]{:S(2)}, u32[]{:S(2)}) collective-permute-start(bf16[128,1024]{1,0:T(8,128)(2,1)S(1)} %collective-permute-done.30.refs_5_), channel_id=1, source_target_pairs={{0,8},{8,0},{16,24},{24,16},{1,9},{9,1},{17,25},{25,17},{2,10},{10... | collective-permute-start | bytes 786440 | tf_op jit(solution)/shard_map/ppermute | solution.py:357
  225.6 17.4 %collective-permute-start.39 = (bf16[256,1024]{1,0:T(8,128)(2,1)S(1)}, bf16[256,1024]{1,0:T(8,128)(2,1)S(1)}, u32[]{:S(2)}, u32[]{:S(2)}) collective-permute-start(bf16[256,1024]{1,0:T(8,128)(2,1)S(1)} %fusion.12), channel_id=1, source_target_pairs={{0,2},{1,3},{2,0},{3,1},{4,6},{5,7},{6,4},{7,5},{8,10},{9,11},{10,... | collective-permute-start | bytes 1572872 | tf_op jit(solution)/shard_map/ppermute | solution.py:357
  231.2 20.6 %collective-permute-start.42 = (bf16[256,1024]{1,0:T(8,128)(2,1)}, bf16[256,1024]{1,0:T(8,128)(2,1)}, u32[]{:S(2)}, u32[]{:S(2)}) collective-permute-start(bf16[256,1024]{1,0:T(8,128)(2,1)} %fusion.8), channel_id=1, source_target_pairs={{0,2},{1,3},{2,0},{3,1},{4,6},{5,7},{6,4},{7,5},{8,10},{9,11},{10,... | collective-permute-start | bytes 1572872 | tf_op jit(solution)/shard_map/ppermute | solution.py:357
  255.0 22.9 %collective-permute-start.48 = (bf16[256,1024]{1,0:T(8,128)(2,1)S(1)}, bf16[256,1024]{1,0:T(8,128)(2,1)}, u32[]{:S(2)}, u32[]{:S(2)}) collective-permute-start(bf16[256,1024]{1,0:T(8,128)(2,1)S(1)} %fusion), channel_id=1, source_target_pairs={{0,2},{1,3},{2,0},{3,1},{4,6},{5,7},{6,4},{7,5},{8,10},{9,11},{10,... | collective-permute-start | bytes 1572872 | tf_op jit(solution)/shard_map/ppermute | solution.py:357
  (67 other events, 842.8 us)

commit v4 on v3

--- a/solution.py
+++ b/solution.py
@@ -439,33 +439,47 @@
     outs, refs = refs[: near + bool(deep)], refs[near + bool(deep) :]
     rows_in, held, sems = refs[0], refs[1:-1], refs[-1]
     count = xs[0].shape[0]
-    copies = [(xs[b], rows_in.at[pl.ds(b * count, count), :]) for b in range(blocks)]
-    copies += list(zip(fixed, held))
-    first = len(copies)
-    at = 0
-    for c in range(deep):
-        depth, both = pieces[4 * c].shape
-        for origin in range(4):
-            target = held[-1].at[pl.ds(at, depth), pl.ds(origin * both, both)]
-            copies.append((pieces[4 * c + origin], target))
-        at += depth
-    copies = [pltpu.make_async_copy(a, b, sems.at[i]) for i, (a, b) in enumerate(copies)]
-    for copy in copies:
-        copy.start()
-    for copy in copies[:first]:
-        copy.wait()
+    made = []
+
+    def bring(source, target):
+        made.append(pltpu.make_async_copy(source, target, sems.at[len(made)]))
+        made[-1].start()
+        return made[-1]
+
+    first = [bring(xs[b], rows_in.at[pl.ds(b * count, count), :]) for b in range(blocks)]
+    halves = [[], []]
     if near:
         hidden = held[0].shape[1]
         tile = hidden // 2
         for j in range(2):
+            cols = pl.ds(j * tile, tile)
+            halves[j] = [bring(w.at[:, cols], h.at[:, cols]) for w, h in zip(fixed, held)]
+    if near:
+        for copy in first + halves[0]:
+            copy.wait()
+    quarters = [[] for _ in range(4)]
+    for origin in range(4 if deep else 0):
+        at = 0
+        for c in range(deep):
+            depth, both = pieces[4 * c].shape
+            target = held[-1].at[pl.ds(at, depth), pl.ds(origin * both, both)]
+            quarters[origin].append(bring(pieces[4 * c + origin], target))
+            at += depth
+    if near:
+        for j in range(2):
             cols = slice(j * tile, (j + 1) * tile)
+            for copy in halves[j] if j else ():
+                copy.wait()
             g = jnp.dot(rows_in[...], held[0][:, cols], preferred_element_type=jnp.float32)
             u = jnp.dot(rows_in[...], held[1][:, cols], preferred_element_type=jnp.float32)
             outs[0][:, cols] = (silu(g) * u * scale[:, 0:1]).astype(jnp.bfloat16)
-    for copy in copies[first:]:
-        copy.wait()
+    else:
+        for copy in first:
+            copy.wait()
     if deep:
         share = both // 2
+        for copy in sum(quarters, []):
+            copy.wait()
         for origin in range(4):
             cols = slice(origin * both, (origin + 1) * both)
             got = jnp.dot(rows_in[...], held[-1][:, cols], preferred_element_type=jnp.float32)
@@ -479,7 +493,8 @@
     width = xs[0].shape[1]
     pieces = [piece for chunk in chunks for piece in chunk]
     away = pl.BlockSpec(memory_space=pl.ANY)
-    copies = len(xs) + len(near) + len(pieces)
+    away_count = len(xs) + len(near) + len(pieces)
+    copies = away_count + len(near)
     hidden = [w.shape[1] for w in near[:1]] + [2 * p.shape[1] for p in pieces[:1]]
     held = [w.shape for w in near] + [(width, 4 * p.shape[1]) for p in pieces[:1]]
     return pl.pallas_call(
@@ -487,7 +502,7 @@
             act_kernel, blocks=len(xs), near=int(bool(near)), deep=len(chunks)
         ),
         out_shape=[jax.ShapeDtypeStruct((rows, h), jnp.bfloat16) for h in hidden],
-        in_specs=[away] * copies + [pl.BlockSpec(memory_space=pltpu.VMEM)],
+        in_specs=[away] * away_count + [pl.BlockSpec(memory_space=pltpu.VMEM)],
         scratch_shapes=[pltpu.VMEM((rows, width), jnp.bfloat16)]
         + [pltpu.VMEM(shape, jnp.bfloat16) for shape in held]
         + [pltpu.SemaphoreType.DMA((copies,))],

time: 283 us -> 282 us (level)
  no operation moved by 1% of the time
where the time goes in v4:
time: 282 us
  Pallas kernels  120 us (43%)
  waiting for transfers between devices  75.9 us (27%)
  starting transfers between devices  62.7 us (22%)
  local copies, waits for them, and re-layouts  12.8 us (5%)
  other arithmetic  9.74 us (3%)
    ppermute x45, waiting for transfers between devices, swap(): return lax.ppermute(array, axis, [(i, i ^ mask) for i in range(peers)])  64.7 us
    ppermute x45, starting transfers between devices, swap(): return lax.ppermute(array, axis, [(i, i ^ mask) for i in range(peers)])  52.7 us
    pallas_call x3, Pallas kernels, act(): pl.pallas_call(functools.partial(act_kernel, blocks=len(xs), near=int(boo...  36.3 us
    pallas_call x2, Pallas kernels, mixer(): pl.pallas_call(functools.partial(back_kernel, before=before if part == 0...  28.7 us
    pallas_call x4, Pallas kernels, down(): pl.pallas_call(functools.partial(down_kernel, halves=len(nears)), grid=(P...  22.7 us
    pallas_call x1, Pallas kernels, mixer(): pl.pallas_call(front_kernel, grid=(groups,), out_shape=(shape((rows, widt...  17.2 us
    pallas_call x1, Pallas kernels, mixer(): pl.pallas_call(ends_kernel, grid=(groups,), out_shape=shape((states + 1,...  15.2 us
    ppermute x4, waiting for transfers between devices, from_behind(): return lax.ppermute(array, axis, pairs)  11.2 us
  transfers between devices with their start and end apart: 49, of which 18 were waited for; matrix products, arithmetic and copies ran while one was open for 4% of the time, Pallas kernels for 43%

profile of v4, /device:TPU:0, one launch (start us, length us, event | category | flops | bytes accessed | tf_op | source)
XLA Modules:
  0.0 281.8 jit_solution(8950029147077319943)
XLA Ops:
  10.4 3.4 %collective-permute-start = (bf16[16,4096]{1,0:T(8,128)(2,1)S(1)}, bf16[16,4096]{1,0:T(8,128)(2,1)S(1)}, u32[]{:S(2)}, u32[]{:S(2)}) collective-permute-start(bf16[16,4096]{1,0:T(8,128)(2,1)S(1)} %slice_bitcast_fusion), channel_id=1, source_target_pairs={{0,8},{8,16},{16,24},{1,9},{9,17},{17,25},{2,10},{10,18},{18,26},{... | collective-permute-start | bytes 393224 | tf_op jit(solution)/shard_map/ppermute | solution.py:31
  16.9 17.2 %mixer_front.1 = (bf16[256,4096]{1,0:T(8,128)(2,1)}, f32[4,2048,128]{2,1,0:T(8,128)}, f32[4,2048,128]{2,1,0:T(8,128)}, f32[256,32]{1,0:T(8,128)}) custom-call(bf16[256,4096]{1,0:T(8,128)(2,1)} %bitcast.51, bf16[16,4096]{1,0:T(8,128)(2,1)} %copy-done.39, f32[1,4096]{1,0:T(1,128)} %bitcast.65, f32[4,4096]{1,0:T(4,128)} %conv_weight.1, f32[1,4096]{1,0:T(1,128)} %bitcast.66, ...), custom_call_target="tpu_custom_call" | custom-call | flops 345000000 | bytes 65536 | tf_op jit(solution)/shard_map/mixer_front/pallas_call | solution.py:271
  34.1 3.4 %collective-permute-start.6 = (bf16[1024,256]{1,0:T(8,128)(2,1)S(1)}, bf16[1024,256]{1,0:T(8,128)(2,1)S(1)}, u32[]{:S(2)}, u32[]{:S(2)}) collective-permute-start(bf16[1024,256]{1,0:T(8,128)(2,1)S(1)} %collective-permute-done.4.refs_4_.refs_6_), channel_id=1, source_target_pairs={{0,16},{8,24},{16,0},{24,8},{1,17},{9,25},{17,1},{25,9},{2,18},{10... | collective-permute-start | bytes 1572872 | tf_op jit(solution)/shard_map/ppermute | solution.py:357
  39.3 15.2 %mixer_ends.1 = f32[17,32,128]{2,1,0:T(8,128)} custom-call(f32[4,256,8,128]{3,2,1,0:T(8,128)} %bitcast.41, f32[4,256,8,128]{3,2,1,0:T(8,128)} %bitcast.44, f32[256,32]{1,0:T(8,128)} %get-tuple-element.87.maps_ref, f32[16,32,128]{2,1,0:T(8,128)} %bitcast.54), custom_call_target="tpu_custom_call" | custom-call | flops 345000000 | bytes 65536 | tf_op jit(solution)/shard_map/mixer_ends/pallas_call | solution.py:302
  64.4 5.0 %collective-permute-done.8.rest_1_ = f32[17,32,128]{2,1,0:T(8,128)S(1)} collective-permute-done((f32[17,32,128]{2,1,0:T(8,128)}, f32[17,32,128]{2,1,0:T(8,128)S(1)}, u32[]{:S(2)}, u32[]{:S(2)}) %collective-permute-start.8) | collective-permute-done | bytes 278560 | tf_op jit(solution)/shard_map/ppermute | solution.py:31
  74.4 14.6 %mixer_back.2 = (f32[128,4096]{1,0:T(8,128)}, bf16[128,4096]{1,0:T(8,128)(2,1)}, f32[16,32,128]{2,1,0:T(8,128)}) custom-call(bf16[256,4096]{1,0:T(8,128)(2,1)} %bitcast.52, bf16[256,4096]{1,0:T(8,128)(2,1)} %get-tuple-element.84.conv_ref, f32[4,256,8,128]{3,2,1,0:T(8,128)} %bitcast.42, f32[4,256,8,128]{3,2,1,0:T(8,128)} %bitcast.45, ...), custom_call_target="tpu_custom_call" | custom-call | flops 345000000 | bytes 65536 | tf_op jit(solution)/shard_map/mixer_back/pallas_call | solution.py:332
  96.1 7.2 %collective-permute-done.16.refs_9_.refs_11_ = bf16[1024,256]{1,0:T(8,128)(2,1)S(1)} collective-permute-done((bf16[1024,256]{1,0:T(8,128)(2,1)S(1)}, bf16[1024,256]{1,0:T(8,128)(2,1)S(1)}, u32[]{:S(2)}, u32[]{:S(2)}) %collective-permute-start.16) | collective-permute-done | bytes 524320 | tf_op jit(solution)/shard_map/ppermute | solution.py:357
  105.0 14.1 %mixer_back.3 = (f32[128,4096]{1,0:T(8,128)}, bf16[128,4096]{1,0:T(8,128)(2,1)}) custom-call(bf16[256,4096]{1,0:T(8,128)(2,1)} %bitcast.53, bf16[256,4096]{1,0:T(8,128)(2,1)} %get-tuple-element.84.conv_ref, f32[4,256,8,128]{3,2,1,0:T(8,128)} %bitcast.43, f32[4,256,8,128]{3,2,1,0:T(8,128)} %bitcast.46, f32[256,32]{1,0:T(8,128)} %get-tuple-element.87.maps_ref, ...), custom_call_target="tpu_custom_call" | custom-call | flops 345000000 | bytes 65536 | tf_op jit(solution)/shard_map/mixer_back/pallas_call | solution.py:332
  119.5 6.7 %collective-permute-done.18.refs_1_ = bf16[128,4096]{1,0:T(8,128)(2,1)S(1)} collective-permute-done((bf16[128,4096]{1,0:T(8,128)(2,1)}, bf16[128,4096]{1,0:T(8,128)(2,1)S(1)}, u32[]{:S(2)}, u32[]{:S(2)}) %collective-permute-start.18) | collective-permute-done | bytes 1048608 | tf_op jit(solution)/shard_map/ppermute | solution.py:357
  135.5 4.0 %collective-permute-start.22 = (bf16[128,2048]{1,0:T(8,128)(2,1)}, bf16[128,2048]{1,0:T(8,128)(2,1)}, u32[]{:S(2)}, u32[]{:S(2)}) collective-permute-start(bf16[128,2048]{1,0:T(8,128)(2,1)} %slice.133), channel_id=1, source_target_pairs={{0,4},{1,5},{2,6},{3,7},{4,0},{5,1},{6,2},{7,3},{8,12},{9,13},{10,... | collective-permute-start | bytes 1572872 | tf_op jit(solution)/shard_map/ppermute | solution.py:357
  140.4 10.2 %act.3.refs_0_ = bf16[512,512]{1,0:T(8,128)(2,1)} custom-call(bf16[128,4096]{1,0:T(8,128)(2,1)} %get-tuple-element.105.refs_0_, bf16[128,4096]{1,0:T(8,128)(2,1)} %copy-done.1, bf16[128,4096]{1,0:T(8,128)(2,1)} %copy-done.2, bf16[128,4096]{1,0:T(8,128)(2,1)} %collective-permute-done.20.refs_3_, bf16[4096,512]{1,0:T(8,128)(2,1)} %bitcast.47, ...), custom_call_target="tpu_custom_call" | custom-call | flops 345000000 | bytes 65536 | tf_op jit(solution)/shard_map/act/pallas_call | solution.py:500
  152.7 11.6 %collective-permute-done.26.refs_1_ = bf16[128,4096]{1,0:T(8,128)(2,1)} collective-permute-done((bf16[128,4096]{1,0:T(8,128)(2,1)}, bf16[128,4096]{1,0:T(8,128)(2,1)}, u32[]{:S(2)}, u32[]{:S(2)}) %collective-permute-start.26) | collective-permute-done | bytes 1048608 | tf_op jit(solution)/shard_map/ppermute | solution.py:357
  164.8 3.8 %collective-permute-start.32 = (bf16[128,2048]{1,0:T(8,128)(2,1)}, bf16[128,2048]{1,0:T(8,128)(2,1)S(1)}, u32[]{:S(2)}, u32[]{:S(2)}) collective-permute-start(bf16[128,2048]{1,0:T(8,128)(2,1)} %collective-permute-done.22.refs_5_), channel_id=1, source_target_pairs={{0,8},{8,0},{16,24},{24,16},{1,9},{9,1},{17,25},{25,17},{2,10},{10... | collective-permute-start | bytes 1572872 | tf_op jit(solution)/shard_map/ppermute | solution.py:357
  171.2 11.1 %act.4.refs_2_ = bf16[512,512]{1,0:T(8,128)(2,1)} custom-call(bf16[128,4096]{1,0:T(8,128)(2,1)} %get-tuple-element.105.refs_0_, bf16[128,4096]{1,0:T(8,128)(2,1)} %copy-done.1, bf16[128,4096]{1,0:T(8,128)(2,1)} %copy-done.2, bf16[128,4096]{1,0:T(8,128)(2,1)} %collective-permute-done.20.refs_3_, bf16[1024,256]{1,0:T(8,128)(2,1)} %copy-done.16, ...), custom_call_target="tpu_custom_call" | custom-call | flops 345000000 | bytes 65536 | tf_op jit(solution)/shard_map/act/pallas_call | solution.py:500
  186.8 15.0 %act.5 = (bf16[512,512]{1,0:T(8,128)(2,1)}, bf16[512,512]{1,0:T(8,128)(2,1)}) custom-call(bf16[128,4096]{1,0:T(8,128)(2,1)} %get-tuple-element.114.refs_0_, bf16[128,4096]{1,0:T(8,128)(2,1)} %collective-permute-done.26.refs_1_, bf16[128,4096]{1,0:T(8,128)(2,1)} %collective-permute-done.27.refs_2_, bf16[128,4096]{1,0:T(8,128)(2,1)} %collective-permute-done.28.refs_3_, ...), custom_call_target="tpu_custom_call" | custom-call | flops 345000000 | bytes 65536 | tf_op jit(solution)/shard_map/act/pallas_call | solution.py:500
  203.9 4.6 %collective-permute-done.35.refs_6_ = bf16[128,1024]{1,0:T(8,128)(2,1)S(1)} collective-permute-done((bf16[128,1024]{1,0:T(8,128)(2,1)S(1)}, bf16[128,1024]{1,0:T(8,128)(2,1)S(1)}, u32[]{:S(2)}, u32[]{:S(2)}) %collective-permute-start.35) | collective-permute-done | bytes 262176 | tf_op jit(solution)/shard_map/ppermute | solution.py:357
  209.4 5.7 %down.4 = (f32[512,1024]{1,0:T(8,128)}, bf16[512,1024]{1,0:T(8,128)(2,1)}) custom-call(bf16[512,512]{1,0:T(8,128)(2,1)} %act.3.refs_0_, bf16[512,512]{1,0:T(8,128)(2,1)} %get-tuple-element.126.refs_1_, bf16[512,512]{1,0:T(8,128)(2,1)} %act.4.refs_2_, bf16[512,512]{1,0:T(8,128)(2,1)} %get-tuple-element.127.refs_3_, bf16[512,4096]{1,0:T(8,128)(2,1)} %bitcast.37, ...), custom_call_target="tpu_custom_call" | custom-call | flops 345000000 | bytes 65536 | tf_op jit(solution)/shard_map/down/pallas_call | solution.py:541
  215.8 5.7 %down.5 = (f32[512,1024]{1,0:T(8,128)}, bf16[512,1024]{1,0:T(8,128)(2,1)}) custom-call(bf16[512,512]{1,0:T(8,128)(2,1)} %act.3.refs_0_, bf16[512,512]{1,0:T(8,128)(2,1)} %get-tuple-element.126.refs_1_, bf16[512,512]{1,0:T(8,128)(2,1)} %act.4.refs_2_, bf16[512,512]{1,0:T(8,128)(2,1)} %get-tuple-element.127.refs_3_, bf16[512,4096]{1,0:T(8,128)(2,1)} %bitcast.38, ...), custom_call_target="tpu_custom_call" | custom-call | flops 345000000 | bytes 65536 | tf_op jit(solution)/shard_map/down/pallas_call | solution.py:541
  230.7 5.6 %collective-permute-done.43.refs_7_ = bf16[128,1024]{1,0:T(8,128)(2,1)} collective-permute-done((bf16[128,1024]{1,0:T(8,128)(2,1)S(1)}, bf16[128,1024]{1,0:T(8,128)(2,1)}, u32[]{:S(2)}, u32[]{:S(2)}) %collective-permute-start.43) | collective-permute-done | bytes 262176 | tf_op jit(solution)/shard_map/ppermute | solution.py:357
  236.2 5.7 %down.6 = (f32[512,1024]{1,0:T(8,128)}, bf16[512,1024]{1,0:T(8,128)(2,1)}) custom-call(bf16[512,512]{1,0:T(8,128)(2,1)} %act.3.refs_0_, bf16[512,512]{1,0:T(8,128)(2,1)} %get-tuple-element.126.refs_1_, bf16[512,512]{1,0:T(8,128)(2,1)} %act.4.refs_2_, bf16[512,512]{1,0:T(8,128)(2,1)} %get-tuple-element.127.refs_3_, bf16[512,4096]{1,0:T(8,128)(2,1)} %bitcast.39, ...), custom_call_target="tpu_custom_call" | custom-call | flops 345000000 | bytes 65536 | tf_op jit(solution)/shard_map/down/pallas_call | solution.py:541
  242.7 5.6 %down.7 = (f32[512,1024]{1,0:T(8,128)}, bf16[512,1024]{1,0:T(8,128)(2,1)}) custom-call(bf16[512,512]{1,0:T(8,128)(2,1)} %act.3.refs_0_, bf16[512,512]{1,0:T(8,128)(2,1)} %get-tuple-element.126.refs_1_, bf16[512,512]{1,0:T(8,128)(2,1)} %act.4.refs_2_, bf16[512,512]{1,0:T(8,128)(2,1)} %get-tuple-element.127.refs_3_, bf16[512,4096]{1,0:T(8,128)(2,1)} %bitcast.40, ...), custom_call_target="tpu_custom_call" | custom-call | flops 345000000 | bytes 65536 | tf_op jit(solution)/shard_map/down/pallas_call | solution.py:541
  256.3 9.7 %collective-permute-done.46 = bf16[256,1024]{1,0:T(8,128)(2,1)S(1)} collective-permute-done((bf16[256,1024]{1,0:T(8,128)(2,1)S(1)}, bf16[256,1024]{1,0:T(8,128)(2,1)S(1)}, u32[]{:S(2)}, u32[]{:S(2)}) %collective-permute-start.46) | collective-permute-done | bytes 524320 | tf_op jit(solution)/shard_map/ppermute | solution.py:357
  266.0 11.0 %collective-permute-done.48 = bf16[256,1024]{1,0:T(8,128)(2,1)} collective-permute-done((bf16[256,1024]{1,0:T(8,128)(2,1)S(1)}, bf16[256,1024]{1,0:T(8,128)(2,1)}, u32[]{:S(2)}, u32[]{:S(2)}) %collective-permute-start.48) | collective-permute-done | bytes 524320 | tf_op jit(solution)/shard_map/ppermute | solution.py:357
  276.9 3.3 %fusion.16 = (bf16[1,256,1024]{2,1,0:T(8,128)(2,1)S(1)}, bf16[1,256,1024]{2,1,0:T(8,128)(2,1)S(1)}, bf16[1,256,1024]{2,1,0:T(8,128)(2,1)S(1)}, bf16[1,256,1024]{2,1,0:T(8,128)(2,1)S(1)}) fusion(bf16[256,1024]{1,0:T(8,128)(2,1)S(1)} %collective-permute-done.39, f32[512,1024]{1,0:T(8,128)S(1)} %convert_element_type.44, f32[512,1024]{1,0:T(8,128)S(1)} %copy-done.9, ...), kind=kLoop, calls=%fused_computation.35 | loop fusion | flops 5242880 | bytes 16777216 | tf_op jit(solution)/shard_map/concatenate | solution.py:602
  (197 shorter events, 82.0 us)
Async XLA Ops:
  6.8 27.3 %collective-permute-start.4 = (bf16[1024,256]{1,0:T(8,128)(2,1)S(1)}, bf16[1024,256]{1,0:T(8,128)(2,1)S(1)}, u32[]{:S(2)}, u32[]{:S(2)}) collective-permute-start(bf16[1024,256]{1,0:T(8,128)(2,1)S(1)} %get-tuple-element.83), channel_id=1, source_target_pairs={{0,4},{1,5},{2,6},{3,7},{4,0},{5,1},{6,2},{7,3},{8,12},{9,13},{10,... | collective-permute-start | bytes 1572872 | tf_op jit(solution)/shard_map/ppermute | solution.py:357
  34.1 20.4 %collective-permute-start.6 = (bf16[1024,256]{1,0:T(8,128)(2,1)S(1)}, bf16[1024,256]{1,0:T(8,128)(2,1)S(1)}, u32[]{:S(2)}, u32[]{:S(2)}) collective-permute-start(bf16[1024,256]{1,0:T(8,128)(2,1)S(1)} %collective-permute-done.4.refs_4_.refs_6_), channel_id=1, source_target_pairs={{0,16},{8,24},{16,0},{24,8},{1,17},{9,25},{17,1},{25,9},{2,18},{10... | collective-permute-start | bytes 1572872 | tf_op jit(solution)/shard_map/ppermute | solution.py:357
  38.2 23.5 %collective-permute-start.11 = (bf16[1024,256]{1,0:T(8,128)(2,1)S(1)}, bf16[1024,256]{1,0:T(8,128)(2,1)S(1)}, u32[]{:S(2)}, u32[]{:S(2)}) collective-permute-start(bf16[1024,256]{1,0:T(8,128)(2,1)S(1)} %get-tuple-element.94), channel_id=1, source_target_pairs={{0,4},{1,5},{2,6},{3,7},{4,0},{5,1},{6,2},{7,3},{8,12},{9,13},{10,... | collective-permute-start | bytes 1572872 | tf_op jit(solution)/shard_map/ppermute | solution.py:357
  61.2 27.8 %collective-permute-start.10 = (bf16[1024,256]{1,0:T(8,128)(2,1)S(1)}, bf16[1024,256]{1,0:T(8,128)(2,1)S(1)}, u32[]{:S(2)}, u32[]{:S(2)}) collective-permute-start(bf16[1024,256]{1,0:T(8,128)(2,1)S(1)} %collective-permute-done.6.refs_6_.refs_8_), channel_id=1, source_target_pairs={{0,8},{8,0},{16,24},{24,16},{1,9},{9,1},{17,25},{25,17},{2,10},{10... | collective-permute-start | bytes 1572872 | tf_op jit(solution)/shard_map/ppermute | solution.py:357
  70.4 18.7 %collective-permute-start.12 = (bf16[1024,256]{1,0:T(8,128)(2,1)S(1)}, bf16[1024,256]{1,0:T(8,128)(2,1)S(1)}, u32[]{:S(2)}, u32[]{:S(2)}) collective-permute-start(bf16[1024,256]{1,0:T(8,128)(2,1)S(1)} %collective-permute-done.11.refs_8_.refs_10_), channel_id=1, source_target_pairs={{0,16},{8,24},{16,0},{24,8},{1,17},{9,25},{17,1},{25,9},{2,18},{10... | collective-permute-start | bytes 1572872 | tf_op jit(solution)/shard_map/ppermute | solution.py:357
  89.1 37.1 %collective-permute-start.18 = (bf16[128,4096]{1,0:T(8,128)(2,1)}, bf16[128,4096]{1,0:T(8,128)(2,1)S(1)}, u32[]{:S(2)}, u32[]{:S(2)}) collective-permute-start(bf16[128,4096]{1,0:T(8,128)(2,1)} %get-tuple-element.105.refs_0_), channel_id=1, source_target_pairs={{0,2},{1,3},{2,0},{3,1},{4,6},{5,7},{6,4},{7,5},{8,10},{9,11},{10,... | collective-permute-start | bytes 3145736 | tf_op jit(solution)/shard_map/ppermute | solution.py:357
  91.7 27.4 %collective-permute-start.15 = (bf16[768,256]{1,0:T(8,128)(2,1)S(1)}, bf16[768,256]{1,0:T(8,128)(2,1)}, u32[]{:S(2)}, u32[]{:S(2)}) collective-permute-start(bf16[768,256]{1,0:T(8,128)(2,1)S(1)} %collective-permute-done.13.refs_12_.refs_14_), channel_id=1, source_target_pairs={{0,16},{8,24},{16,0},{24,8},{1,17},{9,25},{17,1},{25,9},{2,18},{10... | collective-permute-start | bytes 1179656 | tf_op jit(solution)/shard_map/ppermute | solution.py:357
  94.4 33.1 %collective-permute-start.21 = (bf16[1280,256]{1,0:T(8,128)(2,1)}, bf16[1280,256]{1,0:T(8,128)(2,1)}, u32[]{:S(2)}, u32[]{:S(2)}) collective-permute-start(bf16[1280,256]{1,0:T(8,128)(2,1)} %pad_maximum_fusion.1), channel_id=1, source_target_pairs={{0,4},{1,5},{2,6},{3,7},{4,0},{5,1},{6,2},{7,3},{8,12},{9,13},{10,... | collective-permute-start | bytes 1966088 | tf_op jit(solution)/shard_map/ppermute | solution.py:357
  103.3 23.4 %collective-permute-start.17 = (bf16[1024,256]{1,0:T(8,128)(2,1)S(1)}, bf16[1024,256]{1,0:T(8,128)(2,1)S(1)}, u32[]{:S(2)}, u32[]{:S(2)}) collective-permute-start(bf16[1024,256]{1,0:T(8,128)(2,1)S(1)} %collective-permute-done.16.refs_9_.refs_11_), channel_id=1, source_target_pairs={{0,16},{8,24},{16,0},{24,8},{1,17},{9,25},{17,1},{25,9},{2,18},{10... | collective-permute-start | bytes 1572872 | tf_op jit(solution)/shard_map/ppermute | solution.py:357
  103.3 22.9 %collective-permute-start.14 = (bf16[768,256]{1,0:T(8,128)(2,1)S(1)}, bf16[768,256]{1,0:T(8,128)(2,1)S(1)}, u32[]{:S(2)}, u32[]{:S(2)}) collective-permute-start(bf16[768,256]{1,0:T(8,128)(2,1)S(1)} %collective-permute-done.13.refs_12_.refs_14_), channel_id=1, source_target_pairs={{0,8},{8,0},{16,24},{24,16},{1,9},{9,1},{17,25},{25,17},{2,10},{10... | collective-permute-start | bytes 1179656 | tf_op jit(solution)/shard_map/ppermute | solution.py:357
  127.5 36.8 %collective-permute-start.26 = (bf16[128,4096]{1,0:T(8,128)(2,1)}, bf16[128,4096]{1,0:T(8,128)(2,1)}, u32[]{:S(2)}, u32[]{:S(2)}) collective-permute-start(bf16[128,4096]{1,0:T(8,128)(2,1)} %get-tuple-element.114.refs_0_), channel_id=1, source_target_pairs={{0,2},{1,3},{2,0},{3,1},{4,6},{5,7},{6,4},{7,5},{8,10},{9,11},{10,... | collective-permute-start | bytes 3145736 | tf_op jit(solution)/shard_map/ppermute | solution.py:357
  128.9 21.6 %collective-permute-start.24 = (bf16[1280,256]{1,0:T(8,128)(2,1)}, bf16[1280,256]{1,0:T(8,128)(2,1)}, u32[]{:S(2)}, u32[]{:S(2)}) collective-permute-start(bf16[1280,256]{1,0:T(8,128)(2,1)} %collective-permute-done.21.refs_16_.refs_18_), channel_id=1, source_target_pairs={{0,8},{8,0},{16,24},{24,16},{1,9},{9,1},{17,25},{25,17},{2,10},{10... | collective-permute-start | bytes 1966088 | tf_op jit(solution)/shard_map/ppermute | solution.py:357
  135.2 33.4 %collective-permute-start.25 = (bf16[1280,256]{1,0:T(8,128)(2,1)}, bf16[1280,256]{1,0:T(8,128)(2,1)}, u32[]{:S(2)}, u32[]{:S(2)}) collective-permute-start(bf16[1280,256]{1,0:T(8,128)(2,1)} %collective-permute-done.21.refs_16_.refs_18_), channel_id=1, source_target_pairs={{0,16},{8,24},{16,0},{24,8},{1,17},{9,25},{17,1},{25,9},{2,18},{10... | collective-permute-start | bytes 1966088 | tf_op jit(solution)/shard_map/ppermute | solution.py:357
  135.5 29.3 %collective-permute-start.22 = (bf16[128,2048]{1,0:T(8,128)(2,1)}, bf16[128,2048]{1,0:T(8,128)(2,1)}, u32[]{:S(2)}, u32[]{:S(2)}) collective-permute-start(bf16[128,2048]{1,0:T(8,128)(2,1)} %slice.133), channel_id=1, source_target_pairs={{0,4},{1,5},{2,6},{3,7},{4,0},{5,1},{6,2},{7,3},{8,12},{9,13},{10,... | collective-permute-start | bytes 1572872 | tf_op jit(solution)/shard_map/ppermute | solution.py:357
  150.6 19.1 %collective-permute-start.29 = (bf16[1280,256]{1,0:T(8,128)(2,1)}, bf16[1280,256]{1,0:T(8,128)(2,1)S(1)}, u32[]{:S(2)}, u32[]{:S(2)}) collective-permute-start(bf16[1280,256]{1,0:T(8,128)(2,1)} %collective-permute-done.24.refs_17_.refs_19_), channel_id=1, source_target_pairs={{0,16},{8,24},{16,0},{24,8},{1,17},{9,25},{17,1},{25,9},{2,18},{10... | collective-permute-start | bytes 1966088 | tf_op jit(solution)/shard_map/ppermute | solution.py:357
  164.3 22.6 %collective-permute-start.28 = (bf16[128,4096]{1,0:T(8,128)(2,1)}, bf16[128,4096]{1,0:T(8,128)(2,1)}, u32[]{:S(2)}, u32[]{:S(2)}) collective-permute-start(bf16[128,4096]{1,0:T(8,128)(2,1)} %collective-permute-done.26.refs_1_), channel_id=1, source_target_pairs={{0,1},{1,0},{2,3},{3,2},{4,5},{5,4},{6,7},{7,6},{8,9},{9,8},{10,11... | collective-permute-start | bytes 3145736 | tf_op jit(solution)/shard_map/ppermute | solution.py:357
  164.3 22.6 %collective-permute-start.27 = (bf16[128,4096]{1,0:T(8,128)(2,1)S(1)}, bf16[128,4096]{1,0:T(8,128)(2,1)}, u32[]{:S(2)}, u32[]{:S(2)}) collective-permute-start(bf16[128,4096]{1,0:T(8,128)(2,1)S(1)} %copy-done.26), channel_id=1, source_target_pairs={{0,1},{1,0},{2,3},{3,2},{4,5},{5,4},{6,7},{7,6},{8,9},{9,8},{10,11... | collective-permute-start | bytes 3145736 | tf_op jit(solution)/shard_map/ppermute | solution.py:357
  164.8 17.5 %collective-permute-start.32 = (bf16[128,2048]{1,0:T(8,128)(2,1)}, bf16[128,2048]{1,0:T(8,128)(2,1)S(1)}, u32[]{:S(2)}, u32[]{:S(2)}) collective-permute-start(bf16[128,2048]{1,0:T(8,128)(2,1)} %collective-permute-done.22.refs_5_), channel_id=1, source_target_pairs={{0,8},{8,0},{16,24},{24,16},{1,9},{9,1},{17,25},{25,17},{2,10},{10... | collective-permute-start | bytes 1572872 | tf_op jit(solution)/shard_map/ppermute | solution.py:357
  182.3 19.6 %collective-permute-start.33 = (bf16[128,1024]{1,0:T(8,128)(2,1)}, bf16[128,1024]{1,0:T(8,128)(2,1)S(1)}, u32[]{:S(2)}, u32[]{:S(2)}) collective-permute-start(bf16[128,1024]{1,0:T(8,128)(2,1)} %get-tuple-element.123), channel_id=1, source_target_pairs={{0,4},{1,5},{2,6},{3,7},{4,0},{5,1},{6,2},{7,3},{8,12},{9,13},{10,... | collective-permute-start | bytes 786440 | tf_op jit(solution)/shard_map/ppermute | solution.py:357
  183.9 24.7 %collective-permute-start.36 = (bf16[128,2048]{1,0:T(8,128)(2,1)S(1)}, bf16[128,2048]{1,0:T(8,128)(2,1)S(1)}, u32[]{:S(2)}, u32[]{:S(2)}) collective-permute-start(bf16[128,2048]{1,0:T(8,128)(2,1)S(1)} %collective-permute-done.32.refs_6_), channel_id=1, source_target_pairs={{0,16},{8,24},{16,0},{24,8},{1,17},{9,25},{17,1},{25,9},{2,18},{10... | collective-permute-start | bytes 1572872 | tf_op jit(solution)/shard_map/ppermute | solution.py:357
  185.6 18.0 %collective-permute-start.34 = (bf16[128,1024]{1,0:T(8,128)(2,1)S(1)}, bf16[128,1024]{1,0:T(8,128)(2,1)S(1)}, u32[]{:S(2)}, u32[]{:S(2)}) collective-permute-start(bf16[128,1024]{1,0:T(8,128)(2,1)S(1)} %collective-permute-done.30.refs_5_), channel_id=1, source_target_pairs={{0,8},{8,0},{16,24},{24,16},{1,9},{9,1},{17,25},{25,17},{2,10},{10... | collective-permute-start | bytes 786440 | tf_op jit(solution)/shard_map/ppermute | solution.py:357
  224.6 17.4 %collective-permute-start.39 = (bf16[256,1024]{1,0:T(8,128)(2,1)S(1)}, bf16[256,1024]{1,0:T(8,128)(2,1)S(1)}, u32[]{:S(2)}, u32[]{:S(2)}) collective-permute-start(bf16[256,1024]{1,0:T(8,128)(2,1)S(1)} %fusion.12), channel_id=1, source_target_pairs={{0,2},{1,3},{2,0},{3,1},{4,6},{5,7},{6,4},{7,5},{8,10},{9,11},{10,... | collective-permute-start | bytes 1572872 | tf_op jit(solution)/shard_map/ppermute | solution.py:357
  230.2 20.6 %collective-permute-start.42 = (bf16[256,1024]{1,0:T(8,128)(2,1)}, bf16[256,1024]{1,0:T(8,128)(2,1)}, u32[]{:S(2)}, u32[]{:S(2)}) collective-permute-start(bf16[256,1024]{1,0:T(8,128)(2,1)} %fusion.8), channel_id=1, source_target_pairs={{0,2},{1,3},{2,0},{3,1},{4,6},{5,7},{6,4},{7,5},{8,10},{9,11},{10,... | collective-permute-start | bytes 1572872 | tf_op jit(solution)/shard_map/ppermute | solution.py:357
  254.0 22.9 %collective-permute-start.48 = (bf16[256,1024]{1,0:T(8,128)(2,1)S(1)}, bf16[256,1024]{1,0:T(8,128)(2,1)}, u32[]{:S(2)}, u32[]{:S(2)}) collective-permute-start(bf16[256,1024]{1,0:T(8,128)(2,1)S(1)} %fusion), channel_id=1, source_target_pairs={{0,2},{1,3},{2,0},{3,1},{4,6},{5,7},{6,4},{7,5},{8,10},{9,11},{10,... | collective-permute-start | bytes 1572872 | tf_op jit(solution)/shard_map/ppermute | solution.py:357
  (67 other events, 839.7 us)
